TPU v7x, 32 devices: a whole 2x2x4 slice. The times are simulated.
32 devices in a mesh: groups: 2 (over x), row: 16 (over z, y, core).
Axes of the slice: x: 2, y: 2, z: 4, core: 2. Of those that a mesh axis runs over, the one named last changes fastest.
Arguments:
- head_out: bfloat16 [16, 1536, 1024], P('row', 'groups'), parts along dimension 1, may hold values from -6 to 6
- out_grad: bfloat16 [16, 1536, 1024], P('row', 'groups'), parts along dimension 1, may hold values from -6 to 6
- proj_weight: bfloat16 [16, 1024, 1024], P('row'), may hold values from -0.09375 to 0.09375
Outputs:
- projected: bfloat16 [16, 1536, 1024], P('row', 'groups'), parts along dimension 1
- head_grad: bfloat16 [16, 1536, 1024], P('row', 'groups'), parts along dimension 1
There are 2 independent parts, one for each index of `groups`. A program takes and returns all parts, laid end to end along the dimension named above; an argument that names none is the same for every part. Nothing has to cross between parts.
All inputs are finite; a program needn't handle non-finite values.
Results may differ from a plain program's by a relative error of at most 0.001.
Values may be sent and summed in bfloat16 or wider, within the bound.
No kernel may reach another device: no remote copies, remote signals or barrier semaphores. Data moves between devices by JAX's collectives and lax.ppermute only.
A program may use at most 128 MiB of HBM per device.

v0:
```python
import jax
import jax.numpy as jnp
from jax import lax
from jax.sharding import PartitionSpec as P


def partner_2(value, axis, distance):
    return lax.ppermute(value, axis, [(i, i ^ 1 << distance) for i in range(lax.axis_size(axis))])


def bit_at(device_index, position):
    return jnp.bitwise_and(jnp.right_shift(device_index, position), 1)


def grow_panel(own_block, bit_order, offset, device_index, swap_fn):
    panel = own_block
    for level_bit in bit_order:
        own_bit = bit_at(device_index, offset + level_bit)
        partner = swap_fn(panel, offset + level_bit)
        low_part = jnp.where(own_bit == 0, panel, partner)
        high_part = jnp.where(own_bit == 0, partner, panel)
        panel = jnp.stack([low_part, high_part], 0)
    return panel


def turn_panel(panel, layout, device_index, swap_fn, bit_order):
    for level_bit in bit_order:
        axis_at = layout.index(level_bit)
        own_bit = bit_at(device_index, level_bit)
        kept_half = lax.dynamic_index_in_dim(panel, own_bit, axis_at, keepdims=False)
        sent_half = lax.dynamic_index_in_dim(panel, 1 - own_bit, axis_at, keepdims=False)
        partner = swap_fn(sent_half, level_bit)
        low_part = jnp.where(own_bit == 0, kept_half, partner)
        high_part = jnp.where(own_bit == 0, partner, kept_half)
        panel = jnp.stack([low_part, high_part], axis_at)
    return panel


def swap_heads(payload, bit_number):
    return partner_2(payload, "row", bit_number)


def swap_weights(payload, bit_number):
    return partner_2(payload, "row", bit_number)


def swap_cotangents(payload, bit_number):
    return partner_2(payload, "row", bit_number)


def swap_rows(payload, bit_number):
    return partner_2(payload, "row", bit_number)


def local(head_out, out_grad, proj_weight):
    own_heads = head_out[0]
    own_cotangent = out_grad[0]
    own_weight = proj_weight[0]
    levels = (lax.axis_size("row").bit_length() - 1) // 2
    device_index = lax.axis_index("row")
    bit_order = list(range(levels))
    layout = bit_order[::-1]
    letters = "pqrsuv"[:levels]
    head_panel = grow_panel(own_heads, bit_order, 0, device_index, swap_heads)
    weight_panel = grow_panel(own_weight, bit_order, levels, device_index, swap_weights)
    forward = jnp.einsum(
        letters + "ti," + letters + "io->to",
        head_panel,
        weight_panel,
        preferred_element_type=jnp.float32,
    )
    projected = forward.astype(jnp.bfloat16)[None]
    turned = turn_panel(weight_panel, layout, device_index, swap_rows, bit_order)
    grad_panel = grow_panel(own_cotangent, bit_order, 0, device_index, swap_cotangents)
    summed = jnp.einsum(
        letters + "to," + letters + "io->ti", grad_panel, turned, preferred_element_type=jnp.float32
    )
    head_grad = summed.astype(jnp.bfloat16)[None]
    return (projected, head_grad)


def solution(mesh):
    placed = (P("row", "groups", None), P("row", "groups", None), P("row", None, None))
    return jax.shard_map(
        local,
        mesh=mesh,
        in_specs=placed,
        out_specs=(P("row", "groups", None), P("row", "groups", None)),
        check_vma=False,
    )
```

profile of v0, /device:TPU:0, one launch (start us, length us, event | category | flops | bytes accessed | tf_op | source)
XLA Modules:
  0.0 507.9 jit_solution(3587516793645688313)
XLA Ops:
  0.6 3.1 collective-permute-start.2
  3.7 45.9 %collective-permute-done.2 = bf16[1024,1024]{1,0:T(8,128)(2,1)} collective-permute-done((bf16[1024,1024]{1,0:T(8,128)(2,1)}, bf16[1024,1024]{1,0:T(8,128)(2,1)}, u32[]{:S(2)}, u32[]{:S(2)}) %collective-permute-start.2) | collective-permute-done | bytes 2097184 | tf_op jit(solution)/shard_map/ppermute | solution.py:8
  49.7 2.5 select_bitcast_fusion.11
  52.2 0.0 copy-start.10
  52.2 2.6 pad_maximum_fusion.2
  54.8 0.1 copy-done.10
  54.9 2.8 collective-permute-start.3
  57.6 180.1 %collective-permute-done.3 = bf16[2,1024,1024]{2,1,0:T(8,128)(2,1)} collective-permute-done((bf16[2,1024,1024]{2,1,0:T(8,128)(2,1)}, bf16[2,1024,1024]{2,1,0:T(8,128)(2,1)}, u32[]{:S(2)}, u32[]{:S(2)}) %collective-permute-start.3) | collective-permute-done | bytes 4194336 | tf_op jit(solution)/shard_map/ppermute | solution.py:8
  237.7 3.1 select_bitcast_fusion.5
  240.8 0.0 copy-start
  240.8 0.0 copy-start.3
  240.8 0.0 copy-start.13
  240.8 0.0 copy-start.14
  240.9 2.4 fusion.18
  243.3 1.4 copy-done
  244.6 1.3 copy-done.3
  245.9 0.0 collective-permute-start.6
  245.9 0.0 copy-done.13
  245.9 0.5 collective-permute-start.4
  246.4 0.0 copy-done.14
  246.4 0.1 collective-permute-start
  246.5 8.6 %collective-permute-done.4 = bf16[768,1024]{1,0:T(8,128)(2,1)} collective-permute-done((bf16[768,1024]{1,0:T(8,128)(2,1)S(1)}, bf16[768,1024]{1,0:T(8,128)(2,1)}, u32[]{:S(2)}, u32[]{:S(2)}) %collective-permute-start.4) | collective-permute-done | bytes 1572896 | tf_op jit(solution)/shard_map/ppermute | solution.py:8
  255.1 2.2 collective-permute-done
  257.3 3.2 select_bitcast_fusion.13
  260.6 0.0 copy-start.11
  260.6 0.0 copy-start.12
  260.6 1.1 copy-done.11
  261.7 0.5 copy-done.12
  262.2 2.0 pad_maximum_fusion.3
  264.2 1.4 collective-permute-start.1
  265.6 1.9 pad_maximum_fusion.4
  267.5 0.7 collective-permute-start.5
  268.1 0.0 collective-permute-done.6
  268.1 0.0 copy-done.4
  268.1 2.5 select_bitcast_fusion.2
  270.7 2.7 fusion.12
  273.4 0.6 copy-done.6
  273.9 1.3 copy-done.8
  275.2 1.4 collective-permute-start.7
  276.6 58.9 %collective-permute-done.1 = bf16[2,768,1024]{2,1,0:T(8,128)(2,1)} collective-permute-done((bf16[2,768,1024]{2,1,0:T(8,128)(2,1)}, bf16[2,768,1024]{2,1,0:T(8,128)(2,1)}, u32[]{:S(2)}, u32[]{:S(2)}) %collective-permute-start.1) | collective-permute-done | bytes 3145760 | tf_op jit(solution)/shard_map/ppermute | solution.py:8
  335.4 4.2 select_bitcast_fusion.9
  339.6 63.3 %collective-permute-done.5 = bf16[2,768,1024]{2,1,0:T(8,128)(2,1)} collective-permute-done((bf16[2,768,1024]{2,1,0:T(8,128)(2,1)}, bf16[2,768,1024]{2,1,0:T(8,128)(2,1)}, u32[]{:S(2)}, u32[]{:S(2)}) %collective-permute-start.5) | collective-permute-done | bytes 3145760 | tf_op jit(solution)/shard_map/ppermute | solution.py:8
  402.9 4.2 select_bitcast_fusion.7
  407.1 0.0 copy-start.9
  407.1 9.9 %fusion.25 = bf16[1,768,1024]{2,1,0:T(8,128)(2,1)} fusion(bf16[1,2,1024,1024]{3,2,1,0:T(8,128)(2,1)S(1)} %copy-done.5, bf16[1,2,1024,1024]{3,2,1,0:T(8,128)(2,1)S(1)} %copy-done.2, bf16[1,2,768,1024]{3,2,1,0:T(8,128)(2,1)} %get-tuple-element.11, bf16[1,2,768,1024]{3,2,1,0:T(8,128)(2,1)S(1)} %get-tuple-element.10), kind=kOutput, calls=%fused_computation.49 | convolution fusion | flops 6450577408 | bytes 16252928 | tf_op jit(solution)/shard_map/pqti,pqio->to/dot_general | solution.py:66
  417.0 75.2 %collective-permute-done.7 = bf16[2,1024,1024]{2,1,0:T(8,128)(2,1)} collective-permute-done((bf16[2,1024,1024]{2,1,0:T(8,128)(2,1)}, bf16[2,1024,1024]{2,1,0:T(8,128)(2,1)}, u32[]{:S(2)}, u32[]{:S(2)}) %collective-permute-start.7) | collective-permute-done | bytes 4194336 | tf_op jit(solution)/shard_map/ppermute | solution.py:8
  492.2 3.8 select_bitcast_fusion.1
  496.0 11.9 %fusion.28 = bf16[1,768,1024]{2,1,0:T(8,128)(2,1)} fusion(bf16[1,2,1024,1024]{3,2,1,0:T(8,128)(2,1)} %get-tuple-element.3, bf16[1,2,1024,1024]{3,2,1,0:T(8,128)(2,1)S(1)} %get-tuple-element.2, bf16[1,2,768,1024]{3,2,1,0:T(8,128)(2,1)} %get-tuple-element.9, bf16[1,2,768,1024]{3,2,1,0:T(8,128)(2,1)} %get-tuple-element.8), kind=kOutput, calls=%fused_computation.50 | convolution fusion | flops 6450577408 | bytes 16252928 | tf_op jit(solution)/shard_map/pqto,pqio->ti/dot_general | solution.py:75
  (12 shorter events, 0.0 us)
Async XLA Ops:
  0.6 49.0 %collective-permute-start.2 = (bf16[1024,1024]{1,0:T(8,128)(2,1)}, bf16[1024,1024]{1,0:T(8,128)(2,1)}, u32[]{:S(2)}, u32[]{:S(2)}) collective-permute-start(bf16[1024,1024]{1,0:T(8,128)(2,1)} %bitcast.73), channel_id=1, source_target_pairs={{0,4},{1,5},{2,6},{3,7},{4,0},{5,1},{6,2},{7,3},{8,12},{9,13},{10,... | collective-permute-start | bytes 6291464 | tf_op jit(solution)/shard_map/ppermute | solution.py:8
  52.2 2.7 copy-start.10
  54.9 182.9 %collective-permute-start.3 = (bf16[2,1024,1024]{2,1,0:T(8,128)(2,1)}, bf16[2,1024,1024]{2,1,0:T(8,128)(2,1)}, u32[]{:S(2)}, u32[]{:S(2)}) collective-permute-start(bf16[2,1024,1024]{2,1,0:T(8,128)(2,1)} %pad_maximum_fusion.2), channel_id=1, source_target_pairs={{0,8},{1,9},{2,10},{3,11},{4,12},{5,13},{6,14},{7,15},{8,0},{9,1},... | collective-permute-start | bytes 12582920 | tf_op jit(solution)/shard_map/ppermute | solution.py:8
  240.8 3.8 copy-start
  240.8 5.1 copy-start.3
  240.8 5.1 copy-start.13
  240.8 5.6 %copy-start.14 = (bf16[1,768,1024]{2,1,0:T(8,128)(2,1)S(1)}, bf16[1,768,1024]{2,1,0:T(8,128)(2,1)}, u32[]{:S(2)}) copy-start(bf16[1,768,1024]{2,1,0:T(8,128)(2,1)} %param.3) | copy-start | bytes 4718596
  245.9 22.2 %collective-permute-start.6 = (bf16[2,1024,1024]{2,1,0:T(8,128)(2,1)}, bf16[2,1024,1024]{2,1,0:T(8,128)(2,1)}, u32[]{:S(2)}, u32[]{:S(2)}) collective-permute-start(bf16[2,1024,1024]{2,1,0:T(8,128)(2,1)} %fusion.18), channel_id=1, source_target_pairs={{0,1},{1,0},{2,3},{3,2},{4,5},{5,4},{6,7},{7,6},{8,9},{9,8},{10,11... | collective-permute-start | bytes 12582920 | tf_op jit(solution)/shard_map/ppermute | solution.py:8
  245.9 9.2 %collective-permute-start.4 = (bf16[768,1024]{1,0:T(8,128)(2,1)S(1)}, bf16[768,1024]{1,0:T(8,128)(2,1)}, u32[]{:S(2)}, u32[]{:S(2)}) collective-permute-start(bf16[768,1024]{1,0:T(8,128)(2,1)S(1)} %bitcast.74), channel_id=1, source_target_pairs={{0,1},{1,0},{2,3},{3,2},{4,5},{5,4},{6,7},{7,6},{8,9},{9,8},{10,11... | collective-permute-start | bytes 4718600 | tf_op jit(solution)/shard_map/ppermute | solution.py:8
  246.4 10.9 %collective-permute-start = (bf16[768,1024]{1,0:T(8,128)(2,1)S(1)}, bf16[768,1024]{1,0:T(8,128)(2,1)}, u32[]{:S(2)}, u32[]{:S(2)}) collective-permute-start(bf16[768,1024]{1,0:T(8,128)(2,1)S(1)} %bitcast.75), channel_id=1, source_target_pairs={{0,1},{1,0},{2,3},{3,2},{4,5},{5,4},{6,7},{7,6},{8,9},{9,8},{10,11... | collective-permute-start | bytes 4718600 | tf_op jit(solution)/shard_map/ppermute | solution.py:8
  260.6 1.1 copy-start.11
  260.6 1.7 copy-start.12
  262.2 5.9 %copy-start.4 = (bf16[1,2,1024,1024]{3,2,1,0:T(8,128)(2,1)S(1)}, bf16[1,2,1024,1024]{3,2,1,0:T(8,128)(2,1)}, u32[]{:S(2)}) copy-start(bf16[1,2,1024,1024]{3,2,1,0:T(8,128)(2,1)} %copy-done.3) | copy-start | bytes 12582916
  264.2 3.9 copy-start.1
  264.2 71.2 %collective-permute-start.1 = (bf16[2,768,1024]{2,1,0:T(8,128)(2,1)}, bf16[2,768,1024]{2,1,0:T(8,128)(2,1)}, u32[]{:S(2)}, u32[]{:S(2)}) collective-permute-start(bf16[2,768,1024]{2,1,0:T(8,128)(2,1)} %pad_maximum_fusion.3), channel_id=1, source_target_pairs={{0,2},{1,3},{2,0},{3,1},{4,6},{5,7},{6,4},{7,5},{8,10},{9,11},{10,... | collective-permute-start | bytes 9437192 | tf_op jit(solution)/shard_map/ppermute | solution.py:8
  267.5 135.4 %collective-permute-start.5 = (bf16[2,768,1024]{2,1,0:T(8,128)(2,1)}, bf16[2,768,1024]{2,1,0:T(8,128)(2,1)}, u32[]{:S(2)}, u32[]{:S(2)}) collective-permute-start(bf16[2,768,1024]{2,1,0:T(8,128)(2,1)} %pad_maximum_fusion.4), channel_id=1, source_target_pairs={{0,2},{1,3},{2,0},{3,1},{4,6},{5,7},{6,4},{7,5},{8,10},{9,11},{10,... | collective-permute-start | bytes 9437192 | tf_op jit(solution)/shard_map/ppermute | solution.py:8
  270.7 3.3 copy-start.6
  270.7 4.5 copy-start.8
  275.2 217.0 %collective-permute-start.7 = (bf16[2,1024,1024]{2,1,0:T(8,128)(2,1)}, bf16[2,1024,1024]{2,1,0:T(8,128)(2,1)}, u32[]{:S(2)}, u32[]{:S(2)}) collective-permute-start(bf16[2,1024,1024]{2,1,0:T(8,128)(2,1)} %fusion.12), channel_id=1, source_target_pairs={{0,2},{1,3},{2,0},{3,1},{4,6},{5,7},{6,4},{7,5},{8,10},{9,11},{10,... | collective-permute-start | bytes 12582920 | tf_op jit(solution)/shard_map/ppermute | solution.py:8
  339.6 67.5 %copy-start.2 = (bf16[1,2,1024,1024]{3,2,1,0:T(8,128)(2,1)S(1)}, bf16[1,2,1024,1024]{3,2,1,0:T(8,128)(2,1)}, u32[]{:S(2)}) copy-start(bf16[1,2,1024,1024]{3,2,1,0:T(8,128)(2,1)} %copy-done) | copy-start | bytes 12582916
  339.6 67.5 %copy-start.5 = (bf16[1,2,1024,1024]{3,2,1,0:T(8,128)(2,1)S(1)}, bf16[1,2,1024,1024]{3,2,1,0:T(8,128)(2,1)}, u32[]{:S(2)}) copy-start(bf16[1,2,1024,1024]{3,2,1,0:T(8,128)(2,1)} %copy-done.3) | copy-start | bytes 12582916
  407.1 85.1 %copy-start.7 = (bf16[2,1,1024,1024]{3,2,0,1:T(8,128)(2,1)S(1)}, bf16[2,1,1024,1024]{3,2,0,1:T(8,128)(2,1)}, u32[]{:S(2)}) copy-start(bf16[2,1,1024,1024]{3,2,0,1:T(8,128)(2,1)} %copy-done.6) | copy-start | bytes 12582916
  407.1 85.1 %copy-start.9 = (bf16[2,1,1024,1024]{3,2,0,1:T(8,128)(2,1)S(1)}, bf16[2,1,1024,1024]{3,2,0,1:T(8,128)(2,1)}, u32[]{:S(2)}) copy-start(bf16[2,1,1024,1024]{3,2,0,1:T(8,128)(2,1)} %copy-done.8) | copy-start | bytes 12582916
where the time goes:
time: 508 us
  waiting for transfers between devices  434 us (85%)
  other arithmetic  35.1 us (7%)
  matrix products  21.7 us (4%)
  starting transfers between devices  9.86 us (2%)
  local copies, waits for them, and re-layouts  6.24 us (1%)
    ppermute x8, waiting for transfers between devices, partner_2(): lax.ppermute(value, axis, [(i, i ^ 1 << distance) for i in range(lax.axis...  434 us
    another operation x8, other arithmetic, grow_panel(): panel = jnp.stack([low_part, high_part], 0)  23.7 us
    dot_general x1, matrix products, local(): jnp.einsum(letters + 'to,' + letters + 'io->ti', grad_panel, turned, pref...  11.9 us
  transfers between devices with their start and end apart: 8, of which 7 were waited for; matrix products, arithmetic and copies ran while one was open for 6% of the time, Pallas kernels for 0%

commit v1 on v0

v1 whole, which is shorter than its diff:
```python
import jax
import jax.numpy as jnp
from jax import lax
from jax.sharding import Mesh
from jax.sharding import PartitionSpec as P


def partner_2(value, axis, distance):
    return lax.ppermute(value, axis, [(i, i ^ 1 << distance) for i in range(lax.axis_size(axis))])


def bit_at(device_index, position):
    return jnp.bitwise_and(jnp.right_shift(device_index, position), 1)


def grow_panel(own_block, bit_order, offset, device_index):
    panel = own_block
    for level_bit in bit_order:
        own_bit = bit_at(device_index, offset + level_bit)
        partner = partner_2(panel, "row", offset + level_bit)
        low_part = jnp.where(own_bit == 0, panel, partner)
        high_part = jnp.where(own_bit == 0, partner, panel)
        panel = jnp.stack([low_part, high_part], 0)
    return panel


def turn_panel(panel, layout, device_index, bit_order):
    for level_bit in bit_order:
        axis_at = layout.index(level_bit)
        own_bit = bit_at(device_index, level_bit)
        kept_half = lax.dynamic_index_in_dim(panel, own_bit, axis_at, keepdims=False)
        sent_half = lax.dynamic_index_in_dim(panel, 1 - own_bit, axis_at, keepdims=False)
        partner = partner_2(sent_half, "row", level_bit)
        low_part = jnp.where(own_bit == 0, kept_half, partner)
        high_part = jnp.where(own_bit == 0, partner, kept_half)
        panel = jnp.stack([low_part, high_part], axis_at)
    return panel


def any_grid(head_out, out_grad, proj_weight):
    levels = (lax.axis_size("row").bit_length() - 1) // 2
    device_index = lax.axis_index("row")
    bit_order = list(range(levels))
    layout = bit_order[::-1]
    letters = "pqrsuv"[:levels]
    head_panel = grow_panel(head_out[0], bit_order, 0, device_index)
    weight_panel = grow_panel(proj_weight[0], bit_order, levels, device_index)
    forward = jnp.einsum(
        letters + "ti," + letters + "io->to", head_panel, weight_panel, preferred_element_type=jnp.float32
    )
    turned = turn_panel(weight_panel, layout, device_index, bit_order)
    grad_panel = grow_panel(out_grad[0], bit_order, 0, device_index)
    summed = jnp.einsum(
        letters + "to," + letters + "io->ti", grad_panel, turned, preferred_element_type=jnp.float32
    )
    return forward.astype(jnp.bfloat16)[None], summed.astype(jnp.bfloat16)[None]


def swap(value, axis):
    return lax.ppermute(value, axis, [(0, 1), (1, 0)])


def send(value, pairs):
    return lax.ppermute(value, "a", pairs)


def pick(flag, yes, no):
    return jnp.where(flag, yes, no)


def two_of(flag, first, second):
    return pick(flag == 0, first, second), pick(flag == 0, second, first)


def rows_times(left, right):
    return lax.dot_general(left, right, (((1,), (1,)), ((), ())), preferred_element_type=jnp.float32)


def times(left, right):
    return lax.dot_general(left, right, (((1,), (0,)), ((), ())), preferred_element_type=jnp.float32)


def grid_4(head_out, out_grad, proj_weight):
    group = lax.axis_index("g")
    plane = lax.axis_index("a")
    chip = lax.axis_index("b")
    core = lax.axis_index("k")
    tokens, features = head_out.shape[1:]
    half, quarter = features // 2, features // 4

    weight = proj_weight[0].reshape(2, 2, quarter, -1)
    kept = lax.dynamic_index_in_dim(weight, core, 0, keepdims=False)
    given = lax.dynamic_index_in_dim(weight, 1 - core, 0, keepdims=False)
    own_row = jnp.stack([kept, swap(given, "k")], 0)
    mine = lax.dynamic_index_in_dim(own_row, group, 1, keepdims=False)
    other = lax.dynamic_index_in_dim(own_row, 1 - group, 1, keepdims=False)

    heads = head_out[0].reshape(tokens, 2, half)
    head_kept = lax.dynamic_index_in_dim(heads, core, 1, keepdims=False)
    head_given = lax.dynamic_index_in_dim(heads, 1 - core, 1, keepdims=False)
    head_pair = jnp.stack([head_kept, swap(head_given, "k")], 0)
    head_far = swap(head_pair, "b")
    grad_0 = out_grad[0]
    grad_1 = swap(grad_0, "k")

    is_mid = (plane == 1) | (plane == 2)
    near_a = send(mine, [(0, 1), (1, 0), (2, 3), (3, 2)])
    middle = send(mine, [(1, 2), (2, 1)])
    end_1 = send(middle, [(1, 0), (2, 3)])
    cross = send(near_a, [(1, 2), (2, 1)])
    end_2 = send(cross, [(1, 0), (2, 3)])
    far_1 = pick(is_mid, middle, end_1)
    far_2 = pick(is_mid, cross, end_2)
    near_x = swap(near_a, "g")
    far_1x = swap(far_1, "g")
    far_2x = swap(far_2, "g")

    def back(piece):
        return rows_times(grad_0, piece[0]) + rows_times(grad_1, piece[1])

    early = plane // 2 != chip

    def exchange(near_piece, far_piece):
        near_sum, far_sum = back(near_piece), back(far_piece)
        there = swap(pick(early, near_sum, far_sum), "b")
        return (pick(early, far_sum, near_sum) + there).astype(jnp.bfloat16)

    grads_z = exchange(mine, far_1), exchange(near_a, far_2)
    grads_x = exchange(other, far_1x), exchange(near_x, far_2x)
    first = jnp.stack(two_of(group, grads_z[0], grads_x[0]), 1)
    second = jnp.stack(two_of(group, grads_z[1], grads_x[1]), 1)
    parity = pick(early, plane // 2, plane & 1)
    mine_out, theirs_out = two_of(parity ^ core, first, second)
    got = swap(theirs_out, "k")
    low, high = two_of(core, mine_out, got)
    head_grad = jnp.concatenate([low.reshape(tokens, half), high.reshape(tokens, half)], 1)

    head_all = jnp.concatenate([head_pair, head_far], 0).reshape(4, tokens, 2, quarter)

    def head_of(row, of_group):
        slot = 2 * (row // 2 != chip) + ((row & 1) != core)
        return head_all[slot, :, of_group]

    low_plane = plane < 2
    rows = [plane, plane ^ 1, pick(low_plane, 2, 1), pick(low_plane, 3, 0)]
    pieces_z = [mine, near_a, far_1, far_2]
    pieces_x = [other, near_x, far_1x, far_2x]
    lhs = jnp.concatenate([head_of(r, group) for r in rows] + [head_of(r, 1 - group) for r in rows], 1)
    totals = [
        times(lhs, jnp.concatenate([piece[slot] for piece in pieces_z + pieces_x], 0)) for slot in (0, 1)
    ]
    projected = (totals[0] + swap(totals[1], "k")).astype(jnp.bfloat16)
    return projected[None], head_grad[None]


def solution(mesh):
    n_group, n_row = mesh.shape["groups"], mesh.shape["row"]
    if (n_group, n_row) == (2, 16):
        grid = Mesh(mesh.devices.reshape(2, 4, 2, 2), ("g", "a", "b", "k"))
        tokens, whole = P(("a", "b", "k"), "g", None), P(("a", "b", "k"), None, None)
        body = grid_4
    else:
        grid = mesh
        tokens, whole = P("row", "groups", None), P("row", None, None)
        body = any_grid
    return jax.shard_map(
        body, mesh=grid, in_specs=(tokens, tokens, whole), out_specs=(tokens, tokens), check_vma=False
    )
```

time: 508 us -> 176 us (0.35)
  waiting for transfers between devices: 434 us -> 95.6 us
  other arithmetic: 35.1 us -> 15.9 us
  local copies, waits for them, and re-layouts: 6.24 us -> 20.7 us
  starting transfers between devices: 9.86 us -> 19.9 us
    ppermute x8 -> x18, waiting for transfers between devices: 434 us -> 95.6 us  [the longest x13 51.8 us: swap(): return lax.ppermute(value, axis, [(0, 1), (1, 0)])]
    another operation x10 -> x6, other arithmetic: 30.1 us -> 8.13 us  [the longest x1 2.66 us: grid_4(): head_pair = jnp.stack([head_kept, swap(head_given, 'k')], 0)]
    ppermute x8 -> x18, starting transfers between devices: 9.86 us -> 19.9 us  [the longest x13 11.3 us: swap(): return lax.ppermute(value, axis, [(0, 1), (1, 0)])]
    concatenate x0 -> x6, local copies, waits for them, and re-layouts: none -> 8.36 us  [the longest x4 8.24 us: grid_4(): jnp.concatenate([head_pair, head_far], 0).reshape(4, tokens, 2, quarter)]
    select_n x0 -> x8, other arithmetic: none -> 6.04 us  [pick(): return jnp.where(flag, yes, no)]
    dynamic_slice x0 -> x3, local copies, waits for them, and re-layouts: none -> 5.89 us  [the longest x2 3.6 us: grid_4(): head_kept = lax.dynamic_index_in_dim(heads, core, 1, keepdims=False)]
    dot_general x2 -> x18, matrix products: 21.7 us -> 22.4 us  [the longest x2 12.4 us: times(): lax.dot_general(left, right, (((1,), (0,)), ((), ())), preferred_element_...]
  transfers between devices with their start and end apart: 8 -> 18, of which waited for: 7 -> 7; matrix products, arithmetic and copies ran while one was open for 6% -> 27% of each run, Pallas kernels for 0% -> 0%
where the time goes in v1:
time: 176 us
  waiting for transfers between devices  95.6 us (54%)
  matrix products  22.4 us (13%)
  local copies, waits for them, and re-layouts  20.7 us (12%)
  starting transfers between devices  19.9 us (11%)
  other arithmetic  15.9 us (9%)
    ppermute x13, waiting for transfers between devices, swap(): return lax.ppermute(value, axis, [(0, 1), (1, 0)])  51.8 us
    ppermute x5, waiting for transfers between devices, send(): return lax.ppermute(value, 'a', pairs)  43.8 us
    dot_general x2, matrix products, times(): lax.dot_general(left, right, (((1,), (0,)), ((), ())), preferred_element_...  12.4 us
    ppermute x13, starting transfers between devices, swap(): return lax.ppermute(value, axis, [(0, 1), (1, 0)])  11.3 us
    dot_general x16, matrix products, rows_times(): lax.dot_general(left, right, (((1,), (1,)), ((), ())), preferred_element_...  10.1 us
    ppermute x5, starting transfers between devices, send(): return lax.ppermute(value, 'a', pairs)  8.59 us
    concatenate x4, local copies, waits for them, and re-layouts, grid_4(): jnp.concatenate([head_pair, head_far], 0).reshape(4, tokens, 2, quarter)  8.24 us
    select_n x8, other arithmetic, pick(): return jnp.where(flag, yes, no)  6.04 us
  transfers between devices with their start and end apart: 18, of which 7 were waited for; matrix products, arithmetic and copies ran while one was open for 27% of the time, Pallas kernels for 0%

profile of v1, /device:TPU:0, one launch (start us, length us, event | category | flops | bytes accessed | tf_op | source)
XLA Modules:
  0.0 175.8 jit_solution(16664597644762372535)
XLA Ops:
  0.6 3.1 %dynamic-slice_bitcast_fusion = (bf16[2,256,1024]{2,1,0:T(8,128)(2,1)}, bf16[1,2,256,1024]{3,2,1,0:T(8,128)(2,1)}) fusion(bf16[2,2,256,1024]{3,2,1,0:T(8,128)(2,1)} %bitcast.190, s32[]{:T(128)S(6)} %select_n.188, s32[]{:T(128)S(6)} %select_n.187), kind=kLoop, calls=%fused_computation.20 | loop fusion | bytes 4194312 | tf_op jit(solution)/shard_map/jit(dynamic_index_in_dim)/squeeze | solution.py:93
  4.2 0.7 copy.7
  5.0 1.3 constant_dynamic-slice_fusion.2
  6.2 2.3 %copy.8 = bf16[768,1,512]{2,0,1:T(8,128)(2,1)} copy(bf16[768,1,512]{0,2,1:T(8,128)(2,1)} %get-tuple-element.15) | data formatting | bytes 1572864 | tf_op jit(solution)/shard_map/jit(dynamic_index_in_dim)/dynamic_slice | solution.py:100
  9.1 2.3 %copy.9 = bf16[768,1,512]{2,0,1:T(8,128)(2,1)} copy(bf16[768,1,512]{0,2,1:T(8,128)(2,1)} %get-tuple-element.14) | data formatting | bytes 1572864 | tf_op jit(solution)/shard_map/jit(dynamic_index_in_dim)/dynamic_slice | solution.py:99
  11.4 2.3 %copy.10 = bf16[1,768,2,256]{3,1,2,0:T(8,128)(2,1)} copy(bf16[1,768,2,256]{1,3,2,0:T(8,128)(2,1)} %bitcast.184) | data formatting | bytes 1572864 | tf_op jit(solution)/shard_map/concatenate | solution.py:138
  13.7 2.7 %pad_maximum_fusion.1 = bf16[2,768,512]{2,1,0:T(8,128)(2,1)} fusion(bf16[1,768,512]{2,1,0:T(8,128)(2,1)} %bitcast.4, bf16[1,768,512]{2,1,0:T(8,128)(2,1)} %bitcast.187), kind=kLoop, calls=%fused_computation.7 | loop fusion | flops 786432 | bytes 3145728 | tf_op jit(solution)/shard_map/stack | solution.py:101
  16.3 2.5 %collective-permute-start.1 = (bf16[2,768,512]{2,1,0:T(8,128)(2,1)}, bf16[2,768,512]{2,1,0:T(8,128)(2,1)}, u32[]{:S(2)}, u32[]{:S(2)}) collective-permute-start(bf16[2,768,512]{2,1,0:T(8,128)(2,1)} %pad_maximum_fusion.1), channel_id=1, source_target_pairs={{0,2},{2,0},{1,3},{3,1},{4,6},{6,4},{5,7},{7,5},{8,10},{10,8},{9,1... | collective-permute-start | bytes 4718600 | tf_op jit(solution)/shard_map/ppermute | solution.py:60
  18.8 2.9 %concatenate.24 = bf16[1,768,2,256]{3,2,1,0:T(2,128)(2,1)} reshape(bf16[768,512]{1,0:T(8,128)(2,1)} %collective-permute-done) | data formatting | bytes 1572864 | tf_op jit(solution)/shard_map/concatenate | solution.py:138
  21.8 1.2 copy.11
  23.0 1.7 fusion.1
  24.7 0.7 collective-permute-start.4
  25.5 4.4 %collective-permute-start.3 = (bf16[2,256,1024]{2,1,0:T(8,128)(2,1)S(1)}, bf16[2,256,1024]{2,1,0:T(8,128)(2,1)S(1)}, u32[]{:S(2)}, u32[]{:S(2)}) collective-permute-start(bf16[2,256,1024]{2,1,0:T(8,128)(2,1)S(1)} %bitcast.183), channel_id=1, source_target_pairs={{0,4},{4,0},{8,12},{12,8},{1,5},{5,1},{9,13},{13,9},{2,6},{6,2},{1... | collective-permute-start | bytes 3145736 | tf_op jit(solution)/shard_map/ppermute | solution.py:64
  31.2 0.6 convolution_add_fusion.4
  32.5 20.6 %collective-permute-done.3 = bf16[2,256,1024]{2,1,0:T(8,128)(2,1)S(1)} collective-permute-done((bf16[2,256,1024]{2,1,0:T(8,128)(2,1)S(1)}, bf16[2,256,1024]{2,1,0:T(8,128)(2,1)S(1)}, u32[]{:S(2)}, u32[]{:S(2)}) %collective-permute-start.3) | collective-permute-done | bytes 1048608 | tf_op jit(solution)/shard_map/ppermute | solution.py:64
  53.1 0.7 collective-permute-start.6
  53.9 1.6 collective-permute-start.8
  55.4 1.3 collective-permute-start.5
  57.4 0.6 convolution_add_fusion.2
  58.1 1.8 %copy.17 = bf16[2,96,2,8,256]{4,3,1,2,0:T(8,128)(2,1)S(1)} copy(bf16[2,96,2,8,256]{4,3,2,1,0:T(8,128)(2,1)} %bitcast.50) | data formatting | bytes 3145728 | tf_op jit(solution)/shard_map/concatenate | solution.py:138
  60.7 21.3 %collective-permute-done.5 = bf16[2,256,1024]{2,1,0:T(8,128)(2,1)S(1)} collective-permute-done((bf16[2,256,1024]{2,1,0:T(8,128)(2,1)S(1)}, bf16[2,256,1024]{2,1,0:T(8,128)(2,1)S(1)}, u32[]{:S(2)}, u32[]{:S(2)}) %collective-permute-start.5) | collective-permute-done | bytes 1048608 | tf_op jit(solution)/shard_map/ppermute | solution.py:64
  83.3 0.6 convolution_add_fusion.7
  84.0 1.1 select_bitcast_fusion.3
  85.6 1.5 collective-permute-start.7
  87.1 0.6 fusion.25
  87.7 0.6 convolution_add_fusion
  88.5 16.8 %collective-permute-done.9 = bf16[2,256,1024]{2,1,0:T(8,128)(2,1)S(1)} collective-permute-done((bf16[2,256,1024]{2,1,0:T(8,128)(2,1)S(1)}, bf16[2,256,1024]{2,1,0:T(8,128)(2,1)S(1)}, u32[]{:S(2)}, u32[]{:S(2)}) %collective-permute-start.9) | collective-permute-done | bytes 1048608 | tf_op jit(solution)/shard_map/ppermute | solution.py:60
  105.2 0.6 fusion.27
  105.9 0.6 convolution_add_fusion.5
  106.5 1.1 select_bitcast_fusion.2
  108.2 1.8 %collective-permute-done.7 = bf16[2,256,1024]{2,1,0:T(8,128)(2,1)S(1)} collective-permute-done((bf16[2,256,1024]{2,1,0:T(8,128)(2,1)S(1)}, bf16[2,256,1024]{2,1,0:T(8,128)(2,1)S(1)}, u32[]{:S(2)}, u32[]{:S(2)}) %collective-permute-start.7) | collective-permute-done | bytes 1048608 | tf_op jit(solution)/shard_map/ppermute | solution.py:64
  110.1 1.6 collective-permute-start.10
  112.3 0.6 convolution_add_fusion.3
  112.9 1.1 select_bitcast_fusion.1
  114.0 1.5 collective-permute-start.15
  115.9 15.9 %collective-permute-done.10 = bf16[2,256,1024]{2,1,0:T(8,128)(2,1)S(1)} collective-permute-done((bf16[2,256,1024]{2,1,0:T(8,128)(2,1)S(1)}, bf16[2,256,1024]{2,1,0:T(8,128)(2,1)S(1)}, u32[]{:S(2)}, u32[]{:S(2)}) %collective-permute-start.10) | collective-permute-done | bytes 1048608 | tf_op jit(solution)/shard_map/ppermute | solution.py:60
  131.8 5.2 %fusion.43 = f32[768,1024]{1,0:T(8,128)} fusion(bf16[768,2048]{1,0:T(8,128)(2,1)S(1)} %bitcast_dynamic-update-slice_fusion, bf16[2048,1024]{1,0:T(8,128)(2,1)S(1)} %get-tuple-element.17), kind=kOutput, calls=%fused_computation.104 | convolution fusion | flops 3221225472 | bytes 10485760 | tf_op jit(solution)/shard_map/dot_general | solution.py:80
  137.7 0.6 convolution_add_fusion.1
  138.4 1.1 select_bitcast_fusion
  139.5 1.5 collective-permute-start.16
  141.1 1.8 %select_bitcast_fusion.7 = (bf16[768,1,256]{0,2,1:T(8,128)(2,1)S(1)}, bf16[768,256]{0,1:T(8,128)(2,1)S(1)}, bf16[768,256]{0,1:T(8,128)(2,1)S(1)}) fusion(pred[]{:T(512)S(6)} %eq.24, f32[768,256]{0,1:T(8,128)} %collective-permute-done.13, f32[256,768]{1,0:T(8,128)} %copy-done.9, f32[256,768]{1,0:T(8,128)S(1)} %copy-done.4, pred[]{:T(512)S(6)} %ne.75, ...), kind=kLoop, calls=%fused_computation.92 | loop fusion | flops 1376256 | bytes 5898242 | tf_op jit(solution)/shard_map/stack | solution.py:130
  143.0 16.8 %collective-permute-done.16 = f32[768,256]{0,1:T(8,128)} collective-permute-done((f32[768,256]{0,1:T(8,128)}, f32[768,256]{0,1:T(8,128)}, u32[]{:S(2)}, u32[]{:S(2)}) %collective-permute-start.16) | collective-permute-done | bytes 786464 | tf_op jit(solution)/shard_map/ppermute | solution.py:60
  159.8 1.8 %select_bitcast_fusion.5 = (bf16[768,1,256]{0,2,1:T(8,128)(2,1)S(1)}, bf16[768,256]{0,1:T(8,128)(2,1)S(1)}, bf16[768,256]{0,1:T(8,128)(2,1)S(1)}) fusion(pred[]{:T(512)S(6)} %eq.24, f32[768,256]{0,1:T(8,128)} %collective-permute-done.15, f32[256,768]{1,0:T(8,128)S(1)} %copy-done.11, f32[256,768]{1,0:T(8,128)S(1)} %copy-done.6, pred[]{:T(512)S(6)} %ne.75, ...), kind=kLoop, calls=%fused_computation.90 | loop fusion | flops 1376256 | bytes 5898242 | tf_op jit(solution)/shard_map/stack | solution.py:131
  161.9 2.4 %collective-permute-done.17 = bf16[768,2,256]{0,2,1:T(8,128)(2,1)} collective-permute-done((bf16[768,2,256]{0,2,1:T(8,128)(2,1)S(1)}, bf16[768,2,256]{0,2,1:T(8,128)(2,1)}, u32[]{:S(2)}, u32[]{:S(2)}) %collective-permute-start.17) | collective-permute-done | bytes 786464 | tf_op jit(solution)/shard_map/ppermute | solution.py:60
  164.3 1.3 broadcast_select_fusion.5
  166.2 1.4 maximum_bitcast_fusion
  167.6 1.1 copy-done.19
  168.6 7.1 %fusion = bf16[1,768,1024]{2,1,0:T(8,128)(2,1)} fusion(f32[768,1024]{1,0:T(8,128)} %collective-permute-done.11, bf16[768,2048]{1,0:T(8,128)(2,1)S(1)} %copy-done.19, bf16[2048,1024]{1,0:T(8,128)(2,1)} %copy-done.17), kind=kOutput, calls=%fused_computation.9 | convolution fusion | flops 3222798336 | bytes 12058624 | tf_op jit(solution)/shard_map/dot_general | solution.py:80
  (89 shorter events, 9.4 us)
Async XLA Ops:
  0.6 3.6 %copy-start.16 = (bf16[1,768,1024]{2,1,0:T(8,128)(2,1)S(1)}, bf16[1,768,1024]{2,1,0:T(8,128)(2,1)}, u32[]{:S(2)}) copy-start(bf16[1,768,1024]{2,1,0:T(8,128)(2,1)} %param.3) | copy-start | bytes 4718596
  3.8 19.2 %collective-permute-start.2 = (bf16[2,256,1024]{2,1,0:T(8,128)(2,1)}, bf16[2,256,1024]{2,1,0:T(8,128)(2,1)}, u32[]{:S(2)}, u32[]{:S(2)}) collective-permute-start(bf16[2,256,1024]{2,1,0:T(8,128)(2,1)} %get-tuple-element.12), channel_id=1, source_target_pairs={{0,1},{1,0},{2,3},{3,2},{4,5},{5,4},{6,7},{7,6},{8,9},{9,8},{10,11... | collective-permute-start | bytes 3145736 | tf_op jit(solution)/shard_map/ppermute | solution.py:60
  4.9 3.6 %copy-start = (bf16[1,768,1024]{2,1,0:T(8,128)(2,1)S(1)}, bf16[1,768,1024]{2,1,0:T(8,128)(2,1)}, u32[]{:S(2)}) copy-start(bf16[1,768,1024]{2,1,0:T(8,128)(2,1)} %param.4) | copy-start | bytes 4718596
  8.5 5.1 %collective-permute-start = (bf16[768,512]{1,0:T(8,128)(2,1)}, bf16[768,512]{1,0:T(8,128)(2,1)}, u32[]{:S(2)}, u32[]{:S(2)}) collective-permute-start(bf16[768,512]{1,0:T(8,128)(2,1)} %bitcast.2), channel_id=1, source_target_pairs={{0,1},{1,0},{2,3},{3,2},{4,5},{5,4},{6,7},{7,6},{8,9},{9,8},{10,11... | collective-permute-start | bytes 2359304 | tf_op jit(solution)/shard_map/ppermute | solution.py:60
  8.6 22.6 %collective-permute-start.12 = (bf16[768,1024]{1,0:T(8,128)(2,1)S(1)}, bf16[768,1024]{1,0:T(8,128)(2,1)S(1)}, u32[]{:S(2)}, u32[]{:S(2)}) collective-permute-start(bf16[768,1024]{1,0:T(8,128)(2,1)S(1)} %bitcast.181), channel_id=1, source_target_pairs={{0,1},{1,0},{2,3},{3,2},{4,5},{5,4},{6,7},{7,6},{8,9},{9,8},{10,11... | collective-permute-start | bytes 4718600 | tf_op jit(solution)/shard_map/ppermute | solution.py:60
  16.3 41.7 %collective-permute-start.1 = (bf16[2,768,512]{2,1,0:T(8,128)(2,1)}, bf16[2,768,512]{2,1,0:T(8,128)(2,1)}, u32[]{:S(2)}, u32[]{:S(2)}) collective-permute-start(bf16[2,768,512]{2,1,0:T(8,128)(2,1)} %pad_maximum_fusion.1), channel_id=1, source_target_pairs={{0,2},{2,0},{1,3},{3,1},{4,6},{6,4},{5,7},{7,5},{8,10},{10,8},{9,1... | collective-permute-start | bytes 4718600 | tf_op jit(solution)/shard_map/ppermute | solution.py:60
  24.7 30.7 %collective-permute-start.4 = (bf16[2,256,1024]{2,1,0:T(8,128)(2,1)S(1)}, bf16[2,256,1024]{2,1,0:T(8,128)(2,1)S(1)}, u32[]{:S(2)}, u32[]{:S(2)}) collective-permute-start(bf16[2,256,1024]{2,1,0:T(8,128)(2,1)S(1)} %bitcast.182), channel_id=1, source_target_pairs={{4,8},{8,4},{5,9},{9,5},{6,10},{10,6},{7,11},{11,7},{20,24},{24,20... | collective-permute-start | bytes 3145736 | tf_op jit(solution)/shard_map/ppermute | solution.py:64
  25.5 27.7 %collective-permute-start.3 = (bf16[2,256,1024]{2,1,0:T(8,128)(2,1)S(1)}, bf16[2,256,1024]{2,1,0:T(8,128)(2,1)S(1)}, u32[]{:S(2)}, u32[]{:S(2)}) collective-permute-start(bf16[2,256,1024]{2,1,0:T(8,128)(2,1)S(1)} %bitcast.183), channel_id=1, source_target_pairs={{0,4},{4,0},{8,12},{12,8},{1,5},{5,1},{9,13},{13,9},{2,6},{6,2},{1... | collective-permute-start | bytes 3145736 | tf_op jit(solution)/shard_map/ppermute | solution.py:64
  31.8 74.7 %copy-start.1 = (f32[256,768]{1,0:T(8,128)}, f32[256,768]{1,0:T(8,128)S(1)}, u32[]{:S(2)}) copy-start(f32[256,768]{1,0:T(8,128)S(1)} %convolution_add_fusion.4) | copy-start | bytes 2359300
  32.5 51.5 %copy-start.3 = (f32[256,768]{1,0:T(8,128)}, f32[256,768]{1,0:T(8,128)S(1)}, u32[]{:S(2)}) copy-start(f32[256,768]{1,0:T(8,128)S(1)} %convolution_add_fusion.6) | copy-start | bytes 2359300
  53.1 32.5 %collective-permute-start.6 = (bf16[2,256,1024]{2,1,0:T(8,128)(2,1)S(1)}, bf16[2,256,1024]{2,1,0:T(8,128)(2,1)S(1)}, u32[]{:S(2)}, u32[]{:S(2)}) collective-permute-start(bf16[2,256,1024]{2,1,0:T(8,128)(2,1)S(1)} %collective-permute-done.3), channel_id=1, source_target_pairs={{4,8},{8,4},{5,9},{9,5},{6,10},{10,6},{7,11},{11,7},{20,24},{24,20... | collective-permute-start | bytes 3145736 | tf_op jit(solution)/shard_map/ppermute | solution.py:64
  53.9 33.2 %collective-permute-start.8 = (bf16[2,256,1024]{2,1,0:T(8,128)(2,1)S(1)}, bf16[2,256,1024]{2,1,0:T(8,128)(2,1)S(1)}, u32[]{:S(2)}, u32[]{:S(2)}) collective-permute-start(bf16[2,256,1024]{2,1,0:T(8,128)(2,1)S(1)} %collective-permute-done.3), channel_id=1, source_target_pairs={{0,16},{16,0},{1,17},{17,1},{2,18},{18,2},{3,19},{19,3},{4,20},{20... | collective-permute-start | bytes 3145736 | tf_op jit(solution)/shard_map/ppermute | solution.py:60
  55.4 26.6 %collective-permute-start.5 = (bf16[2,256,1024]{2,1,0:T(8,128)(2,1)S(1)}, bf16[2,256,1024]{2,1,0:T(8,128)(2,1)S(1)}, u32[]{:S(2)}, u32[]{:S(2)}) collective-permute-start(bf16[2,256,1024]{2,1,0:T(8,128)(2,1)S(1)} %collective-permute-done.4), channel_id=1, source_target_pairs={{4,0},{8,12},{5,1},{9,13},{6,2},{10,14},{7,3},{11,15},{20,16},{24,... | collective-permute-start | bytes 3145736 | tf_op jit(solution)/shard_map/ppermute | solution.py:64
  57.4 2.5 %copy-start.15 = (bf16[1,768,2,256]{3,1,2,0:T(8,128)(2,1)S(1)}, bf16[1,768,2,256]{3,1,2,0:T(8,128)(2,1)}, u32[]{:S(2)}) copy-start(bf16[1,768,2,256]{3,1,2,0:T(8,128)(2,1)} %copy.10) | copy-start | bytes 2359300
  58.1 54.9 %copy-start.5 = (f32[256,768]{1,0:T(8,128)}, f32[256,768]{1,0:T(8,128)S(1)}, u32[]{:S(2)}) copy-start(f32[256,768]{1,0:T(8,128)S(1)} %convolution_add_fusion.2) | copy-start | bytes 2359300
  60.7 71.1 %copy-start.18 = (bf16[768,2048]{1,0:T(8,128)(2,1)}, bf16[768,2048]{1,0:T(8,128)(2,1)S(1)}, u32[]{:S(2)}) copy-start(bf16[768,2048]{1,0:T(8,128)(2,1)S(1)} %bitcast_dynamic-update-slice_fusion) | copy-start | bytes 9437188
  82.1 23.1 %collective-permute-start.9 = (bf16[2,256,1024]{2,1,0:T(8,128)(2,1)S(1)}, bf16[2,256,1024]{2,1,0:T(8,128)(2,1)S(1)}, u32[]{:S(2)}, u32[]{:S(2)}) collective-permute-start(bf16[2,256,1024]{2,1,0:T(8,128)(2,1)S(1)} %broadcast_select_fusion.1), channel_id=1, source_target_pairs={{0,16},{16,0},{1,17},{17,1},{2,18},{18,2},{3,19},{19,3},{4,20},{20... | collective-permute-start | bytes 3145736 | tf_op jit(solution)/shard_map/ppermute | solution.py:60
  84.0 4.4 %copy-start.9 = (f32[256,768]{1,0:T(8,128)}, f32[256,768]{1,0:T(8,128)S(1)}, u32[]{:S(2)}) copy-start(f32[256,768]{1,0:T(8,128)S(1)} %convolution_add_fusion.7) | copy-start | bytes 2359300
  85.1 56.0 %collective-permute-start.13 = (f32[768,256]{0,1:T(8,128)}, f32[768,256]{0,1:T(8,128)}, u32[]{:S(2)}, u32[]{:S(2)}) collective-permute-start(f32[768,256]{0,1:T(8,128)} %select_bitcast_fusion.3), channel_id=1, source_target_pairs={{0,2},{2,0},{1,3},{3,1},{4,6},{6,4},{5,7},{7,5},{8,10},{10,8},{9,1... | collective-permute-start | bytes 2359304 | tf_op jit(solution)/shard_map/ppermute | solution.py:60
  85.6 24.4 %collective-permute-start.7 = (bf16[2,256,1024]{2,1,0:T(8,128)(2,1)S(1)}, bf16[2,256,1024]{2,1,0:T(8,128)(2,1)S(1)}, u32[]{:S(2)}, u32[]{:S(2)}) collective-permute-start(bf16[2,256,1024]{2,1,0:T(8,128)(2,1)S(1)} %collective-permute-done.6), channel_id=1, source_target_pairs={{4,0},{8,12},{5,1},{9,13},{6,2},{10,14},{7,3},{11,15},{20,16},{24,... | collective-permute-start | bytes 3145736 | tf_op jit(solution)/shard_map/ppermute | solution.py:64
  88.4 50.0 %copy-start.7 = (f32[256,768]{1,0:T(8,128)}, f32[256,768]{1,0:T(8,128)S(1)}, u32[]{:S(2)}) copy-start(f32[256,768]{1,0:T(8,128)S(1)} %convolution_add_fusion) | copy-start | bytes 2359300
  106.5 1.6 copy-start.12
  107.7 33.4 %collective-permute-start.14 = (f32[768,256]{0,1:T(8,128)}, f32[768,256]{0,1:T(8,128)}, u32[]{:S(2)}, u32[]{:S(2)}) collective-permute-start(f32[768,256]{0,1:T(8,128)} %select_bitcast_fusion.2), channel_id=1, source_target_pairs={{0,2},{2,0},{1,3},{3,1},{4,6},{6,4},{5,7},{7,5},{8,10},{10,8},{9,1... | collective-permute-start | bytes 2359304 | tf_op jit(solution)/shard_map/ppermute | solution.py:60
  110.1 21.6 %collective-permute-start.10 = (bf16[2,256,1024]{2,1,0:T(8,128)(2,1)S(1)}, bf16[2,256,1024]{2,1,0:T(8,128)(2,1)S(1)}, u32[]{:S(2)}, u32[]{:S(2)}) collective-permute-start(bf16[2,256,1024]{2,1,0:T(8,128)(2,1)S(1)} %broadcast_select_fusion), channel_id=1, source_target_pairs={{0,16},{16,0},{1,17},{17,1},{2,18},{18,2},{3,19},{19,3},{4,20},{20... | collective-permute-start | bytes 3145736 | tf_op jit(solution)/shard_map/ppermute | solution.py:60
  112.9 2.8 %copy-start.10 = (f32[256,768]{1,0:T(8,128)}, f32[256,768]{1,0:T(8,128)S(1)}, u32[]{:S(2)}) copy-start(f32[256,768]{1,0:T(8,128)S(1)} %convolution_add_fusion.3) | copy-start | bytes 2359300
  114.0 29.0 %collective-permute-start.15 = (f32[768,256]{0,1:T(8,128)}, f32[768,256]{0,1:T(8,128)}, u32[]{:S(2)}, u32[]{:S(2)}) collective-permute-start(f32[768,256]{0,1:T(8,128)} %select_bitcast_fusion.1), channel_id=1, source_target_pairs={{0,2},{2,0},{1,3},{3,1},{4,6},{6,4},{5,7},{7,5},{8,10},{10,8},{9,1... | collective-permute-start | bytes 2359304 | tf_op jit(solution)/shard_map/ppermute | solution.py:60
  131.8 5.3 %copy-start.17 = (bf16[2048,1024]{1,0:T(8,128)(2,1)}, bf16[2048,1024]{1,0:T(8,128)(2,1)S(1)}, u32[]{:S(2)}) copy-start(bf16[2048,1024]{1,0:T(8,128)(2,1)S(1)} %get-tuple-element.16) | copy-start | bytes 12582916
  137.1 30.5 %collective-permute-start.11 = (f32[768,1024]{1,0:T(8,128)}, f32[768,1024]{1,0:T(8,128)}, u32[]{:S(2)}, u32[]{:S(2)}) collective-permute-start(f32[768,1024]{1,0:T(8,128)} %fusion.43), channel_id=1, source_target_pairs={{0,1},{1,0},{2,3},{3,2},{4,5},{5,4},{6,7},{7,6},{8,9},{9,8},{10,11... | collective-permute-start | bytes 9437192 | tf_op jit(solution)/shard_map/ppermute | solution.py:60
  137.7 3.4 %copy-start.2 = (f32[256,768]{1,0:T(8,128)S(1)}, f32[256,768]{1,0:T(8,128)}, u32[]{:S(2)}) copy-start(f32[256,768]{1,0:T(8,128)} %copy-done.1) | copy-start | bytes 2359300
  137.7 3.4 %copy-start.4 = (f32[256,768]{1,0:T(8,128)S(1)}, f32[256,768]{1,0:T(8,128)}, u32[]{:S(2)}) copy-start(f32[256,768]{1,0:T(8,128)} %copy-done.3) | copy-start | bytes 2359300
  138.4 1.1 copy-start.13
  139.5 20.3 %collective-permute-start.16 = (f32[768,256]{0,1:T(8,128)}, f32[768,256]{0,1:T(8,128)}, u32[]{:S(2)}, u32[]{:S(2)}) collective-permute-start(f32[768,256]{0,1:T(8,128)} %select_bitcast_fusion), channel_id=1, source_target_pairs={{0,2},{2,0},{1,3},{3,1},{4,6},{6,4},{5,7},{7,5},{8,10},{10,8},{9,1... | collective-permute-start | bytes 2359304 | tf_op jit(solution)/shard_map/ppermute | solution.py:60
  141.0 18.7 %copy-start.6 = (f32[256,768]{1,0:T(8,128)S(1)}, f32[256,768]{1,0:T(8,128)}, u32[]{:S(2)}) copy-start(f32[256,768]{1,0:T(8,128)} %copy-done.5) | copy-start | bytes 2359300
  141.0 18.7 %copy-start.8 = (f32[256,768]{1,0:T(8,128)S(1)}, f32[256,768]{1,0:T(8,128)}, u32[]{:S(2)}) copy-start(f32[256,768]{1,0:T(8,128)} %copy-done.7) | copy-start | bytes 2359300
  141.1 18.7 %copy-start.11 = (f32[256,768]{1,0:T(8,128)S(1)}, f32[256,768]{1,0:T(8,128)}, u32[]{:S(2)}) copy-start(f32[256,768]{1,0:T(8,128)} %copy-done.10) | copy-start | bytes 2359300
  141.1 18.8 %copy-start.14 = (f32[256,768]{1,0:T(8,128)S(1)}, f32[256,768]{1,0:T(8,128)}, u32[]{:S(2)}) copy-start(f32[256,768]{1,0:T(8,128)} %copy-done.13) | copy-start | bytes 2359300
  161.8 2.5 %collective-permute-start.17 = (bf16[768,2,256]{0,2,1:T(8,128)(2,1)S(1)}, bf16[768,2,256]{0,2,1:T(8,128)(2,1)}, u32[]{:S(2)}, u32[]{:S(2)}) collective-permute-start(bf16[768,2,256]{0,2,1:T(8,128)(2,1)S(1)} %broadcast_select_fusion.2), channel_id=1, source_target_pairs={{0,1},{1,0},{2,3},{3,2},{4,5},{5,4},{6,7},{7,6},{8,9},{9,8},{10,11... | collective-permute-start | bytes 2359304 | tf_op jit(solution)/shard_map/ppermute | solution.py:60
  166.2 2.5 %copy-start.19 = (bf16[768,2048]{1,0:T(8,128)(2,1)S(1)}, bf16[768,2048]{1,0:T(8,128)(2,1)}, u32[]{:S(2)}) copy-start(bf16[768,2048]{1,0:T(8,128)(2,1)} %copy-done.18) | copy-start | bytes 9437188

commit v2 on v1

v2 whole, which is shorter than its diff:
```python
import functools

import jax
import jax.numpy as jnp
from jax import lax
from jax.experimental import pallas as pl
from jax.experimental.pallas import tpu as pltpu
from jax.sharding import Mesh
from jax.sharding import PartitionSpec as P


def partner_2(value, axis, distance):
    return lax.ppermute(value, axis, [(i, i ^ 1 << distance) for i in range(lax.axis_size(axis))])


def bit_at(device_index, position):
    return jnp.bitwise_and(jnp.right_shift(device_index, position), 1)


def grow_panel(own_block, bit_order, offset, device_index):
    panel = own_block
    for level_bit in bit_order:
        own_bit = bit_at(device_index, offset + level_bit)
        partner = partner_2(panel, "row", offset + level_bit)
        low_part = jnp.where(own_bit == 0, panel, partner)
        high_part = jnp.where(own_bit == 0, partner, panel)
        panel = jnp.stack([low_part, high_part], 0)
    return panel


def turn_panel(panel, layout, device_index, bit_order):
    for level_bit in bit_order:
        axis_at = layout.index(level_bit)
        own_bit = bit_at(device_index, level_bit)
        kept_half = lax.dynamic_index_in_dim(panel, own_bit, axis_at, keepdims=False)
        sent_half = lax.dynamic_index_in_dim(panel, 1 - own_bit, axis_at, keepdims=False)
        partner = partner_2(sent_half, "row", level_bit)
        low_part = jnp.where(own_bit == 0, kept_half, partner)
        high_part = jnp.where(own_bit == 0, partner, kept_half)
        panel = jnp.stack([low_part, high_part], axis_at)
    return panel


def any_grid(head_out, out_grad, proj_weight):
    levels = (lax.axis_size("row").bit_length() - 1) // 2
    device_index = lax.axis_index("row")
    bit_order = list(range(levels))
    layout = bit_order[::-1]
    letters = "pqrsuv"[:levels]
    head_panel = grow_panel(head_out[0], bit_order, 0, device_index)
    weight_panel = grow_panel(proj_weight[0], bit_order, levels, device_index)
    forward = jnp.einsum(
        letters + "ti," + letters + "io->to", head_panel, weight_panel, preferred_element_type=jnp.float32
    )
    turned = turn_panel(weight_panel, layout, device_index, bit_order)
    grad_panel = grow_panel(out_grad[0], bit_order, 0, device_index)
    summed = jnp.einsum(
        letters + "to," + letters + "io->ti", grad_panel, turned, preferred_element_type=jnp.float32
    )
    return forward.astype(jnp.bfloat16)[None], summed.astype(jnp.bfloat16)[None]


def swap(value, axis):
    return lax.ppermute(value, axis, [(0, 1), (1, 0)])


def send(value, pairs):
    return lax.ppermute(value, "a", pairs)


def after(value, *earlier):
    return lax.optimization_barrier((value, *earlier))[0]


def pick(flag, yes, no):
    return jnp.where(flag, yes, no)


def times(left, right):
    return lax.dot_general(left, right, (((1,), (0,)), ((), ())), preferred_element_type=jnp.float32)


def times_rows(left, right):
    return lax.dot_general(left, right, (((1,), (1,)), ((), ())), preferred_element_type=jnp.float32)


def sum_of_products(n_base, numbers, *refs):
    heads, base, pieces, out = refs[:4], refs[4 : 4 + n_base], refs[4 + n_base : -1], refs[-1]
    quarter = pieces[0].shape[0]
    total = None
    for term, piece in enumerate(pieces):
        slot, side = numbers[1 + 2 * term], numbers[2 + 2 * term]
        head = heads[3][...]
        for other in (2, 1, 0):
            head = jnp.where(slot == other, heads[other][...], head)
        head = jnp.where(side == 0, head[:, :quarter], head[:, quarter:])
        product = times(head, piece[...])
        total = product if total is None else total + product
    for term in base:
        total = total + term[...]
    out[...] = total.astype(out.dtype)


def forward_sum(numbers, heads, base, pieces, dtype):
    tokens, width = heads[0].shape
    tile = tokens // 2
    by_rows = pl.BlockSpec((tile, width), lambda i, _: (i, 0))
    spec = pltpu.PrefetchScalarGridSpec(
        num_scalar_prefetch=1,
        grid=(tokens // tile,),
        in_specs=[pl.BlockSpec((tile, width // 2), lambda i, numbers: (i, numbers[0]))] * 4
        + [by_rows] * len(base)
        + [pl.BlockSpec(p.shape, lambda i, _: (0, 0)) for p in pieces],
        out_specs=by_rows,
    )
    return pl.pallas_call(
        functools.partial(sum_of_products, len(base)),
        grid_spec=spec,
        out_shape=jax.ShapeDtypeStruct((tokens, width), dtype),
        compiler_params=pltpu.CompilerParams(
            dimension_semantics=("arbitrary",), vmem_limit_bytes=26 * 1024 * 1024
        ),
        cost_estimate=pl.CostEstimate(flops=1000, bytes_accessed=1000, transcendentals=0),
    )(jnp.stack(numbers).astype(jnp.int32), *heads, *base, *pieces)


INWARD = [(0, 1), (3, 2)]
MIDDLE = [(1, 2), (2, 1)]
OUTWARD = [(1, 0), (2, 3)]
BOTH = INWARD + OUTWARD


def grid_4(head_out, out_grad, proj_weight):
    group = lax.axis_index("g")
    plane = lax.axis_index("a")
    chip = lax.axis_index("b")
    core = lax.axis_index("k")
    heads, grad_0, weight = head_out[0], out_grad[0], proj_weight[0]
    tokens, width = heads.shape
    half, quarter = width // 2, width // 4
    is_mid = (plane == 1) | (plane == 2)
    early = plane // 2 != chip

    def weight_rows(block, of_core, of_group):
        return lax.dynamic_slice_in_dim(block, of_core * half + of_group * quarter, quarter, 0)

    mine_0 = weight_rows(weight, core, group)
    middle_0 = send(mine_0, MIDDLE)
    mine_1 = swap(weight_rows(after(weight, mine_0), 1 - core, group), "k")
    head_y = swap(heads, "b")
    near_1 = send(mine_1, BOTH)
    middle_1 = send(after(mine_1, middle_0), MIDDLE)
    grad_1 = swap(grad_0, "k")
    x_1 = swap(near_1, "g")
    ahead = is_mid & jnp.logical_not(early)
    out_2 = send(pick(ahead, middle_0, after(mine_0, near_1)), BOTH)
    cross_1 = send(after(near_1, middle_1), MIDDLE)
    mid_3 = pick(early, middle_0, after(middle_1, near_1))
    at_2 = pick(ahead, middle_0, out_2)
    out_3 = send(after(mid_3, out_2), OUTWARD)
    x_2 = swap(after(at_2, x_1, grad_1, head_y), "g")
    cross_0 = send(after(out_2, cross_1), MIDDLE)
    late_weight = after(weight, x_1)
    other_0 = weight_rows(late_weight, core, 1 - group)
    other_1 = swap(weight_rows(late_weight, 1 - core, 1 - group), "k")
    mid_4 = pick(early, middle_1, after(cross_1, out_3))
    out_4 = send(mid_4, OUTWARD)
    at_3 = pick(is_mid, mid_3, after(out_3, x_1))
    x_3 = swap(after(at_3, x_2), "g")
    mid_5 = pick(early, cross_1, after(cross_0, out_4))
    out_5 = send(mid_5, OUTWARD)
    at_4 = pick(is_mid, mid_4, after(out_4, x_2))
    x_4 = swap(after(at_4, x_3, other_1), "g")
    out_6 = send(pick(early, cross_0, after(mine_0, out_5)), OUTWARD)
    at_5 = pick(is_mid, mid_5, after(out_5, x_3))
    x_5 = swap(after(at_5, x_4), "g")
    at_6 = pick(is_mid, pick(early, cross_0, out_2), after(out_6, x_4))
    x_6 = swap(after(at_6, x_5), "g")

    def sums(early_pieces, late_pieces):
        slot_0, slot_1 = (pick(early, e, l) for e, l in zip(early_pieces, late_pieces))
        return times_rows(grad_0, slot_0) + times_rows(grad_1, slot_1)

    due = sums((mine_0, mine_1), (at_2, at_3))
    there = swap(after(due, head_y), "b")
    due = sums((other_0, other_1), (x_2, x_3))
    first, due = lax.optimization_barrier((there, due))
    there = swap(due, "b")
    head_1, head_3 = swap(after(heads, x_2), "k"), swap(after(head_y, x_2), "k")
    kept_1 = sums((at_3, at_4), (mine_0, mine_1))
    due = sums((at_2, near_1), (at_5, at_4))
    second, due, kept_1, head_1, head_3 = lax.optimization_barrier((there, due, kept_1, head_1, head_3))
    there = swap(due, "b")

    head_all = [heads, head_1, head_y, head_3]

    def forward(rows, pieces, base=(), dtype=jnp.float32):
        numbers = [core]
        for row in rows:
            slot = 2 * (row // 2 != chip) + ((row & 1) != core)
            numbers += [slot, group, slot, 1 - group]
        return forward_sum(numbers, head_all, list(base), pieces, dtype)

    low = plane < 2
    near, far, far_next = plane ^ 1, pick(low, 2, 1), pick(low, 3, 0)
    rows_1 = [plane, near, pick(early, far, far_next), pick(early, far_next, far)]
    rows_0 = [plane, pick(early, near, far), pick(early, far, far_next), pick(early, far_next, near)]
    pieces_1 = [mine_1, other_1, near_1, x_1, at_4, x_4, pick(early, at_5, at_3), pick(early, x_5, x_3)]
    pieces_0 = [mine_0, other_0, at_2, x_2, pick(early, at_3, at_5), pick(early, x_3, x_5), at_6]
    total_1 = forward(rows_1, pieces_1)
    kept_2 = sums((x_3, x_4), (other_0, other_1))
    due = sums((x_2, x_1), (x_5, x_4))
    third, due, total_1, kept_2, x_6 = lax.optimization_barrier((there, due, total_1, kept_2, x_6))
    there = swap(due, "b")
    projected = forward(rows_0, pieces_0 + [x_6], [swap(total_1, "k")], jnp.bfloat16)

    kept_3 = sums((at_6, at_5), (at_6, near_1))
    kept_4 = sums((x_6, x_5), (x_6, x_1))
    done = [(k + t).astype(jnp.bfloat16) for k, t in ((kept_1, first), (kept_2, second), (kept_3, third))]
    done, kept_4, projected, there = lax.optimization_barrier((done, kept_4, projected, there))
    done.append((kept_4 + there).astype(jnp.bfloat16))
    first_mine = pick(early, plane // 2, plane & 1) == core
    head_grad = jnp.zeros_like(heads)
    for of_group, one, two in ((group, done[0], done[2]), (1 - group, done[1], done[3])):
        here = pick(first_mine, one, two)
        got = swap(pick(first_mine, two, one), "k")
        head_grad = lax.dynamic_update_slice_in_dim(head_grad, here, core * half + of_group * quarter, 1)
        head_grad = lax.dynamic_update_slice_in_dim(head_grad, got, (1 - core) * half + of_group * quarter, 1)
    return projected[None], head_grad[None]


def solution(mesh):
    n_group, n_row = mesh.shape["groups"], mesh.shape["row"]
    if (n_group, n_row) == (2, 16):
        grid = Mesh(mesh.devices.reshape(2, 4, 2, 2), ("g", "a", "b", "k"))
        tokens, whole = P(("a", "b", "k"), "g", None), P(("a", "b", "k"), None, None)
        body = grid_4
    else:
        grid = mesh
        tokens, whole = P("row", "groups", None), P("row", None, None)
        body = any_grid
    return jax.shard_map(
        body, mesh=grid, in_specs=(tokens, tokens, whole), out_specs=(tokens, tokens), check_vma=False
    )
```

time: 176 us -> 158 us (0.90)
  waiting for transfers between devices: 95.6 us -> 66 us
  Pallas kernels: 0 us -> 13.5 us
  starting transfers between devices: 19.9 us -> 32.3 us
  other arithmetic: 15.9 us -> 7.22 us
  local copies, waits for them, and re-layouts: 20.7 us -> 12.6 us
  matrix products: 22.4 us -> 24.5 us
    ppermute x13 -> x19, waiting for transfers between devices: 51.8 us -> 15.8 us  [swap(): return lax.ppermute(value, axis, [(0, 1), (1, 0)])]
    pallas_call x0 -> x2, Pallas kernels: none -> 13.5 us  [forward_sum(): pl.pallas_call(functools.partial(sum_of_products, len(base)), grid_spec=s...]
    ppermute x5 -> x10, starting transfers between devices: 8.59 us -> 17.4 us  [send(): return lax.ppermute(value, 'a', pairs)]
    concatenate x6 -> x0, local copies, waits for them, and re-layouts: 8.36 us -> none  [the longest x4 8.24 us: grid_4(): jnp.concatenate([head_pair, head_far], 0).reshape(4, tokens, 2, quarter)]
    another operation x6 -> x0, other arithmetic: 8.13 us -> none  [the longest x1 2.66 us: grid_4(): head_pair = jnp.stack([head_kept, swap(head_given, 'k')], 0)]
    ppermute x5 -> x10, waiting for transfers between devices: 43.8 us -> 50.2 us  [send(): return lax.ppermute(value, 'a', pairs)]
    ppermute x13 -> x19, starting transfers between devices: 11.3 us -> 14.9 us  [swap(): return lax.ppermute(value, axis, [(0, 1), (1, 0)])]
    squeeze x1 -> x0, local copies, waits for them, and re-layouts: 3.14 us -> none  [grid_4(): given = lax.dynamic_index_in_dim(weight, 1 - core, 0, keepdims=False)]
  transfers between devices with their start and end apart: 18 -> 29, of which waited for: 7 -> 12; matrix products, arithmetic and copies ran while one was open for 27% -> 22% of each run, Pallas kernels for 0% -> 9%
where the time goes in v2:
time: 158 us; the launch traced here: 157 us
  waiting for transfers between devices  66 us (42%)
  starting transfers between devices  32.3 us (20%)
  matrix products  24.5 us (16%)
  Pallas kernels  13.5 us (9%)
  local copies, waits for them, and re-layouts  12.6 us (8%)
  other arithmetic  7.22 us (5%)
    ppermute x10, waiting for transfers between devices, send(): return lax.ppermute(value, 'a', pairs)  50.2 us
    dot_general x16, matrix products, times_rows(): lax.dot_general(left, right, (((1,), (1,)), ((), ())), preferred_element_...  24.5 us
    ppermute x10, starting transfers between devices, send(): return lax.ppermute(value, 'a', pairs)  17.4 us
    ppermute x19, waiting for transfers between devices, swap(): return lax.ppermute(value, axis, [(0, 1), (1, 0)])  15.8 us
    ppermute x19, starting transfers between devices, swap(): return lax.ppermute(value, axis, [(0, 1), (1, 0)])  14.9 us
    pallas_call x2, Pallas kernels, forward_sum(): pl.pallas_call(functools.partial(sum_of_products, len(base)), grid_spec=s...  13.5 us
    select_n x13, other arithmetic, pick(): return jnp.where(flag, yes, no)  7 us
    unnamed x68, local copies, waits for them, and re-layouts  5.81 us
  transfers between devices with their start and end apart: 29, of which 12 were waited for; matrix products, arithmetic and copies ran while one was open for 22% of the time, Pallas kernels for 9%

profile of v2, /device:TPU:0, one launch (start us, length us, event | category | flops | bytes accessed | tf_op | source)
XLA Modules:
  0.0 157.4 jit_solution(14850134814544281383)
XLA Ops:
  0.7 1.2 dynamic-slice_bitcast_fusion.refs_5_
  1.9 1.1 constant_dynamic-slice_fusion.2
  5.0 4.6 %collective-permute-start.2 = (bf16[256,1024]{1,0:T(8,128)(2,1)S(1)}, bf16[256,1024]{1,0:T(8,128)(2,1)}, u32[]{:S(2)}, u32[]{:S(2)}) collective-permute-start(bf16[256,1024]{1,0:T(8,128)(2,1)S(1)} %collective-permute-done.1.refs_4_), channel_id=1, source_target_pairs={{0,4},{12,8},{4,0},{8,12},{1,5},{13,9},{5,1},{9,13},{2,6},{14,10},... | collective-permute-start | bytes 1572872 | tf_op jit(solution)/shard_map/ppermute | solution.py:68
  9.6 1.5 collective-permute-start.8
  11.8 10.2 %collective-permute-done.2.refs_6_ = bf16[256,1024]{1,0:T(8,128)(2,1)} collective-permute-done((bf16[256,1024]{1,0:T(8,128)(2,1)S(1)}, bf16[256,1024]{1,0:T(8,128)(2,1)}, u32[]{:S(2)}, u32[]{:S(2)}) %collective-permute-start.2) | collective-permute-done | bytes 524320 | tf_op jit(solution)/shard_map/ppermute | solution.py:68
  22.1 3.8 %collective-permute-start.3 = (bf16[256,1024]{1,0:T(8,128)(2,1)S(1)}, bf16[256,1024]{1,0:T(8,128)(2,1)S(1)}, u32[]{:S(2)}, u32[]{:S(2)}) collective-permute-start(bf16[256,1024]{1,0:T(8,128)(2,1)S(1)} %broadcast_select_fusion.4), channel_id=1, source_target_pairs={{0,4},{12,8},{4,0},{8,12},{1,5},{13,9},{5,1},{9,13},{2,6},{14,10},... | collective-permute-start | bytes 1572872 | tf_op jit(solution)/shard_map/ppermute | solution.py:68
  25.9 1.5 collective-permute-start.14
  27.3 1.5 collective-permute-start.6
  28.8 8.7 %collective-permute-done.3 = bf16[256,1024]{1,0:T(8,128)(2,1)S(1)} collective-permute-done((bf16[256,1024]{1,0:T(8,128)(2,1)S(1)}, bf16[256,1024]{1,0:T(8,128)(2,1)S(1)}, u32[]{:S(2)}, u32[]{:S(2)}) %collective-permute-start.3) | collective-permute-done | bytes 524320 | tf_op jit(solution)/shard_map/ppermute | solution.py:68
  37.5 1.0 broadcast_select_fusion.3
  38.5 1.3 collective-permute-start.5
  40.7 1.3 constant_dynamic-slice_fusion.1
  42.8 3.7 %collective-permute-done.8.refs_2_ = bf16[768,1024]{1,0:T(8,128)(2,1)} collective-permute-done((bf16[768,1024]{1,0:T(8,128)(2,1)S(1)}, bf16[768,1024]{1,0:T(8,128)(2,1)}, u32[]{:S(2)}, u32[]{:S(2)}) %collective-permute-start.8) | collective-permute-done | bytes 1572896 | tf_op jit(solution)/shard_map/ppermute | solution.py:64
  46.5 1.5 collective-permute-start.10
  48.0 7.9 %collective-permute-done.5 = bf16[256,1024]{1,0:T(8,128)(2,1)} collective-permute-done((bf16[256,1024]{1,0:T(8,128)(2,1)}, bf16[256,1024]{1,0:T(8,128)(2,1)}, u32[]{:S(2)}, u32[]{:S(2)}) %collective-permute-start.5) | collective-permute-done | bytes 524320 | tf_op jit(solution)/shard_map/ppermute | solution.py:68
  55.9 1.1 broadcast_select_fusion.2
  57.0 1.1 broadcast_select_fusion.11
  58.2 1.4 collective-permute-start.16
  59.6 2.0 %fusion.29 = f32[256,768]{1,0:T(8,128)S(1)} fusion(bf16[768,1024]{1,0:T(8,128)(2,1)} %collective-permute-done.7, bf16[256,1024]{1,0:T(8,128)(2,1)S(1)} %copy-done.10, bf16[256,1024]{1,0:T(8,128)(2,1)S(1)} %broadcast_select_fusion.2, pred[]{:T(512)S(6)} %ne.91), kind=kOutput, calls=%fused_computation.41 | convolution fusion | flops 402915328 | bytes 3407873 | tf_op jit(solution)/shard_map/dot_general | solution.py:84
  63.4 11.8 %collective-permute-done.16 = bf16[256,1024]{1,0:T(8,128)(2,1)S(1)} collective-permute-done((bf16[256,1024]{1,0:T(8,128)(2,1)S(1)}, bf16[256,1024]{1,0:T(8,128)(2,1)S(1)}, u32[]{:S(2)}, u32[]{:S(2)}) %collective-permute-start.16) | collective-permute-done | bytes 524320 | tf_op jit(solution)/shard_map/ppermute | solution.py:68
  75.9 2.0 %fusion.20 = f32[256,768]{1,0:T(8,128)S(1)} fusion(bf16[768,1024]{1,0:T(8,128)(2,1)} %collective-permute-done.7, bf16[256,1024]{1,0:T(8,128)(2,1)S(1)} %broadcast_select_fusion.refs_8_, bf16[256,1024]{1,0:T(8,128)(2,1)S(1)} %copy-done.10, pred[]{:T(512)S(6)} %ne.91), kind=kOutput, calls=%fused_computation.32 | convolution fusion | flops 402915328 | bytes 3407873 | tf_op jit(solution)/shard_map/dot_general | solution.py:84
  77.9 1.5 fusion.5
  79.5 1.3 collective-permute-start.17
  81.4 2.0 %fusion.26 = f32[256,768]{1,0:T(8,128)S(1)} fusion(bf16[768,1024]{1,0:T(8,128)(2,1)} %collective-permute-done.7, bf16[256,1024]{1,0:T(8,128)(2,1)S(1)} %collective-permute-done.11.refs_5_, bf16[256,1024]{1,0:T(8,128)(2,1)S(1)} %collective-permute-done.12, pred[]{:T(512)S(6)} %ne.91), kind=kOutput, calls=%fused_computation.38 | convolution fusion | flops 402915328 | bytes 3407873 | tf_op jit(solution)/shard_map/dot_general | solution.py:84
  84.0 2.0 %fusion.23 = f32[256,768]{1,0:T(8,128)S(1)} fusion(bf16[768,1024]{1,0:T(8,128)(2,1)} %collective-permute-done.7, bf16[256,1024]{1,0:T(8,128)(2,1)} %collective-permute-done.2.refs_6_, bf16[256,1024]{1,0:T(8,128)(2,1)S(1)} %broadcast_select_fusion.refs_8_, pred[]{:T(512)S(6)} %ne.91), kind=kOutput, calls=%fused_computation.35 | convolution fusion | flops 402915328 | bytes 3407873 | tf_op jit(solution)/shard_map/dot_general | solution.py:84
  86.1 1.8 %collective-permute-start.13 = (f32[768,256]{0,1:T(8,128)S(1)}, f32[768,256]{0,1:T(8,128)S(1)}, u32[]{:S(2)}, u32[]{:S(2)}) collective-permute-start(f32[768,256]{0,1:T(8,128)S(1)} %fusion.7), channel_id=1, source_target_pairs={{0,2},{2,0},{1,3},{3,1},{4,6},{6,4},{5,7},{7,5},{8,10},{10,8},{9,1... | collective-permute-start | bytes 2359304 | tf_op jit(solution)/shard_map/ppermute | solution.py:64
  87.8 7.4 %collective-permute-done.17 = bf16[256,1024]{1,0:T(8,128)(2,1)S(1)} collective-permute-done((bf16[256,1024]{1,0:T(8,128)(2,1)S(1)}, bf16[256,1024]{1,0:T(8,128)(2,1)S(1)}, u32[]{:S(2)}, u32[]{:S(2)}) %collective-permute-start.17) | collective-permute-done | bytes 524320 | tf_op jit(solution)/shard_map/ppermute | solution.py:68
  95.2 0.9 broadcast_select_fusion.6
  96.7 1.5 collective-permute-start.23
  98.2 2.0 %fusion.14 = f32[256,768]{1,0:T(8,128)S(1)} fusion(bf16[768,1024]{1,0:T(8,128)(2,1)} %collective-permute-done.7, bf16[256,1024]{1,0:T(8,128)(2,1)S(1)} %collective-permute-done.21.refs_9_, bf16[256,1024]{1,0:T(8,128)(2,1)S(1)} %collective-permute-done.11.refs_5_, pred[]{:T(512)S(6)} %ne.91), kind=kOutput, calls=%fused_computation.26 | convolution fusion | flops 402915328 | bytes 3407873 | tf_op jit(solution)/shard_map/dot_general | solution.py:84
  100.9 1.5 fusion.3
  102.4 2.0 %fusion.17 = f32[256,768]{1,0:T(8,128)S(1)} fusion(bf16[768,1024]{1,0:T(8,128)(2,1)} %collective-permute-done.7, bf16[256,1024]{1,0:T(8,128)(2,1)} %collective-permute-done.6.refs_7_, bf16[256,1024]{1,0:T(8,128)(2,1)S(1)} %collective-permute-done.21.refs_9_, pred[]{:T(512)S(6)} %ne.91), kind=kOutput, calls=%fused_computation.29 | convolution fusion | flops 402915328 | bytes 3407873 | tf_op jit(solution)/shard_map/dot_general | solution.py:84
  105.4 1.7 %collective-permute-start.20 = (f32[768,256]{0,1:T(8,128)S(1)}, f32[768,256]{0,1:T(8,128)S(1)}, u32[]{:S(2)}, u32[]{:S(2)}) collective-permute-start(f32[768,256]{0,1:T(8,128)S(1)} %fusion.6), channel_id=1, source_target_pairs={{0,2},{2,0},{1,3},{3,1},{4,6},{6,4},{5,7},{7,5},{8,10},{10,8},{9,1... | collective-permute-start | bytes 2359304 | tf_op jit(solution)/shard_map/ppermute | solution.py:64
  107.1 4.2 %collective-permute-done.23 = bf16[256,1024]{1,0:T(8,128)(2,1)S(1)} collective-permute-done((bf16[256,1024]{1,0:T(8,128)(2,1)S(1)}, bf16[256,1024]{1,0:T(8,128)(2,1)S(1)}, u32[]{:S(2)}, u32[]{:S(2)}) %collective-permute-start.23) | collective-permute-done | bytes 524320 | tf_op jit(solution)/shard_map/ppermute | solution.py:68
  111.4 1.6 collective-permute-start.24
  113.9 6.8 %shard_map.50 = f32[768,1024]{1,0:T(8,128)} custom-call(s32[17]{0:T(128)S(1)} %stack.29.numbers, bf16[768,1024]{1,0:T(8,128)(2,1)S(1)} %bitcast.69, bf16[768,1024]{1,0:T(8,128)(2,1)S(1)} %collective-permute-done.18.refs_1_, bf16[768,1024]{1,0:T(8,128)(2,1)} %collective-permute-done.8.refs_2_, bf16[768,1024]{1,0:T(8,128)(2,1)S(1)} %collective-permute-done.19.refs_3_, ...), custom_call_target="tpu_custom_call" | custom-call | flops 1000 | bytes 1000 | tf_op jit(solution)/shard_map/pallas_call | solution.py:116
  120.7 1.5 fusion.4
  122.2 1.1 collective-permute-done.24.refs_12_
  124.1 0.9 copy-done.32
  125.1 2.3 %fusion.12 = f32[256,768]{1,0:T(8,128)S(1)} fusion(bf16[768,1024]{1,0:T(8,128)(2,1)} %collective-permute-done.7, bf16[256,1024]{1,0:T(8,128)(2,1)} %copy-done.17, bf16[256,1024]{1,0:T(8,128)(2,1)} %collective-permute-done.2.refs_6_, pred[]{:T(512)S(6)} %ne.91), kind=kOutput, calls=%fused_computation.23 | convolution fusion | flops 402915328 | bytes 3407873 | tf_op jit(solution)/shard_map/dot_general | solution.py:84
  127.5 0.9 copy-done.19
  128.5 2.3 %fusion.10 = f32[256,768]{1,0:T(8,128)S(1)} fusion(bf16[768,1024]{1,0:T(8,128)(2,1)} %collective-permute-done.7, bf16[256,1024]{1,0:T(8,128)(2,1)S(1)} %copy-done.19, bf16[256,1024]{1,0:T(8,128)(2,1)} %collective-permute-done.6.refs_7_, pred[]{:T(512)S(6)} %ne.91), kind=kOutput, calls=%fused_computation.21 | convolution fusion | flops 402915328 | bytes 3407873 | tf_op jit(solution)/shard_map/dot_general | solution.py:84
  130.8 1.4 collective-permute-start.26
  135.7 6.7 %shard_map.51 = bf16[768,1024]{1,0:T(8,128)(2,1)} custom-call(s32[17]{0:T(128)S(1)} %stack.32.numbers, bf16[768,1024]{1,0:T(8,128)(2,1)S(1)} %bitcast.70, bf16[768,1024]{1,0:T(8,128)(2,1)S(1)} %copy-done.2, bf16[768,1024]{1,0:T(8,128)(2,1)} %collective-permute-done.8.refs_2_, bf16[768,1024]{1,0:T(8,128)(2,1)S(1)} %copy-done.4, ...), custom_call_target="tpu_custom_call" | custom-call | flops 1000 | bytes 1000 | tf_op jit(solution)/shard_map/pallas_call | solution.py:116
  142.4 8.5 %collective-permute-done.26 = f32[768,256]{0,1:T(8,128)S(1)} collective-permute-done((f32[768,256]{0,1:T(8,128)S(1)}, f32[768,256]{0,1:T(8,128)S(1)}, u32[]{:S(2)}, u32[]{:S(2)}) %collective-permute-start.26) | collective-permute-done | bytes 786464 | tf_op jit(solution)/shard_map/ppermute | solution.py:64
  153.7 1.2 copy.6
  154.9 1.2 copy.8
  156.3 1.1 copy-done.26
  (126 shorter events, 18.6 us)
Async XLA Ops:
  0.6 9.0 %copy-start = (bf16[1,768,1024]{2,1,0:T(8,128)(2,1)S(1)}, bf16[1,768,1024]{2,1,0:T(8,128)(2,1)}, u32[]{:S(2)}) copy-start(bf16[1,768,1024]{2,1,0:T(8,128)(2,1)} %param.3) | copy-start | bytes 4718596
  2.9 2.1 %collective-permute-start.1 = (bf16[256,1024]{1,0:T(8,128)(2,1)S(1)}, bf16[256,1024]{1,0:T(8,128)(2,1)S(1)}, u32[]{:S(2)}, u32[]{:S(2)}) collective-permute-start(bf16[256,1024]{1,0:T(8,128)(2,1)S(1)} %constant_dynamic-slice_fusion.2), channel_id=1, source_target_pairs={{0,1},{1,0},{2,3},{3,2},{4,5},{5,4},{6,7},{7,6},{8,9},{9,8},{10,11... | collective-permute-start | bytes 1572872 | tf_op jit(solution)/shard_map/ppermute | solution.py:64
  3.5 7.7 %collective-permute-start = (bf16[256,1024]{1,0:T(8,128)(2,1)S(1)}, bf16[256,1024]{1,0:T(8,128)(2,1)S(1)}, u32[]{:S(2)}, u32[]{:S(2)}) collective-permute-start(bf16[256,1024]{1,0:T(8,128)(2,1)S(1)} %dynamic-slice_bitcast_fusion.refs_5_), channel_id=1, source_target_pairs={{4,8},{8,4},{5,9},{9,5},{6,10},{10,6},{7,11},{11,7},{20,24},{24,20... | collective-permute-start | bytes 1572872 | tf_op jit(solution)/shard_map/ppermute | solution.py:68
  5.0 23.8 %copy-start.9 = (bf16[256,1024]{1,0:T(8,128)(2,1)}, bf16[256,1024]{1,0:T(8,128)(2,1)S(1)}, u32[]{:S(2)}) copy-start(bf16[256,1024]{1,0:T(8,128)(2,1)S(1)} %collective-permute-done.1.refs_4_) | copy-start | bytes 1572868
  5.0 17.0 %collective-permute-start.2 = (bf16[256,1024]{1,0:T(8,128)(2,1)S(1)}, bf16[256,1024]{1,0:T(8,128)(2,1)}, u32[]{:S(2)}, u32[]{:S(2)}) collective-permute-start(bf16[256,1024]{1,0:T(8,128)(2,1)S(1)} %collective-permute-done.1.refs_4_), channel_id=1, source_target_pairs={{0,4},{12,8},{4,0},{8,12},{1,5},{13,9},{5,1},{9,13},{2,6},{14,10},... | collective-permute-start | bytes 1572872 | tf_op jit(solution)/shard_map/ppermute | solution.py:68
  9.6 33.2 %collective-permute-start.7 = (bf16[768,1024]{1,0:T(8,128)(2,1)}, bf16[768,1024]{1,0:T(8,128)(2,1)}, u32[]{:S(2)}, u32[]{:S(2)}) collective-permute-start(bf16[768,1024]{1,0:T(8,128)(2,1)} %bitcast.71), channel_id=1, source_target_pairs={{0,1},{1,0},{2,3},{3,2},{4,5},{5,4},{6,7},{7,6},{8,9},{9,8},{10,11... | collective-permute-start | bytes 4718600 | tf_op jit(solution)/shard_map/ppermute | solution.py:64
  9.6 36.9 %collective-permute-start.8 = (bf16[768,1024]{1,0:T(8,128)(2,1)S(1)}, bf16[768,1024]{1,0:T(8,128)(2,1)}, u32[]{:S(2)}, u32[]{:S(2)}) collective-permute-start(bf16[768,1024]{1,0:T(8,128)(2,1)S(1)} %bitcast.67), channel_id=1, source_target_pairs={{0,2},{2,0},{1,3},{3,1},{4,6},{6,4},{5,7},{7,5},{8,10},{10,8},{9,1... | collective-permute-start | bytes 4718600 | tf_op jit(solution)/shard_map/ppermute | solution.py:64
  11.2 14.7 %collective-permute-start.4 = (bf16[256,1024]{1,0:T(8,128)(2,1)S(1)}, bf16[256,1024]{1,0:T(8,128)(2,1)S(1)}, u32[]{:S(2)}, u32[]{:S(2)}) collective-permute-start(bf16[256,1024]{1,0:T(8,128)(2,1)S(1)} %collective-permute-done.1.refs_4_), channel_id=1, source_target_pairs={{4,8},{8,4},{5,9},{9,5},{6,10},{10,6},{7,11},{11,7},{20,24},{24,20... | collective-permute-start | bytes 1572872 | tf_op jit(solution)/shard_map/ppermute | solution.py:68
  22.1 15.4 %collective-permute-start.3 = (bf16[256,1024]{1,0:T(8,128)(2,1)S(1)}, bf16[256,1024]{1,0:T(8,128)(2,1)S(1)}, u32[]{:S(2)}, u32[]{:S(2)}) collective-permute-start(bf16[256,1024]{1,0:T(8,128)(2,1)S(1)} %broadcast_select_fusion.4), channel_id=1, source_target_pairs={{0,4},{12,8},{4,0},{8,12},{1,5},{13,9},{5,1},{9,13},{2,6},{14,10},... | collective-permute-start | bytes 1572872 | tf_op jit(solution)/shard_map/ppermute | solution.py:68
  25.9 11.6 %copy-start.22 = (bf16[256,1024]{1,0:T(8,128)(2,1)}, bf16[256,1024]{1,0:T(8,128)(2,1)S(1)}, u32[]{:S(2)}) copy-start(bf16[256,1024]{1,0:T(8,128)(2,1)S(1)} %collective-permute-done.4) | copy-start | bytes 1572868
  25.9 16.2 %collective-permute-start.14 = (bf16[256,1024]{1,0:T(8,128)(2,1)}, bf16[256,1024]{1,0:T(8,128)(2,1)}, u32[]{:S(2)}, u32[]{:S(2)}) collective-permute-start(bf16[256,1024]{1,0:T(8,128)(2,1)} %collective-permute-done.2.refs_6_), channel_id=1, source_target_pairs={{4,8},{8,4},{5,9},{9,5},{6,10},{10,6},{7,11},{11,7},{20,24},{24,20... | collective-permute-start | bytes 1572872 | tf_op jit(solution)/shard_map/ppermute | solution.py:68
  27.3 13.4 %collective-permute-start.6 = (bf16[256,1024]{1,0:T(8,128)(2,1)}, bf16[256,1024]{1,0:T(8,128)(2,1)}, u32[]{:S(2)}, u32[]{:S(2)}) collective-permute-start(bf16[256,1024]{1,0:T(8,128)(2,1)} %collective-permute-done.2.refs_6_), channel_id=1, source_target_pairs={{0,16},{16,0},{1,17},{17,1},{2,18},{18,2},{3,19},{19,3},{4,20},{20... | collective-permute-start | bytes 1572872 | tf_op jit(solution)/shard_map/ppermute | solution.py:64
  38.5 17.5 %collective-permute-start.5 = (bf16[256,1024]{1,0:T(8,128)(2,1)}, bf16[256,1024]{1,0:T(8,128)(2,1)}, u32[]{:S(2)}, u32[]{:S(2)}) collective-permute-start(bf16[256,1024]{1,0:T(8,128)(2,1)} %get-tuple-element.47), channel_id=1, source_target_pairs={{4,0},{8,12},{5,1},{9,13},{6,2},{10,14},{7,3},{11,15},{20,16},{24,... | collective-permute-start | bytes 1572872 | tf_op jit(solution)/shard_map/ppermute | solution.py:68
  40.0 17.1 %copy-start.23 = (bf16[256,1024]{1,0:T(8,128)(2,1)S(1)}, bf16[256,1024]{1,0:T(8,128)(2,1)}, u32[]{:S(2)}) copy-start(bf16[256,1024]{1,0:T(8,128)(2,1)} %copy-done.22) | copy-start | bytes 1572868
  42.0 37.5 %collective-permute-start.11 = (bf16[256,1024]{1,0:T(8,128)(2,1)S(1)}, bf16[256,1024]{1,0:T(8,128)(2,1)S(1)}, u32[]{:S(2)}, u32[]{:S(2)}) collective-permute-start(bf16[256,1024]{1,0:T(8,128)(2,1)S(1)} %get-tuple-element.89), channel_id=1, source_target_pairs={{0,1},{1,0},{2,3},{3,2},{4,5},{5,4},{6,7},{7,6},{8,9},{9,8},{10,11... | collective-permute-start | bytes 1572872 | tf_op jit(solution)/shard_map/ppermute | solution.py:64
  42.1 33.2 %collective-permute-start.15 = (bf16[256,1024]{1,0:T(8,128)(2,1)S(1)}, bf16[256,1024]{1,0:T(8,128)(2,1)S(1)}, u32[]{:S(2)}, u32[]{:S(2)}) collective-permute-start(bf16[256,1024]{1,0:T(8,128)(2,1)S(1)} %copy-done.25), channel_id=1, source_target_pairs={{4,8},{8,4},{5,9},{9,5},{6,10},{10,6},{7,11},{11,7},{20,24},{24,20... | collective-permute-start | bytes 1572872 | tf_op jit(solution)/shard_map/ppermute | solution.py:68
  46.5 13.1 %copy-start.10 = (bf16[256,1024]{1,0:T(8,128)(2,1)S(1)}, bf16[256,1024]{1,0:T(8,128)(2,1)}, u32[]{:S(2)}) copy-start(bf16[256,1024]{1,0:T(8,128)(2,1)} %copy-done.9) | copy-start | bytes 1572868
  46.5 16.3 %collective-permute-start.10 = (bf16[256,1024]{1,0:T(8,128)(2,1)S(1)}, bf16[256,1024]{1,0:T(8,128)(2,1)S(1)}, u32[]{:S(2)}, u32[]{:S(2)}) collective-permute-start(bf16[256,1024]{1,0:T(8,128)(2,1)S(1)} %get-tuple-element.51.refs_7_), channel_id=1, source_target_pairs={{0,16},{16,0},{1,17},{17,1},{2,18},{18,2},{3,19},{19,3},{4,20},{20... | collective-permute-start | bytes 1572872 | tf_op jit(solution)/shard_map/ppermute | solution.py:64
  58.2 3.5 %copy-start.15 = (bf16[1,768,1024]{2,1,0:T(8,128)(2,1)S(1)}, bf16[1,768,1024]{2,1,0:T(8,128)(2,1)}, u32[]{:S(2)}) copy-start(bf16[1,768,1024]{2,1,0:T(8,128)(2,1)} %param.4) | copy-start | bytes 4718596
  58.2 17.0 %collective-permute-start.16 = (bf16[256,1024]{1,0:T(8,128)(2,1)S(1)}, bf16[256,1024]{1,0:T(8,128)(2,1)S(1)}, u32[]{:S(2)}, u32[]{:S(2)}) collective-permute-start(bf16[256,1024]{1,0:T(8,128)(2,1)S(1)} %broadcast_select_fusion.11), channel_id=1, source_target_pairs={{4,0},{8,12},{5,1},{9,13},{6,2},{10,14},{7,3},{11,15},{20,16},{24,... | collective-permute-start | bytes 1572872 | tf_op jit(solution)/shard_map/ppermute | solution.py:68
  62.3 23.8 %collective-permute-start.9 = (f32[768,256]{0,1:T(8,128)S(1)}, f32[768,256]{0,1:T(8,128)S(1)}, u32[]{:S(2)}, u32[]{:S(2)}) collective-permute-start(f32[768,256]{0,1:T(8,128)S(1)} %fusion.8), channel_id=1, source_target_pairs={{0,2},{2,0},{1,3},{3,1},{4,6},{6,4},{5,7},{7,5},{8,10},{10,8},{9,1... | collective-permute-start | bytes 2359304 | tf_op jit(solution)/shard_map/ppermute | solution.py:64
  62.9 57.8 %copy-start.5 = (bf16[256,1024]{1,0:T(8,128)(2,1)}, bf16[256,1024]{1,0:T(8,128)(2,1)S(1)}, u32[]{:S(2)}) copy-start(bf16[256,1024]{1,0:T(8,128)(2,1)S(1)} %collective-permute-done.10.refs_8_) | copy-start | bytes 1572868
  62.9 17.9 %collective-permute-start.12 = (bf16[256,1024]{1,0:T(8,128)(2,1)S(1)}, bf16[256,1024]{1,0:T(8,128)(2,1)S(1)}, u32[]{:S(2)}, u32[]{:S(2)}) collective-permute-start(bf16[256,1024]{1,0:T(8,128)(2,1)S(1)} %broadcast_select_fusion.2), channel_id=1, source_target_pairs={{0,16},{16,0},{1,17},{17,1},{2,18},{18,2},{3,19},{19,3},{4,20},{20... | collective-permute-start | bytes 1572872 | tf_op jit(solution)/shard_map/ppermute | solution.py:64
  75.2 30.1 %collective-permute-start.18 = (bf16[768,1024]{1,0:T(8,128)(2,1)S(1)}, bf16[768,1024]{1,0:T(8,128)(2,1)S(1)}, u32[]{:S(2)}, u32[]{:S(2)}) collective-permute-start(bf16[768,1024]{1,0:T(8,128)(2,1)S(1)} %bitcast.68), channel_id=1, source_target_pairs={{0,1},{1,0},{2,3},{3,2},{4,5},{5,4},{6,7},{7,6},{8,9},{9,8},{10,11... | collective-permute-start | bytes 4718600 | tf_op jit(solution)/shard_map/ppermute | solution.py:64
  75.3 30.1 %collective-permute-start.19 = (bf16[768,1024]{1,0:T(8,128)(2,1)}, bf16[768,1024]{1,0:T(8,128)(2,1)S(1)}, u32[]{:S(2)}, u32[]{:S(2)}) collective-permute-start(bf16[768,1024]{1,0:T(8,128)(2,1)} %collective-permute-done.8.refs_2_), channel_id=1, source_target_pairs={{0,1},{1,0},{2,3},{3,2},{4,5},{5,4},{6,7},{7,6},{8,9},{9,8},{10,11... | collective-permute-start | bytes 4718600 | tf_op jit(solution)/shard_map/ppermute | solution.py:64
  79.5 15.7 %collective-permute-start.17 = (bf16[256,1024]{1,0:T(8,128)(2,1)S(1)}, bf16[256,1024]{1,0:T(8,128)(2,1)S(1)}, u32[]{:S(2)}, u32[]{:S(2)}) collective-permute-start(bf16[256,1024]{1,0:T(8,128)(2,1)S(1)} %broadcast_select_fusion.10), channel_id=1, source_target_pairs={{4,0},{8,12},{5,1},{9,13},{6,2},{10,14},{7,3},{11,15},{20,16},{24,... | collective-permute-start | bytes 1572872 | tf_op jit(solution)/shard_map/ppermute | solution.py:68
  80.8 15.3 %collective-permute-start.21 = (bf16[256,1024]{1,0:T(8,128)(2,1)S(1)}, bf16[256,1024]{1,0:T(8,128)(2,1)S(1)}, u32[]{:S(2)}, u32[]{:S(2)}) collective-permute-start(bf16[256,1024]{1,0:T(8,128)(2,1)S(1)} %broadcast_select_fusion.refs_8_), channel_id=1, source_target_pairs={{0,16},{16,0},{1,17},{17,1},{2,18},{18,2},{3,19},{19,3},{4,20},{20... | collective-permute-start | bytes 1572872 | tf_op jit(solution)/shard_map/ppermute | solution.py:64
  86.1 10.6 %copy-start.28 = (f32[768,256]{0,1:T(8,128)}, f32[768,256]{0,1:T(8,128)S(1)}, u32[]{:S(2)}) copy-start(f32[768,256]{0,1:T(8,128)S(1)} %collective-permute-done.9) | copy-start | bytes 2359300
  86.1 19.3 %collective-permute-start.13 = (f32[768,256]{0,1:T(8,128)S(1)}, f32[768,256]{0,1:T(8,128)S(1)}, u32[]{:S(2)}, u32[]{:S(2)}) collective-permute-start(f32[768,256]{0,1:T(8,128)S(1)} %fusion.7), channel_id=1, source_target_pairs={{0,2},{2,0},{1,3},{3,1},{4,6},{6,4},{5,7},{7,5},{8,10},{10,8},{9,1... | collective-permute-start | bytes 2359304 | tf_op jit(solution)/shard_map/ppermute | solution.py:64
  96.1 8.3 %copy-start.17 = (bf16[256,1024]{1,0:T(8,128)(2,1)}, bf16[256,1024]{1,0:T(8,128)(2,1)S(1)}, u32[]{:S(2)}) copy-start(bf16[256,1024]{1,0:T(8,128)(2,1)S(1)} %get-tuple-element.66) | copy-start | bytes 1572868
  96.1 15.3 %collective-permute-start.22 = (bf16[256,1024]{1,0:T(8,128)(2,1)S(1)}, bf16[256,1024]{1,0:T(8,128)(2,1)S(1)}, u32[]{:S(2)}, u32[]{:S(2)}) collective-permute-start(bf16[256,1024]{1,0:T(8,128)(2,1)S(1)} %get-tuple-element.66), channel_id=1, source_target_pairs={{0,16},{16,0},{1,17},{17,1},{2,18},{18,2},{3,19},{19,3},{4,20},{20... | collective-permute-start | bytes 1572872 | tf_op jit(solution)/shard_map/ppermute | solution.py:64
  96.7 14.6 %collective-permute-start.23 = (bf16[256,1024]{1,0:T(8,128)(2,1)S(1)}, bf16[256,1024]{1,0:T(8,128)(2,1)S(1)}, u32[]{:S(2)}, u32[]{:S(2)}) collective-permute-start(bf16[256,1024]{1,0:T(8,128)(2,1)S(1)} %broadcast_select_fusion.7), channel_id=1, source_target_pairs={{4,0},{8,12},{5,1},{9,13},{6,2},{10,14},{7,3},{11,15},{20,16},{24,... | collective-permute-start | bytes 1572872 | tf_op jit(solution)/shard_map/ppermute | solution.py:68
  105.3 8.5 %copy-start.30 = (f32[768,256]{0,1:T(8,128)}, f32[768,256]{0,1:T(8,128)S(1)}, u32[]{:S(2)}) copy-start(f32[768,256]{0,1:T(8,128)S(1)} %collective-permute-done.13) | copy-start | bytes 2359300
  105.3 8.5 %copy-start.1 = (bf16[768,1024]{1,0:T(8,128)(2,1)}, bf16[768,1024]{1,0:T(8,128)(2,1)S(1)}, u32[]{:S(2)}) copy-start(bf16[768,1024]{1,0:T(8,128)(2,1)S(1)} %collective-permute-done.18.refs_1_) | copy-start | bytes 4718596
  105.4 8.5 %copy-start.3 = (bf16[768,1024]{1,0:T(8,128)(2,1)}, bf16[768,1024]{1,0:T(8,128)(2,1)S(1)}, u32[]{:S(2)}) copy-start(bf16[768,1024]{1,0:T(8,128)(2,1)S(1)} %collective-permute-done.19.refs_3_) | copy-start | bytes 4718596
  105.4 18.7 %collective-permute-start.20 = (f32[768,256]{0,1:T(8,128)S(1)}, f32[768,256]{0,1:T(8,128)S(1)}, u32[]{:S(2)}, u32[]{:S(2)}) collective-permute-start(f32[768,256]{0,1:T(8,128)S(1)} %fusion.6), channel_id=1, source_target_pairs={{0,2},{2,0},{1,3},{3,1},{4,6},{6,4},{5,7},{7,5},{8,10},{10,8},{9,1... | collective-permute-start | bytes 2359304 | tf_op jit(solution)/shard_map/ppermute | solution.py:64
  111.4 9.3 %copy-start.7 = (bf16[256,1024]{1,0:T(8,128)(2,1)}, bf16[256,1024]{1,0:T(8,128)(2,1)S(1)}, u32[]{:S(2)}) copy-start(bf16[256,1024]{1,0:T(8,128)(2,1)S(1)} %select_select_fusion.refs_11_) | copy-start | bytes 1572868
  111.4 9.3 %copy-start.18 = (bf16[256,1024]{1,0:T(8,128)(2,1)}, bf16[256,1024]{1,0:T(8,128)(2,1)S(1)}, u32[]{:S(2)}) copy-start(bf16[256,1024]{1,0:T(8,128)(2,1)S(1)} %collective-permute-done.22) | copy-start | bytes 1572868
  111.4 11.9 %collective-permute-start.24 = (bf16[256,1024]{1,0:T(8,128)(2,1)S(1)}, bf16[256,1024]{1,0:T(8,128)(2,1)S(1)}, u32[]{:S(2)}, u32[]{:S(2)}) collective-permute-start(bf16[256,1024]{1,0:T(8,128)(2,1)S(1)} %select_select_fusion.refs_11_), channel_id=1, source_target_pairs={{0,16},{16,0},{1,17},{17,1},{2,18},{18,2},{3,19},{19,3},{4,20},{20... | collective-permute-start | bytes 1572872 | tf_op jit(solution)/shard_map/ppermute | solution.py:64
  125.0 9.4 %collective-permute-start.25 = (f32[768,1024]{1,0:T(8,128)}, f32[768,1024]{1,0:T(8,128)}, u32[]{:S(2)}, u32[]{:S(2)}) collective-permute-start(f32[768,1024]{1,0:T(8,128)} %shard_map.50), channel_id=1, source_target_pairs={{0,1},{1,0},{2,3},{3,2},{4,5},{5,4},{6,7},{7,6},{8,9},{9,8},{10,11... | collective-permute-start | bytes 9437192 | tf_op jit(solution)/shard_map/ppermute | solution.py:64
  125.1 2.3 %copy-start.20 = (f32[768,256]{0,1:T(8,128)S(1)}, f32[768,256]{0,1:T(8,128)}, u32[]{:S(2)}) copy-start(f32[768,256]{0,1:T(8,128)} %fusion.5) | copy-start | bytes 2359300
  127.4 4.8 %copy-start.31 = (f32[768,256]{0,1:T(8,128)S(1)}, f32[768,256]{0,1:T(8,128)}, u32[]{:S(2)}) copy-start(f32[768,256]{0,1:T(8,128)} %copy-done.30) | copy-start | bytes 2359300
  128.5 2.4 %copy-start.27 = (f32[768,256]{0,1:T(8,128)S(1)}, f32[768,256]{0,1:T(8,128)}, u32[]{:S(2)}) copy-start(f32[768,256]{0,1:T(8,128)} %fusion.4) | copy-start | bytes 2359300
  128.5 3.8 %copy-start.21 = (f32[768,256]{0,1:T(8,128)S(1)}, f32[768,256]{0,1:T(8,128)}, u32[]{:S(2)}) copy-start(f32[768,256]{0,1:T(8,128)} %fusion.3) | copy-start | bytes 2359300
  128.5 3.9 %copy-start.16 = (bf16[1,768,1024]{2,1,0:T(8,128)(2,1)S(1)}, bf16[1,768,1024]{2,1,0:T(8,128)(2,1)}, u32[]{:S(2)}) copy-start(bf16[1,768,1024]{2,1,0:T(8,128)(2,1)} %param.4) | copy-start | bytes 4718596
  130.8 20.0 %collective-permute-start.26 = (f32[768,256]{0,1:T(8,128)S(1)}, f32[768,256]{0,1:T(8,128)S(1)}, u32[]{:S(2)}, u32[]{:S(2)}) collective-permute-start(f32[768,256]{0,1:T(8,128)S(1)} %copy-done.27), channel_id=1, source_target_pairs={{0,2},{2,0},{1,3},{3,1},{4,6},{6,4},{5,7},{7,5},{8,10},{10,8},{9,1... | collective-permute-start | bytes 2359304 | tf_op jit(solution)/shard_map/ppermute | solution.py:64
  151.7 2.1 %collective-permute-start.27 = (bf16[768,256]{0,1:T(8,128)(2,1)}, bf16[768,256]{0,1:T(8,128)(2,1)}, u32[]{:S(2)}, u32[]{:S(2)}) collective-permute-start(bf16[768,256]{0,1:T(8,128)(2,1)} %get-tuple-element.92), channel_id=1, source_target_pairs={{0,1},{1,0},{2,3},{3,2},{4,5},{5,4},{6,7},{7,6},{8,9},{9,8},{10,11... | collective-permute-start | bytes 1179656 | tf_op jit(solution)/shard_map/ppermute | solution.py:64
  152.5 2.4 %collective-permute-start.28 = (bf16[768,256]{0,1:T(8,128)(2,1)}, bf16[768,256]{0,1:T(8,128)(2,1)}, u32[]{:S(2)}, u32[]{:S(2)}) collective-permute-start(bf16[768,256]{0,1:T(8,128)(2,1)} %get-tuple-element.84), channel_id=1, source_target_pairs={{0,1},{1,0},{2,3},{3,2},{4,5},{5,4},{6,7},{7,6},{8,9},{9,8},{10,11... | collective-permute-start | bytes 1179656 | tf_op jit(solution)/shard_map/ppermute | solution.py:64
  (15 other events, 22.6 us)

commit v3 on v2

--- a/solution.py
+++ b/solution.py
@@ -101,6 +101,40 @@
     out[...] = total.astype(out.dtype)
 
 
+def kept_sums(flags, grad_0, grad_1, there, *refs):
+    pieces, outs = refs[:8], refs[8:]
+    flag = flags[0] != 0
+    for number, out in enumerate(outs):
+        early_0, early_1, late_0, late_1 = pieces[4 * number : 4 * number + 4]
+        total = times_rows(grad_0[...], jnp.where(flag, early_0[...], late_0[...]))
+        total = total + times_rows(grad_1[...], jnp.where(flag, early_1[...], late_1[...]))
+        if number == 0:
+            total = total + there[...]
+        out[...] = total.astype(out.dtype)
+
+
+def keep(early, grads, there, pieces):
+    tokens, width = grads[0].shape
+    quarter = pieces[0][0][0].shape[0]
+    tile = tokens // 2
+    by_rows = lambda columns: pl.BlockSpec((tile, columns), lambda i: (i, 0))
+    flat = [p for four in pieces for two in four for p in two]
+    return pl.pallas_call(
+        kept_sums,
+        grid=(tokens // tile,),
+        in_specs=[pl.BlockSpec(memory_space=pltpu.SMEM)]
+        + [by_rows(width)] * 2
+        + [by_rows(quarter)]
+        + [pl.BlockSpec(p.shape, lambda i: (0, 0), pipeline_mode=pl.Buffered(1)) for p in flat],
+        out_specs=[by_rows(quarter)] * 2,
+        out_shape=[jax.ShapeDtypeStruct((tokens, quarter), d) for d in (jnp.bfloat16, jnp.float32)],
+        compiler_params=pltpu.CompilerParams(
+            dimension_semantics=("arbitrary",), vmem_limit_bytes=60 * 1024 * 1024
+        ),
+        cost_estimate=pl.CostEstimate(flops=1000, bytes_accessed=1000, transcendentals=0),
+    )(early.astype(jnp.int32).reshape(1), *grads, there, *flat)
+
+
 def forward_sum(numbers, heads, base, pieces, dtype):
     tokens, width = heads[0].shape
     tile = tokens // 2
@@ -110,7 +144,7 @@
         grid=(tokens // tile,),
         in_specs=[pl.BlockSpec((tile, width // 2), lambda i, numbers: (i, numbers[0]))] * 4
         + [by_rows] * len(base)
-        + [pl.BlockSpec(p.shape, lambda i, _: (0, 0)) for p in pieces],
+        + [pl.BlockSpec(p.shape, lambda i, _: (0, 0), pipeline_mode=pl.Buffered(1)) for p in pieces],
         out_specs=by_rows,
     )
     return pl.pallas_call(
@@ -118,7 +152,7 @@
         grid_spec=spec,
         out_shape=jax.ShapeDtypeStruct((tokens, width), dtype),
         compiler_params=pltpu.CompilerParams(
-            dimension_semantics=("arbitrary",), vmem_limit_bytes=26 * 1024 * 1024
+            dimension_semantics=("arbitrary",), vmem_limit_bytes=60 * 1024 * 1024
         ),
         cost_estimate=pl.CostEstimate(flops=1000, bytes_accessed=1000, transcendentals=0),
     )(jnp.stack(numbers).astype(jnp.int32), *heads, *base, *pieces)
@@ -144,53 +178,59 @@
     def weight_rows(block, of_core, of_group):
         return lax.dynamic_slice_in_dim(block, of_core * half + of_group * quarter, quarter, 0)
 
+    def sums(early_pieces, late_pieces):
+        slot_0, slot_1 = (pick(early, e, l) for e, l in zip(early_pieces, late_pieces))
+        return times_rows(grad_0, slot_0) + times_rows(grad_1, slot_1)
+
     mine_0 = weight_rows(weight, core, group)
     middle_0 = send(mine_0, MIDDLE)
     mine_1 = swap(weight_rows(after(weight, mine_0), 1 - core, group), "k")
     head_y = swap(heads, "b")
     near_1 = send(mine_1, BOTH)
-    middle_1 = send(after(mine_1, middle_0), MIDDLE)
+    middle_1 = send(after(mine_1, near_1, middle_0), MIDDLE)
     grad_1 = swap(grad_0, "k")
     x_1 = swap(near_1, "g")
     ahead = is_mid & jnp.logical_not(early)
-    out_2 = send(pick(ahead, middle_0, after(mine_0, near_1)), BOTH)
+    mid_2 = pick(ahead, middle_0, mine_0)
+    out_2 = send(after(mid_2, near_1), BOTH)
     cross_1 = send(after(near_1, middle_1), MIDDLE)
-    mid_3 = pick(early, middle_0, after(middle_1, near_1))
-    at_2 = pick(ahead, middle_0, out_2)
-    out_3 = send(after(mid_3, out_2), OUTWARD)
-    x_2 = swap(after(at_2, x_1, grad_1, head_y), "g")
+    mid_3 = pick(early, middle_0, after(middle_1, mid_2))
+    out_3 = send(after(mid_3, out_2, x_1), OUTWARD)
+    at_2 = pick(ahead, middle_0, after(out_2, mid_3))
+    x_2 = swap(after(at_2, x_1, grad_1), "g")
     cross_0 = send(after(out_2, cross_1), MIDDLE)
     late_weight = after(weight, x_1)
     other_0 = weight_rows(late_weight, core, 1 - group)
     other_1 = swap(weight_rows(late_weight, 1 - core, 1 - group), "k")
-    mid_4 = pick(early, middle_1, after(cross_1, out_3))
-    out_4 = send(mid_4, OUTWARD)
-    at_3 = pick(is_mid, mid_3, after(out_3, x_1))
-    x_3 = swap(after(at_3, x_2), "g")
-    mid_5 = pick(early, cross_1, after(cross_0, out_4))
-    out_5 = send(mid_5, OUTWARD)
-    at_4 = pick(is_mid, mid_4, after(out_4, x_2))
-    x_4 = swap(after(at_4, x_3, other_1), "g")
-    out_6 = send(pick(early, cross_0, after(mine_0, out_5)), OUTWARD)
-    at_5 = pick(is_mid, mid_5, after(out_5, x_3))
-    x_5 = swap(after(at_5, x_4), "g")
-    at_6 = pick(is_mid, pick(early, cross_0, out_2), after(out_6, x_4))
-    x_6 = swap(after(at_6, x_5), "g")
-
-    def sums(early_pieces, late_pieces):
-        slot_0, slot_1 = (pick(early, e, l) for e, l in zip(early_pieces, late_pieces))
-        return times_rows(grad_0, slot_0) + times_rows(grad_1, slot_1)
-
-    due = sums((mine_0, mine_1), (at_2, at_3))
-    there = swap(after(due, head_y), "b")
+    mid_4 = pick(early, middle_1, after(cross_1, at_2))
+    out_4 = send(after(mid_4, out_3), OUTWARD)
+    at_3 = pick(is_mid, mid_3, after(out_3, x_1, other_0, other_1, mid_4, head_y))
+    due_1 = sums((mine_0, mine_1), (at_2, at_3))
+    x_3 = swap(after(at_3, x_2, due_1), "g")
+
+    there = swap(after(due_1, head_y), "b")
     due = sums((other_0, other_1), (x_2, x_3))
     first, due = lax.optimization_barrier((there, due))
     there = swap(due, "b")
+    mid_5 = pick(early, cross_1, after(cross_0, at_3))
+    out_5 = send(after(mid_5, out_4), OUTWARD)
+    at_4 = pick(is_mid, mid_4, after(out_4, x_2, mid_5))
+    x_4 = swap(after(at_4, x_3), "g")
+    late_6 = pick(early, cross_0, after(mine_0, at_4))
+    out_6 = send(after(late_6, out_5), OUTWARD)
+    at_5 = pick(is_mid, mid_5, after(out_5, x_3, late_6))
+    x_5 = swap(after(at_5, x_4), "g")
+
     head_1, head_3 = swap(after(heads, x_2), "k"), swap(after(head_y, x_2), "k")
-    kept_1 = sums((at_3, at_4), (mine_0, mine_1))
     due = sums((at_2, near_1), (at_5, at_4))
-    second, due, kept_1, head_1, head_3 = lax.optimization_barrier((there, due, kept_1, head_1, head_3))
+    kept_1 = sums(*after(((at_3, at_4), (mine_0, mine_1)), first))
+    kept_2 = sums((x_3, x_4), (other_0, other_1))
+    second, due, head_1, head_3, kept_1, kept_2 = lax.optimization_barrier(
+        (there, due, head_1, head_3, kept_1, kept_2)
+    )
     there = swap(due, "b")
+    at_6 = pick(is_mid, pick(early, cross_0, out_2), after(out_6, second))
+    x_6 = swap(after(at_6, x_5), "g")
 
     head_all = [heads, head_1, head_y, head_3]
 
@@ -208,24 +248,32 @@
     pieces_1 = [mine_1, other_1, near_1, x_1, at_4, x_4, pick(early, at_5, at_3), pick(early, x_5, x_3)]
     pieces_0 = [mine_0, other_0, at_2, x_2, pick(early, at_3, at_5), pick(early, x_3, x_5), at_6]
     total_1 = forward(rows_1, pieces_1)
-    kept_2 = sums((x_3, x_4), (other_0, other_1))
     due = sums((x_2, x_1), (x_5, x_4))
-    third, due, total_1, kept_2, x_6 = lax.optimization_barrier((there, due, total_1, kept_2, x_6))
+    third, due, total_1, x_6 = lax.optimization_barrier((there, due, total_1, x_6))
     there = swap(due, "b")
-    projected = forward(rows_0, pieces_0 + [x_6], [swap(total_1, "k")], jnp.bfloat16)
-
-    kept_3 = sums((at_6, at_5), (at_6, near_1))
-    kept_4 = sums((x_6, x_5), (x_6, x_1))
-    done = [(k + t).astype(jnp.bfloat16) for k, t in ((kept_1, first), (kept_2, second), (kept_3, third))]
-    done, kept_4, projected, there = lax.optimization_barrier((done, kept_4, projected, there))
-    done.append((kept_4 + there).astype(jnp.bfloat16))
+    other_part = swap(total_1, "k")
+    projected = forward(rows_0, pieces_0 + [x_6], [other_part], jnp.bfloat16)
+
+    done = [(k + t).astype(jnp.bfloat16) for k, t in ((kept_1, first), (kept_2, second))]
+    last, kept = keep(
+        early, [grad_0, grad_1], third, [((at_6, at_5), (at_6, near_1)), ((x_6, x_5), (x_6, x_1))]
+    )
+    done.append(last)
     first_mine = pick(early, plane // 2, plane & 1) == core
+    here_z, got_z = pick(first_mine, done[0], done[2]), swap(pick(first_mine, done[2], done[0]), "k")
+    done, kept, projected, here_z, got_z, there = lax.optimization_barrier(
+        (done, kept, projected, here_z, got_z, there)
+    )
+    done.append((kept + there).astype(jnp.bfloat16))
+    here_x, got_x = pick(first_mine, done[1], done[3]), swap(pick(first_mine, done[3], done[1]), "k")
     head_grad = jnp.zeros_like(heads)
-    for of_group, one, two in ((group, done[0], done[2]), (1 - group, done[1], done[3])):
-        here = pick(first_mine, one, two)
-        got = swap(pick(first_mine, two, one), "k")
-        head_grad = lax.dynamic_update_slice_in_dim(head_grad, here, core * half + of_group * quarter, 1)
-        head_grad = lax.dynamic_update_slice_in_dim(head_grad, got, (1 - core) * half + of_group * quarter, 1)
+    for of_core, of_group, part in (
+        (core, group, here_z),
+        (1 - core, group, got_z),
+        (core, 1 - group, here_x),
+        (1 - core, 1 - group, got_x),
+    ):
+        head_grad = lax.dynamic_update_slice_in_dim(head_grad, part, of_core * half + of_group * quarter, 1)
     return projected[None], head_grad[None]
 
 

time: 158 us -> 141 us (0.89)
  waiting for transfers between devices: 66 us -> 49 us
  Pallas kernels: 13.5 us -> 23.3 us
  matrix products: 24.5 us -> 15.1 us
  local copies, waits for them, and re-layouts: 12.6 us -> 8.12 us
  other arithmetic: 7.22 us -> 11.4 us
    ppermute x10, waiting for transfers between devices: 50.2 us -> 32.5 us  [send(): return lax.ppermute(value, 'a', pairs)]
    dot_general x16 -> x12, matrix products: 24.5 us -> 15.1 us  [times_rows(): lax.dot_general(left, right, (((1,), (1,)), ((), ())), preferred_element_...]
    pallas_call x0 -> x1, Pallas kernels: none -> 6.17 us  [keep(): pl.pallas_call(kept_sums, grid=(tokens // tile,), in_specs=[pl.BlockSpec(...]
    select_n x13 -> x15, other arithmetic: 7 us -> 11.2 us  [pick(): return jnp.where(flag, yes, no)]
    unnamed x68 -> x52, local copies, waits for them, and re-layouts: 5.81 us -> 2.07 us
    pallas_call x2, Pallas kernels: 13.5 us -> 17.1 us  [forward_sum(): pl.pallas_call(functools.partial(sum_of_products, len(base)), grid_spec=s...]
    broadcast_in_dim x5 -> x1, local copies, waits for them, and re-layouts: 2.85 us -> 0.18 us  [grid_4(): return (projected[None], head_grad[None])]
  transfers between devices with their start and end apart: 29 -> 29, of which waited for: 12 -> 14; matrix products, arithmetic and copies ran while one was open for 22% -> 21% of each run, Pallas kernels for 9% -> 17%
where the time goes in v3:
time: 141 us; the launch traced here: 139 us
  waiting for transfers between devices  49 us (35%)
  starting transfers between devices  31.4 us (22%)
  Pallas kernels  23.3 us (17%)
  matrix products  15.1 us (11%)
  other arithmetic  11.4 us (8%)
  local copies, waits for them, and re-layouts  8.12 us (6%)
    ppermute x10, waiting for transfers between devices, send(): return lax.ppermute(value, 'a', pairs)  32.5 us
    pallas_call x2, Pallas kernels, forward_sum(): pl.pallas_call(functools.partial(sum_of_products, len(base)), grid_spec=s...  17.1 us
    ppermute x10, starting transfers between devices, send(): return lax.ppermute(value, 'a', pairs)  17 us
    ppermute x19, waiting for transfers between devices, swap(): return lax.ppermute(value, axis, [(0, 1), (1, 0)])  16.5 us
    dot_general x12, matrix products, times_rows(): lax.dot_general(left, right, (((1,), (1,)), ((), ())), preferred_element_...  15.1 us
    ppermute x19, starting transfers between devices, swap(): return lax.ppermute(value, axis, [(0, 1), (1, 0)])  14.5 us
    select_n x15, other arithmetic, pick(): return jnp.where(flag, yes, no)  11.2 us
    pallas_call x1, Pallas kernels, keep(): pl.pallas_call(kept_sums, grid=(tokens // tile,), in_specs=[pl.BlockSpec(...  6.17 us
  transfers between devices with their start and end apart: 29, of which 14 were waited for; matrix products, arithmetic and copies ran while one was open for 21% of the time, Pallas kernels for 17%

profile of v3, /device:TPU:0, one launch (start us, length us, event | category | flops | bytes accessed | tf_op | source)
XLA Modules:
  0.0 139.4 jit_solution(18030946062981479030)
XLA Ops:
  0.7 2.0 %dynamic-slice_bitcast_fusion.refs_5_ = bf16[256,1024]{1,0:T(8,128)(2,1)} fusion(bf16[1,1024,1024]{2,1,0:T(8,128)(2,1)} %param.5, s32[]{:T(128)S(6)} %select_n.205), kind=kLoop, calls=%fused_computation.34 | loop fusion | bytes 1048580 | tf_op jit(solution)/shard_map/dynamic_slice | solution.py:179
  2.7 1.1 constant_dynamic-slice_fusion.2
  4.3 1.5 %collective-permute-start = (bf16[256,1024]{1,0:T(8,128)(2,1)}, bf16[256,1024]{1,0:T(8,128)(2,1)}, u32[]{:S(2)}, u32[]{:S(2)}) collective-permute-start(bf16[256,1024]{1,0:T(8,128)(2,1)} %dynamic-slice_bitcast_fusion.refs_5_), channel_id=1, source_target_pairs={{4,8},{8,4},{5,9},{9,5},{6,10},{10,6},{7,11},{11,7},{20,24},{24,20... | collective-permute-start | bytes 1572872 | tf_op jit(solution)/shard_map/ppermute | solution.py:68
  6.0 4.5 %collective-permute-start.2 = (bf16[256,1024]{1,0:T(8,128)(2,1)}, bf16[256,1024]{1,0:T(8,128)(2,1)}, u32[]{:S(2)}, u32[]{:S(2)}) collective-permute-start(bf16[256,1024]{1,0:T(8,128)(2,1)} %collective-permute-done.1.refs_4_), channel_id=1, source_target_pairs={{0,4},{12,8},{4,0},{8,12},{1,5},{13,9},{5,1},{9,13},{2,6},{14,10},... | collective-permute-start | bytes 1572872 | tf_op jit(solution)/shard_map/ppermute | solution.py:68
  10.4 1.5 %collective-permute-start.9 = (bf16[768,1024]{1,0:T(8,128)(2,1)}, bf16[768,1024]{1,0:T(8,128)(2,1)}, u32[]{:S(2)}, u32[]{:S(2)}) collective-permute-start(bf16[768,1024]{1,0:T(8,128)(2,1)} %bitcast.58), channel_id=1, source_target_pairs={{0,2},{2,0},{1,3},{3,1},{4,6},{6,4},{5,7},{7,5},{8,10},{10,8},{9,1... | collective-permute-start | bytes 4718600 | tf_op jit(solution)/shard_map/ppermute | solution.py:64
  12.0 11.1 %collective-permute-done.2.refs_6_.refs_3_ = bf16[256,1024]{1,0:T(8,128)(2,1)} collective-permute-done((bf16[256,1024]{1,0:T(8,128)(2,1)}, bf16[256,1024]{1,0:T(8,128)(2,1)}, u32[]{:S(2)}, u32[]{:S(2)}) %collective-permute-start.2) | collective-permute-done | bytes 524320 | tf_op jit(solution)/shard_map/ppermute | solution.py:68
  23.1 1.5 %collective-permute-start.4 = (bf16[256,1024]{1,0:T(8,128)(2,1)}, bf16[256,1024]{1,0:T(8,128)(2,1)}, u32[]{:S(2)}, u32[]{:S(2)}) collective-permute-start(bf16[256,1024]{1,0:T(8,128)(2,1)} %collective-permute-done.1.refs_4_), channel_id=1, source_target_pairs={{4,8},{8,4},{5,9},{9,5},{6,10},{10,6},{7,11},{11,7},{20,24},{24,20... | collective-permute-start | bytes 1572872 | tf_op jit(solution)/shard_map/ppermute | solution.py:68
  24.5 2.0 %broadcast_select_fusion.4 = bf16[256,1024]{1,0:T(8,128)(2,1)} fusion(bf16[256,1024]{1,0:T(8,128)(2,1)} %collective-permute-done, pred[]{:T(512)S(6)} %and.55, bf16[1,1024,1024]{2,1,0:T(8,128)(2,1)} %param.5, s32[]{:T(128)S(6)} %select_n.205), kind=kLoop, calls=%fused_computation.39 | loop fusion | flops 262144 | bytes 1572869 | tf_op jit(solution)/shard_map/jit(_where)/select_n | solution.py:76
  26.6 2.8 %collective-permute-start.3 = (bf16[256,1024]{1,0:T(8,128)(2,1)}, bf16[256,1024]{1,0:T(8,128)(2,1)}, u32[]{:S(2)}, u32[]{:S(2)}) collective-permute-start(bf16[256,1024]{1,0:T(8,128)(2,1)} %broadcast_select_fusion.4), channel_id=1, source_target_pairs={{0,4},{12,8},{4,0},{8,12},{1,5},{13,9},{5,1},{9,13},{2,6},{14,10},... | collective-permute-start | bytes 1572872 | tf_op jit(solution)/shard_map/ppermute | solution.py:68
  29.4 1.5 %collective-permute-start.5 = (bf16[256,1024]{1,0:T(8,128)(2,1)}, bf16[256,1024]{1,0:T(8,128)(2,1)}, u32[]{:S(2)}, u32[]{:S(2)}) collective-permute-start(bf16[256,1024]{1,0:T(8,128)(2,1)} %collective-permute-done.2.refs_6_.refs_3_), channel_id=1, source_target_pairs={{0,16},{16,0},{1,17},{17,1},{2,18},{18,2},{3,19},{19,3},{4,20},{20... | collective-permute-start | bytes 1572872 | tf_op jit(solution)/shard_map/ppermute | solution.py:64
  32.2 1.1 broadcast_select_fusion.12
  33.3 7.6 %collective-permute-done.3 = bf16[256,1024]{1,0:T(8,128)(2,1)} collective-permute-done((bf16[256,1024]{1,0:T(8,128)(2,1)}, bf16[256,1024]{1,0:T(8,128)(2,1)}, u32[]{:S(2)}, u32[]{:S(2)}) %collective-permute-start.3) | collective-permute-done | bytes 524320 | tf_op jit(solution)/shard_map/ppermute | solution.py:68
  40.9 1.5 %collective-permute-done.5.refs_7_ = bf16[256,1024]{1,0:T(8,128)(2,1)} collective-permute-done((bf16[256,1024]{1,0:T(8,128)(2,1)}, bf16[256,1024]{1,0:T(8,128)(2,1)}, u32[]{:S(2)}, u32[]{:S(2)}) %collective-permute-start.5) | collective-permute-done | bytes 524320 | tf_op jit(solution)/shard_map/ppermute | solution.py:64
  42.4 1.3 collective-permute-start.6
  43.7 1.3 constant_dynamic-slice_fusion
  45.1 1.2 broadcast_select_fusion.3.refs_7_
  46.3 1.6 %collective-permute-start.12 = (bf16[256,1024]{1,0:T(8,128)(2,1)S(1)}, bf16[256,1024]{1,0:T(8,128)(2,1)S(1)}, u32[]{:S(2)}, u32[]{:S(2)}) collective-permute-start(bf16[256,1024]{1,0:T(8,128)(2,1)S(1)} %broadcast_select_fusion.3.refs_7_), channel_id=1, source_target_pairs={{0,16},{16,0},{1,17},{17,1},{2,18},{18,2},{3,19},{19,3},{4,20},{20... | collective-permute-start | bytes 1572872 | tf_op jit(solution)/shard_map/ppermute | solution.py:64
  48.0 8.1 %collective-permute-done.6 = bf16[256,1024]{1,0:T(8,128)(2,1)S(1)} collective-permute-done((bf16[256,1024]{1,0:T(8,128)(2,1)S(1)}, bf16[256,1024]{1,0:T(8,128)(2,1)S(1)}, u32[]{:S(2)}, u32[]{:S(2)}) %collective-permute-start.6) | collective-permute-done | bytes 524320 | tf_op jit(solution)/shard_map/ppermute | solution.py:68
  56.8 1.3 collective-permute-start.16
  59.4 1.2 collective-permute-done.12.refs_8_
  60.6 1.5 %collective-permute-start.13 = (bf16[256,1024]{1,0:T(8,128)(2,1)S(1)}, bf16[256,1024]{1,0:T(8,128)(2,1)S(1)}, u32[]{:S(2)}, u32[]{:S(2)}) collective-permute-start(bf16[256,1024]{1,0:T(8,128)(2,1)S(1)} %broadcast_select_fusion.2), channel_id=1, source_target_pairs={{0,16},{16,0},{1,17},{17,1},{2,18},{18,2},{3,19},{19,3},{4,20},{20... | collective-permute-start | bytes 1572872 | tf_op jit(solution)/shard_map/ppermute | solution.py:64
  62.1 2.5 %collective-permute-start.11 = (f32[768,256]{1,0:T(8,128)S(1)}, f32[768,256]{1,0:T(8,128)S(1)}, u32[]{:S(2)}, u32[]{:S(2)}) collective-permute-start(f32[768,256]{1,0:T(8,128)S(1)} %fusion.5), channel_id=1, source_target_pairs={{0,2},{2,0},{1,3},{3,1},{4,6},{6,4},{5,7},{7,5},{8,10},{10,8},{9,1... | collective-permute-start | bytes 2359304 | tf_op jit(solution)/shard_map/ppermute | solution.py:64
  65.1 4.5 %collective-permute-done.16 = bf16[256,1024]{1,0:T(8,128)(2,1)S(1)} collective-permute-done((bf16[256,1024]{1,0:T(8,128)(2,1)S(1)}, bf16[256,1024]{1,0:T(8,128)(2,1)S(1)}, u32[]{:S(2)}, u32[]{:S(2)}) %collective-permute-start.16) | collective-permute-done | bytes 524320 | tf_op jit(solution)/shard_map/ppermute | solution.py:68
  69.7 1.3 collective-permute-start.17
  71.0 3.0 %collective-permute-done.13 = bf16[256,1024]{1,0:T(8,128)(2,1)S(1)} collective-permute-done((bf16[256,1024]{1,0:T(8,128)(2,1)S(1)}, bf16[256,1024]{1,0:T(8,128)(2,1)S(1)}, u32[]{:S(2)}, u32[]{:S(2)}) %collective-permute-start.13) | collective-permute-done | bytes 524320 | tf_op jit(solution)/shard_map/ppermute | solution.py:64
  74.0 1.5 %collective-permute-start.20 = (bf16[256,1024]{1,0:T(8,128)(2,1)S(1)}, bf16[256,1024]{1,0:T(8,128)(2,1)S(1)}, u32[]{:S(2)}, u32[]{:S(2)}) collective-permute-start(bf16[256,1024]{1,0:T(8,128)(2,1)S(1)} %broadcast_select_fusion.1.refs_8_), channel_id=1, source_target_pairs={{0,16},{16,0},{1,17},{17,1},{2,18},{18,2},{3,19},{19,3},{4,20},{20... | collective-permute-start | bytes 1572872 | tf_op jit(solution)/shard_map/ppermute | solution.py:64
  76.1 1.1 broadcast_select_fusion.9
  78.5 2.4 %collective-permute-done.11 = f32[768,256]{1,0:T(8,128)S(1)} collective-permute-done((f32[768,256]{1,0:T(8,128)S(1)}, f32[768,256]{1,0:T(8,128)S(1)}, u32[]{:S(2)}, u32[]{:S(2)}) %collective-permute-start.11) | collective-permute-done | bytes 786464 | tf_op jit(solution)/shard_map/ppermute | solution.py:64
  80.8 1.4 %collective-permute-start.14 = (f32[768,256]{1,0:T(8,128)S(1)}, f32[768,256]{1,0:T(8,128)S(1)}, u32[]{:S(2)}, u32[]{:S(2)}) collective-permute-start(f32[768,256]{1,0:T(8,128)S(1)} %fusion.4), channel_id=1, source_target_pairs={{0,2},{2,0},{1,3},{3,1},{4,6},{6,4},{5,7},{7,5},{8,10},{10,8},{9,1... | collective-permute-start | bytes 2359304 | tf_op jit(solution)/shard_map/ppermute | solution.py:64
  82.3 1.7 %fusion.12 = f32[256,768]{0,1:T(8,128)S(1)} fusion(bf16[768,1024]{1,0:T(8,128)(2,1)S(1)} %collective-permute-done.10.grad_1, bf16[256,1024]{1,0:T(8,128)(2,1)S(1)} %broadcast_select_fusion.1.refs_8_, bf16[256,1024]{1,0:T(8,128)(2,1)} %collective-permute-done.1.refs_4_, pred[]{:T(512)S(6)} %ne.91), kind=kOutput, calls=%fused_computation.22 | convolution fusion | flops 402915328 | bytes 3407873 | tf_op jit(solution)/shard_map/dot_general | solution.py:84
  83.9 2.5 %fusion.2 = f32[768,256]{1,0:T(8,128)} fusion(f32[256,768]{0,1:T(8,128)S(1)} %fusion.12, bf16[256,1024]{1,0:T(8,128)(2,1)S(1)} %broadcast_select_fusion.2, bf16[256,1024]{1,0:T(8,128)(2,1)} %dynamic-slice_bitcast_fusion.refs_5_, pred[]{:T(512)S(6)} %ne.91, bf16[1,768,1024]{2,1,0:T(8,128)(2,1)S(1)} %copy-done), kind=kOutput, calls=%fused_computation.5 | convolution fusion | flops 403111936 | bytes 4194305 | tf_op jit(solution)/shard_map/dot_general | solution.py:84
  86.5 1.5 %collective-permute-start.23 = (bf16[256,1024]{1,0:T(8,128)(2,1)S(1)}, bf16[256,1024]{1,0:T(8,128)(2,1)S(1)}, u32[]{:S(2)}, u32[]{:S(2)}) collective-permute-start(bf16[256,1024]{1,0:T(8,128)(2,1)S(1)} %broadcast_select_fusion.9), channel_id=1, source_target_pairs={{4,0},{8,12},{5,1},{9,13},{6,2},{10,14},{7,3},{11,15},{20,16},{24,... | collective-permute-start | bytes 1572872 | tf_op jit(solution)/shard_map/ppermute | solution.py:68
  90.0 1.5 %fusion.3 = f32[768,256]{1,0:T(8,128)} fusion(f32[256,768]{0,1:T(8,128)S(1)} %fusion.15, bf16[256,1024]{1,0:T(8,128)(2,1)S(1)} %broadcast_select_fusion.3.refs_7_, bf16[256,1024]{1,0:T(8,128)(2,1)S(1)} %get-tuple-element.86.refs_1_, pred[]{:T(512)S(6)} %ne.91, bf16[1,768,1024]{2,1,0:T(8,128)(2,1)S(1)} %copy-done), kind=kOutput, calls=%fused_computation.7 | convolution fusion | flops 403111936 | bytes 4194305 | tf_op jit(solution)/shard_map/dot_general | solution.py:84
  91.5 1.5 %fusion.1 = f32[768,256]{1,0:T(8,128)} fusion(f32[256,768]{0,1:T(8,128)S(1)} %fusion.9, bf16[256,1024]{1,0:T(8,128)(2,1)S(1)} %collective-permute-done.13, bf16[256,1024]{1,0:T(8,128)(2,1)S(1)} %get-tuple-element.111.refs_6_, pred[]{:T(512)S(6)} %ne.91, bf16[1,768,1024]{2,1,0:T(8,128)(2,1)S(1)} %copy-done), kind=kOutput, calls=%fused_computation.3 | convolution fusion | flops 403111936 | bytes 4194305 | tf_op jit(solution)/shard_map/dot_general | solution.py:84
  93.1 1.5 %fusion.6 = f32[256,768]{0,1:T(8,128)} fusion(bf16[768,1024]{1,0:T(8,128)(2,1)S(1)} %collective-permute-done.10.grad_1, bf16[256,1024]{1,0:T(8,128)(2,1)} %collective-permute-done.5.refs_7_, bf16[256,1024]{1,0:T(8,128)(2,1)S(1)} %collective-permute-done.20.refs_9_, pred[]{:T(512)S(6)} %ne.91), kind=kOutput, calls=%fused_computation.16 | convolution fusion | flops 402915328 | bytes 3407873 | tf_op jit(solution)/shard_map/dot_general | solution.py:84
  95.4 2.7 %collective-permute-done.14 = f32[768,256]{1,0:T(8,128)S(1)} collective-permute-done((f32[768,256]{1,0:T(8,128)S(1)}, f32[768,256]{1,0:T(8,128)S(1)}, u32[]{:S(2)}, u32[]{:S(2)}) %collective-permute-start.14) | collective-permute-done | bytes 786464 | tf_op jit(solution)/shard_map/ppermute | solution.py:64
  98.2 1.2 collective-permute-done.23
  99.4 1.2 select_select_fusion.refs_0_.refs_2_.refs_11_
  101.2 1.1 broadcast_select_fusion.5
  102.3 8.4 %shard_map.50 = f32[768,1024]{1,0:T(8,128)} custom-call(s32[17]{0:T(128)} %stack.29.numbers, bf16[768,1024]{1,0:T(8,128)(2,1)} %bitcast.59, bf16[768,1024]{1,0:T(8,128)(2,1)} %copy-done.9, bf16[768,1024]{1,0:T(8,128)(2,1)} %collective-permute-done.9.refs_2_, bf16[768,1024]{1,0:T(8,128)(2,1)} %copy-done.8, bf16[256,1024]{1,0:T(8,128)(2,1)} %collective-permute-done.1.refs_4_, ...), custom_call_target="tpu_custom_call" | custom-call | flops 1000 | bytes 1000 | tf_op jit(solution)/shard_map/pallas_call | solution.py:150
  110.7 2.7 %fusion = f32[768,256]{1,0:T(8,128)} fusion(f32[256,768]{0,1:T(8,128)} %fusion.6, bf16[256,1024]{1,0:T(8,128)(2,1)S(1)} %copy-done.11, bf16[256,1024]{1,0:T(8,128)(2,1)S(1)} %copy-done.13, pred[]{:T(512)S(6)} %ne.91, bf16[1,768,1024]{2,1,0:T(8,128)(2,1)S(1)} %copy-done), kind=kOutput, calls=%fused_computation.1 | convolution fusion | flops 403111936 | bytes 4194305 | tf_op jit(solution)/shard_map/dot_general | solution.py:84
  113.4 2.0 %collective-permute-done.21.there = f32[768,256]{1,0:T(8,128)} collective-permute-done((f32[768,256]{1,0:T(8,128)}, f32[768,256]{1,0:T(8,128)}, u32[]{:S(2)}, u32[]{:S(2)}) %collective-permute-start.21) | collective-permute-done | bytes 786464 | tf_op jit(solution)/shard_map/ppermute | solution.py:64
  116.7 6.2 %shard_map.51 = (bf16[768,256]{1,0:T(8,128)(2,1)}, f32[768,256]{1,0:T(8,128)}) custom-call(s32[1]{0:T(128)} %bitcast.9.flags, bf16[768,1024]{1,0:T(8,128)(2,1)} %bitcast.56, bf16[768,1024]{1,0:T(8,128)(2,1)} %copy-done.1, f32[768,256]{1,0:T(8,128)} %collective-permute-done.21.there, bf16[256,1024]{1,0:T(8,128)(2,1)} %copy-done.5, ...), custom_call_target="tpu_custom_call" | custom-call | flops 1000 | bytes 1000 | tf_op jit(solution)/shard_map/pallas_call | solution.py:122
  122.9 1.3 broadcast_select_fusion.14
  125.3 8.7 %shard_map.52 = bf16[768,1024]{1,0:T(8,128)(2,1)} custom-call(s32[17]{0:T(128)} %stack.32.numbers, bf16[768,1024]{1,0:T(8,128)(2,1)} %bitcast.60, bf16[768,1024]{1,0:T(8,128)(2,1)} %copy-done.9, bf16[768,1024]{1,0:T(8,128)(2,1)} %collective-permute-done.9.refs_2_, bf16[768,1024]{1,0:T(8,128)(2,1)} %copy-done.8, f32[768,1024]{1,0:T(8,128)} %collective-permute-done.25.refs_4_, ...), custom_call_target="tpu_custom_call" | custom-call | flops 1000 | bytes 1000 | tf_op jit(solution)/shard_map/pallas_call | solution.py:150
  134.0 2.3 %collective-permute-done.27 = f32[768,256]{1,0:T(8,128)S(1)} collective-permute-done((f32[768,256]{1,0:T(8,128)}, f32[768,256]{1,0:T(8,128)S(1)}, u32[]{:S(2)}, u32[]{:S(2)}) %collective-permute-start.27) | collective-permute-done | bytes 786464 | tf_op jit(solution)/shard_map/ppermute | solution.py:64
  136.9 1.3 collective-permute-done.28
  138.2 1.1 copy-done.19
  (103 shorter events, 13.3 us)
Async XLA Ops:
  0.6 9.8 %copy-start = (bf16[1,768,1024]{2,1,0:T(8,128)(2,1)S(1)}, bf16[1,768,1024]{2,1,0:T(8,128)(2,1)}, u32[]{:S(2)}) copy-start(bf16[1,768,1024]{2,1,0:T(8,128)(2,1)} %param.4) | copy-start | bytes 4718596
  3.8 2.2 %collective-permute-start.1 = (bf16[256,1024]{1,0:T(8,128)(2,1)S(1)}, bf16[256,1024]{1,0:T(8,128)(2,1)}, u32[]{:S(2)}, u32[]{:S(2)}) collective-permute-start(bf16[256,1024]{1,0:T(8,128)(2,1)S(1)} %constant_dynamic-slice_fusion.2), channel_id=1, source_target_pairs={{0,1},{1,0},{2,3},{3,2},{4,5},{5,4},{6,7},{7,6},{8,9},{9,8},{10,11... | collective-permute-start | bytes 1572872 | tf_op jit(solution)/shard_map/ppermute | solution.py:64
  4.3 7.7 %collective-permute-start = (bf16[256,1024]{1,0:T(8,128)(2,1)}, bf16[256,1024]{1,0:T(8,128)(2,1)}, u32[]{:S(2)}, u32[]{:S(2)}) collective-permute-start(bf16[256,1024]{1,0:T(8,128)(2,1)} %dynamic-slice_bitcast_fusion.refs_5_), channel_id=1, source_target_pairs={{4,8},{8,4},{5,9},{9,5},{6,10},{10,6},{7,11},{11,7},{20,24},{24,20... | collective-permute-start | bytes 1572872 | tf_op jit(solution)/shard_map/ppermute | solution.py:68
  6.0 17.1 %collective-permute-start.2 = (bf16[256,1024]{1,0:T(8,128)(2,1)}, bf16[256,1024]{1,0:T(8,128)(2,1)}, u32[]{:S(2)}, u32[]{:S(2)}) collective-permute-start(bf16[256,1024]{1,0:T(8,128)(2,1)} %collective-permute-done.1.refs_4_), channel_id=1, source_target_pairs={{0,4},{12,8},{4,0},{8,12},{1,5},{13,9},{5,1},{9,13},{2,6},{14,10},... | collective-permute-start | bytes 1572872 | tf_op jit(solution)/shard_map/ppermute | solution.py:68
  10.4 35.8 %collective-permute-start.10 = (bf16[768,1024]{1,0:T(8,128)(2,1)S(1)}, bf16[768,1024]{1,0:T(8,128)(2,1)S(1)}, u32[]{:S(2)}, u32[]{:S(2)}) collective-permute-start(bf16[768,1024]{1,0:T(8,128)(2,1)S(1)} %bitcast.57), channel_id=1, source_target_pairs={{0,1},{1,0},{2,3},{3,2},{4,5},{5,4},{6,7},{7,6},{8,9},{9,8},{10,11... | collective-permute-start | bytes 4718600 | tf_op jit(solution)/shard_map/ppermute | solution.py:64
  10.4 37.5 %collective-permute-start.9 = (bf16[768,1024]{1,0:T(8,128)(2,1)}, bf16[768,1024]{1,0:T(8,128)(2,1)}, u32[]{:S(2)}, u32[]{:S(2)}) collective-permute-start(bf16[768,1024]{1,0:T(8,128)(2,1)} %bitcast.58), channel_id=1, source_target_pairs={{0,2},{2,0},{1,3},{3,1},{4,6},{6,4},{5,7},{7,5},{8,10},{10,8},{9,1... | collective-permute-start | bytes 4718600 | tf_op jit(solution)/shard_map/ppermute | solution.py:64
  23.1 8.5 %collective-permute-start.4 = (bf16[256,1024]{1,0:T(8,128)(2,1)}, bf16[256,1024]{1,0:T(8,128)(2,1)}, u32[]{:S(2)}, u32[]{:S(2)}) collective-permute-start(bf16[256,1024]{1,0:T(8,128)(2,1)} %collective-permute-done.1.refs_4_), channel_id=1, source_target_pairs={{4,8},{8,4},{5,9},{9,5},{6,10},{10,6},{7,11},{11,7},{20,24},{24,20... | collective-permute-start | bytes 1572872 | tf_op jit(solution)/shard_map/ppermute | solution.py:68
  26.6 14.4 %collective-permute-start.3 = (bf16[256,1024]{1,0:T(8,128)(2,1)}, bf16[256,1024]{1,0:T(8,128)(2,1)}, u32[]{:S(2)}, u32[]{:S(2)}) collective-permute-start(bf16[256,1024]{1,0:T(8,128)(2,1)} %broadcast_select_fusion.4), channel_id=1, source_target_pairs={{0,4},{12,8},{4,0},{8,12},{1,5},{13,9},{5,1},{9,13},{2,6},{14,10},... | collective-permute-start | bytes 1572872 | tf_op jit(solution)/shard_map/ppermute | solution.py:68
  29.4 13.0 %collective-permute-start.5 = (bf16[256,1024]{1,0:T(8,128)(2,1)}, bf16[256,1024]{1,0:T(8,128)(2,1)}, u32[]{:S(2)}, u32[]{:S(2)}) collective-permute-start(bf16[256,1024]{1,0:T(8,128)(2,1)} %collective-permute-done.2.refs_6_.refs_3_), channel_id=1, source_target_pairs={{0,16},{16,0},{1,17},{17,1},{2,18},{18,2},{3,19},{19,3},{4,20},{20... | collective-permute-start | bytes 1572872 | tf_op jit(solution)/shard_map/ppermute | solution.py:64
  31.5 16.4 %collective-permute-start.8 = (bf16[256,1024]{1,0:T(8,128)(2,1)}, bf16[256,1024]{1,0:T(8,128)(2,1)S(1)}, u32[]{:S(2)}, u32[]{:S(2)}) collective-permute-start(bf16[256,1024]{1,0:T(8,128)(2,1)} %collective-permute-done.2.refs_6_.refs_3_), channel_id=1, source_target_pairs={{4,8},{8,4},{5,9},{9,5},{6,10},{10,6},{7,11},{11,7},{20,24},{24,20... | collective-permute-start | bytes 1572872 | tf_op jit(solution)/shard_map/ppermute | solution.py:68
  42.4 13.7 %collective-permute-start.6 = (bf16[256,1024]{1,0:T(8,128)(2,1)S(1)}, bf16[256,1024]{1,0:T(8,128)(2,1)S(1)}, u32[]{:S(2)}, u32[]{:S(2)}) collective-permute-start(bf16[256,1024]{1,0:T(8,128)(2,1)S(1)} %broadcast_select_fusion.12), channel_id=1, source_target_pairs={{4,0},{8,12},{5,1},{9,13},{6,2},{10,14},{7,3},{11,15},{20,16},{24,... | collective-permute-start | bytes 1572872 | tf_op jit(solution)/shard_map/ppermute | solution.py:68
  45.0 46.6 %copy-start.4 = (bf16[256,1024]{1,0:T(8,128)(2,1)}, bf16[256,1024]{1,0:T(8,128)(2,1)S(1)}, u32[]{:S(2)}) copy-start(bf16[256,1024]{1,0:T(8,128)(2,1)S(1)} %get-tuple-element.111.refs_6_) | copy-start | bytes 1572868
  45.0 11.1 %collective-permute-start.7 = (bf16[256,1024]{1,0:T(8,128)(2,1)S(1)}, bf16[256,1024]{1,0:T(8,128)(2,1)S(1)}, u32[]{:S(2)}, u32[]{:S(2)}) collective-permute-start(bf16[256,1024]{1,0:T(8,128)(2,1)S(1)} %get-tuple-element.110), channel_id=1, source_target_pairs={{0,1},{1,0},{2,3},{3,2},{4,5},{5,4},{6,7},{7,6},{8,9},{9,8},{10,11... | collective-permute-start | bytes 1572872 | tf_op jit(solution)/shard_map/ppermute | solution.py:64
  46.3 43.7 %copy-start.2 = (bf16[256,1024]{1,0:T(8,128)(2,1)}, bf16[256,1024]{1,0:T(8,128)(2,1)S(1)}, u32[]{:S(2)}) copy-start(bf16[256,1024]{1,0:T(8,128)(2,1)S(1)} %broadcast_select_fusion.3.refs_7_) | copy-start | bytes 1572868
  46.3 46.8 %copy-start.1 = (bf16[768,1024]{1,0:T(8,128)(2,1)}, bf16[768,1024]{1,0:T(8,128)(2,1)S(1)}, u32[]{:S(2)}) copy-start(bf16[768,1024]{1,0:T(8,128)(2,1)S(1)} %collective-permute-done.10.grad_1) | copy-start | bytes 4718596
  46.3 14.3 %collective-permute-start.12 = (bf16[256,1024]{1,0:T(8,128)(2,1)S(1)}, bf16[256,1024]{1,0:T(8,128)(2,1)S(1)}, u32[]{:S(2)}, u32[]{:S(2)}) collective-permute-start(bf16[256,1024]{1,0:T(8,128)(2,1)S(1)} %broadcast_select_fusion.3.refs_7_), channel_id=1, source_target_pairs={{0,16},{16,0},{1,17},{17,1},{2,18},{18,2},{3,19},{19,3},{4,20},{20... | collective-permute-start | bytes 1572872 | tf_op jit(solution)/shard_map/ppermute | solution.py:64
  56.1 33.3 %copy-start.15 = (bf16[256,1024]{1,0:T(8,128)(2,1)}, bf16[256,1024]{1,0:T(8,128)(2,1)S(1)}, u32[]{:S(2)}) copy-start(bf16[256,1024]{1,0:T(8,128)(2,1)S(1)} %collective-permute-done.7.refs_5_) | copy-start | bytes 1572868
  56.1 8.4 %collective-permute-start.15 = (bf16[256,1024]{1,0:T(8,128)(2,1)}, bf16[256,1024]{1,0:T(8,128)(2,1)S(1)}, u32[]{:S(2)}, u32[]{:S(2)}) collective-permute-start(bf16[256,1024]{1,0:T(8,128)(2,1)} %collective-permute-done.3), channel_id=1, source_target_pairs={{4,8},{8,4},{5,9},{9,5},{6,10},{10,6},{7,11},{11,7},{20,24},{24,20... | collective-permute-start | bytes 1572872 | tf_op jit(solution)/shard_map/ppermute | solution.py:68
  56.8 12.8 %collective-permute-start.16 = (bf16[256,1024]{1,0:T(8,128)(2,1)S(1)}, bf16[256,1024]{1,0:T(8,128)(2,1)S(1)}, u32[]{:S(2)}, u32[]{:S(2)}) collective-permute-start(bf16[256,1024]{1,0:T(8,128)(2,1)S(1)} %broadcast_select_fusion.11), channel_id=1, source_target_pairs={{4,0},{8,12},{5,1},{9,13},{6,2},{10,14},{7,3},{11,15},{20,16},{24,... | collective-permute-start | bytes 1572872 | tf_op jit(solution)/shard_map/ppermute | solution.py:68
  58.8 5.8 %copy-start.7 = (bf16[1,768,1024]{2,1,0:T(8,128)(2,1)S(1)}, bf16[1,768,1024]{2,1,0:T(8,128)(2,1)}, u32[]{:S(2)}) copy-start(bf16[1,768,1024]{2,1,0:T(8,128)(2,1)} %param.3) | copy-start | bytes 4718596
  60.6 17.2 %copy-start.10 = (bf16[256,1024]{1,0:T(8,128)(2,1)}, bf16[256,1024]{1,0:T(8,128)(2,1)S(1)}, u32[]{:S(2)}) copy-start(bf16[256,1024]{1,0:T(8,128)(2,1)S(1)} %collective-permute-done.12.refs_8_) | copy-start | bytes 1572868
  60.6 13.4 %collective-permute-start.13 = (bf16[256,1024]{1,0:T(8,128)(2,1)S(1)}, bf16[256,1024]{1,0:T(8,128)(2,1)S(1)}, u32[]{:S(2)}, u32[]{:S(2)}) collective-permute-start(bf16[256,1024]{1,0:T(8,128)(2,1)S(1)} %broadcast_select_fusion.2), channel_id=1, source_target_pairs={{0,16},{16,0},{1,17},{17,1},{2,18},{18,2},{3,19},{19,3},{4,20},{20... | collective-permute-start | bytes 1572872 | tf_op jit(solution)/shard_map/ppermute | solution.py:64
  62.1 18.7 %collective-permute-start.11 = (f32[768,256]{1,0:T(8,128)S(1)}, f32[768,256]{1,0:T(8,128)S(1)}, u32[]{:S(2)}, u32[]{:S(2)}) collective-permute-start(f32[768,256]{1,0:T(8,128)S(1)} %fusion.5), channel_id=1, source_target_pairs={{0,2},{2,0},{1,3},{3,1},{4,6},{6,4},{5,7},{7,5},{8,10},{10,8},{9,1... | collective-permute-start | bytes 2359304 | tf_op jit(solution)/shard_map/ppermute | solution.py:64
  64.5 33.6 %collective-permute-start.19 = (bf16[768,1024]{1,0:T(8,128)(2,1)}, bf16[768,1024]{1,0:T(8,128)(2,1)S(1)}, u32[]{:S(2)}, u32[]{:S(2)}) collective-permute-start(bf16[768,1024]{1,0:T(8,128)(2,1)} %collective-permute-done.9.refs_2_), channel_id=1, source_target_pairs={{0,1},{1,0},{2,3},{3,2},{4,5},{5,4},{6,7},{7,6},{8,9},{9,8},{10,11... | collective-permute-start | bytes 4718600 | tf_op jit(solution)/shard_map/ppermute | solution.py:64
  64.6 33.6 %collective-permute-start.18 = (bf16[768,1024]{1,0:T(8,128)(2,1)S(1)}, bf16[768,1024]{1,0:T(8,128)(2,1)S(1)}, u32[]{:S(2)}, u32[]{:S(2)}) collective-permute-start(bf16[768,1024]{1,0:T(8,128)(2,1)S(1)} %bitcast.61), channel_id=1, source_target_pairs={{0,1},{1,0},{2,3},{3,2},{4,5},{5,4},{6,7},{7,6},{8,9},{9,8},{10,11... | collective-permute-start | bytes 4718600 | tf_op jit(solution)/shard_map/ppermute | solution.py:64
  69.7 12.6 %copy-start.6 = (bf16[256,1024]{1,0:T(8,128)(2,1)}, bf16[256,1024]{1,0:T(8,128)(2,1)S(1)}, u32[]{:S(2)}) copy-start(bf16[256,1024]{1,0:T(8,128)(2,1)S(1)} %broadcast_select_fusion.1.refs_8_) | copy-start | bytes 1572868
  69.7 16.8 %collective-permute-start.17 = (bf16[256,1024]{1,0:T(8,128)(2,1)S(1)}, bf16[256,1024]{1,0:T(8,128)(2,1)S(1)}, u32[]{:S(2)}, u32[]{:S(2)}) collective-permute-start(bf16[256,1024]{1,0:T(8,128)(2,1)S(1)} %broadcast_select_fusion.10), channel_id=1, source_target_pairs={{4,0},{8,12},{5,1},{9,13},{6,2},{10,14},{7,3},{11,15},{20,16},{24,... | collective-permute-start | bytes 1572872 | tf_op jit(solution)/shard_map/ppermute | solution.py:68
  74.0 14.9 %collective-permute-start.20 = (bf16[256,1024]{1,0:T(8,128)(2,1)S(1)}, bf16[256,1024]{1,0:T(8,128)(2,1)S(1)}, u32[]{:S(2)}, u32[]{:S(2)}) collective-permute-start(bf16[256,1024]{1,0:T(8,128)(2,1)S(1)} %broadcast_select_fusion.1.refs_8_), channel_id=1, source_target_pairs={{0,16},{16,0},{1,17},{17,1},{2,18},{18,2},{3,19},{19,3},{4,20},{20... | collective-permute-start | bytes 1572872 | tf_op jit(solution)/shard_map/ppermute | solution.py:64
  80.8 17.4 %collective-permute-start.14 = (f32[768,256]{1,0:T(8,128)S(1)}, f32[768,256]{1,0:T(8,128)S(1)}, u32[]{:S(2)}, u32[]{:S(2)}) collective-permute-start(f32[768,256]{1,0:T(8,128)S(1)} %fusion.4), channel_id=1, source_target_pairs={{0,2},{2,0},{1,3},{3,1},{4,6},{6,4},{5,7},{7,5},{8,10},{10,8},{9,1... | collective-permute-start | bytes 2359304 | tf_op jit(solution)/shard_map/ppermute | solution.py:64
  86.5 12.9 %collective-permute-start.23 = (bf16[256,1024]{1,0:T(8,128)(2,1)S(1)}, bf16[256,1024]{1,0:T(8,128)(2,1)S(1)}, u32[]{:S(2)}, u32[]{:S(2)}) collective-permute-start(bf16[256,1024]{1,0:T(8,128)(2,1)S(1)} %broadcast_select_fusion.9), channel_id=1, source_target_pairs={{4,0},{8,12},{5,1},{9,13},{6,2},{10,14},{7,3},{11,15},{20,16},{24,... | collective-permute-start | bytes 1572872 | tf_op jit(solution)/shard_map/ppermute | solution.py:68
  88.8 5.7 %copy-start.3 = (bf16[256,1024]{1,0:T(8,128)(2,1)}, bf16[256,1024]{1,0:T(8,128)(2,1)S(1)}, u32[]{:S(2)}) copy-start(bf16[256,1024]{1,0:T(8,128)(2,1)S(1)} %get-tuple-element.86.refs_1_) | copy-start | bytes 1572868
  88.8 4.2 %copy-start.16 = (bf16[256,1024]{1,0:T(8,128)(2,1)}, bf16[256,1024]{1,0:T(8,128)(2,1)S(1)}, u32[]{:S(2)}) copy-start(bf16[256,1024]{1,0:T(8,128)(2,1)S(1)} %collective-permute-done.20.refs_9_) | copy-start | bytes 1572868
  88.8 11.8 %collective-permute-start.22 = (bf16[256,1024]{1,0:T(8,128)(2,1)S(1)}, bf16[256,1024]{1,0:T(8,128)(2,1)S(1)}, u32[]{:S(2)}, u32[]{:S(2)}) collective-permute-start(bf16[256,1024]{1,0:T(8,128)(2,1)S(1)} %get-tuple-element.86.refs_1_), channel_id=1, source_target_pairs={{0,16},{16,0},{1,17},{17,1},{2,18},{18,2},{3,19},{19,3},{4,20},{20... | collective-permute-start | bytes 1572872 | tf_op jit(solution)/shard_map/ppermute | solution.py:64
  98.2 4.1 %copy-start.23 = (f32[768,256]{1,0:T(8,128)}, f32[768,256]{1,0:T(8,128)S(1)}, u32[]{:S(2)}) copy-start(f32[768,256]{1,0:T(8,128)S(1)} %collective-permute-done.14) | copy-start | bytes 2359300
  98.2 4.1 %copy-start.8 = (bf16[768,1024]{1,0:T(8,128)(2,1)}, bf16[768,1024]{1,0:T(8,128)(2,1)S(1)}, u32[]{:S(2)}) copy-start(bf16[768,1024]{1,0:T(8,128)(2,1)S(1)} %collective-permute-done.19.refs_3_) | copy-start | bytes 4718596
  98.2 4.1 %copy-start.9 = (bf16[768,1024]{1,0:T(8,128)(2,1)}, bf16[768,1024]{1,0:T(8,128)(2,1)S(1)}, u32[]{:S(2)}) copy-start(bf16[768,1024]{1,0:T(8,128)(2,1)S(1)} %collective-permute-done.18.refs_1_) | copy-start | bytes 4718596
  99.4 16.0 %collective-permute-start.21 = (f32[768,256]{1,0:T(8,128)}, f32[768,256]{1,0:T(8,128)}, u32[]{:S(2)}, u32[]{:S(2)}) collective-permute-start(f32[768,256]{1,0:T(8,128)} %fusion.3), channel_id=1, source_target_pairs={{0,2},{2,0},{1,3},{3,1},{4,6},{6,4},{5,7},{7,5},{8,10},{10,8},{9,1... | collective-permute-start | bytes 2359304 | tf_op jit(solution)/shard_map/ppermute | solution.py:64
  100.6 10.1 %copy-start.5 = (bf16[256,1024]{1,0:T(8,128)(2,1)}, bf16[256,1024]{1,0:T(8,128)(2,1)S(1)}, u32[]{:S(2)}) copy-start(bf16[256,1024]{1,0:T(8,128)(2,1)S(1)} %select_select_fusion.refs_0_.refs_2_.refs_11_) | copy-start | bytes 1572868
  100.6 12.8 %collective-permute-start.24 = (bf16[256,1024]{1,0:T(8,128)(2,1)S(1)}, bf16[256,1024]{1,0:T(8,128)(2,1)S(1)}, u32[]{:S(2)}, u32[]{:S(2)}) collective-permute-start(bf16[256,1024]{1,0:T(8,128)(2,1)S(1)} %select_select_fusion.refs_0_.refs_2_.refs_11_), channel_id=1, source_target_pairs={{0,16},{16,0},{1,17},{17,1},{2,18},{18,2},{3,19},{19,3},{4,20},{20... | collective-permute-start | bytes 1572872 | tf_op jit(solution)/shard_map/ppermute | solution.py:64
  102.3 8.4 %copy-start.11 = (bf16[256,1024]{1,0:T(8,128)(2,1)S(1)}, bf16[256,1024]{1,0:T(8,128)(2,1)}, u32[]{:S(2)}) copy-start(bf16[256,1024]{1,0:T(8,128)(2,1)} %copy-done.10) | copy-start | bytes 1572868
  102.3 8.4 %copy-start.13 = (bf16[256,1024]{1,0:T(8,128)(2,1)S(1)}, bf16[256,1024]{1,0:T(8,128)(2,1)}, u32[]{:S(2)}) copy-start(bf16[256,1024]{1,0:T(8,128)(2,1)} %copy-done.12) | copy-start | bytes 1572868
  115.4 9.8 %collective-permute-start.25 = (f32[768,1024]{1,0:T(8,128)}, f32[768,1024]{1,0:T(8,128)}, u32[]{:S(2)}, u32[]{:S(2)}) collective-permute-start(f32[768,1024]{1,0:T(8,128)} %shard_map.50), channel_id=1, source_target_pairs={{0,1},{1,0},{2,3},{3,2},{4,5},{5,4},{6,7},{7,6},{8,9},{9,8},{10,11... | collective-permute-start | bytes 9437192 | tf_op jit(solution)/shard_map/ppermute | solution.py:64
  116.1 20.2 %collective-permute-start.27 = (f32[768,256]{1,0:T(8,128)}, f32[768,256]{1,0:T(8,128)S(1)}, u32[]{:S(2)}, u32[]{:S(2)}) collective-permute-start(f32[768,256]{1,0:T(8,128)} %fusion), channel_id=1, source_target_pairs={{0,2},{2,0},{1,3},{3,1},{4,6},{6,4},{5,7},{7,5},{8,10},{10,8},{9,1... | collective-permute-start | bytes 2359304 | tf_op jit(solution)/shard_map/ppermute | solution.py:64
  116.7 6.2 %copy-start.17 = (f32[768,256]{1,0:T(8,128)S(1)}, f32[768,256]{1,0:T(8,128)}, u32[]{:S(2)}) copy-start(f32[768,256]{1,0:T(8,128)} %fusion.2) | copy-start | bytes 2359300
  116.7 6.2 %copy-start.22 = (f32[768,256]{1,0:T(8,128)S(1)}, f32[768,256]{1,0:T(8,128)}, u32[]{:S(2)}) copy-start(f32[768,256]{1,0:T(8,128)} %copy-done.21) | copy-start | bytes 2359300
  124.2 9.8 %collective-permute-start.26 = (bf16[768,256]{1,0:T(8,128)(2,1)S(1)}, bf16[768,256]{1,0:T(8,128)(2,1)S(1)}, u32[]{:S(2)}, u32[]{:S(2)}) collective-permute-start(bf16[768,256]{1,0:T(8,128)(2,1)S(1)} %get-tuple-element.106), channel_id=1, source_target_pairs={{0,1},{1,0},{2,3},{3,2},{4,5},{5,4},{6,7},{7,6},{8,9},{9,8},{10,11... | collective-permute-start | bytes 1179656 | tf_op jit(solution)/shard_map/ppermute | solution.py:64
  125.2 11.0 %copy-start.25 = (f32[768,256]{1,0:T(8,128)S(1)}, f32[768,256]{1,0:T(8,128)}, u32[]{:S(2)}) copy-start(f32[768,256]{1,0:T(8,128)} %get-tuple-element.102) | copy-start | bytes 2359300
  136.4 1.8 %collective-permute-start.28 = (bf16[768,256]{1,0:T(8,128)(2,1)S(1)}, bf16[768,256]{1,0:T(8,128)(2,1)S(1)}, u32[]{:S(2)}, u32[]{:S(2)}) collective-permute-start(bf16[768,256]{1,0:T(8,128)(2,1)S(1)} %get-tuple-element.104), channel_id=1, source_target_pairs={{0,1},{1,0},{2,3},{3,2},{4,5},{5,4},{6,7},{7,6},{8,9},{9,8},{10,11... | collective-permute-start | bytes 1179656 | tf_op jit(solution)/shard_map/ppermute | solution.py:64
  (7 other events, 13.1 us)

commit v4 on v3

--- a/solution.py
+++ b/solution.py
@@ -155,7 +155,7 @@
             dimension_semantics=("arbitrary",), vmem_limit_bytes=60 * 1024 * 1024
         ),
         cost_estimate=pl.CostEstimate(flops=1000, bytes_accessed=1000, transcendentals=0),
-    )(jnp.stack(numbers).astype(jnp.int32), *heads, *base, *pieces)
+    )(numbers, *heads, *base, *pieces)
 
 
 INWARD = [(0, 1), (3, 2)]
@@ -181,6 +181,19 @@
     def sums(early_pieces, late_pieces):
         slot_0, slot_1 = (pick(early, e, l) for e, l in zip(early_pieces, late_pieces))
         return times_rows(grad_0, slot_0) + times_rows(grad_1, slot_1)
+
+    low = plane < 2
+    near, far, far_next = plane ^ 1, pick(low, 2, 1), pick(low, 3, 0)
+
+    def numbers_of(rows):
+        numbers = [core]
+        for row in rows:
+            slot = 2 * (row // 2 != chip) + ((row & 1) != core)
+            numbers += [slot, group, slot, 1 - group]
+        return jnp.stack(numbers).astype(jnp.int32)
+
+    numbers_1 = numbers_of([plane, near, pick(early, far, far_next), pick(early, far_next, far)])
+    numbers_0 = numbers_of([plane, pick(early, near, far), pick(early, far, far_next), pick(early, far_next, near)])
 
     mine_0 = weight_rows(weight, core, group)
     middle_0 = send(mine_0, MIDDLE)
@@ -210,7 +223,7 @@
 
     there = swap(after(due_1, head_y), "b")
     due = sums((other_0, other_1), (x_2, x_3))
-    first, due = lax.optimization_barrier((there, due))
+    first, due, numbers_0, numbers_1 = lax.optimization_barrier((there, due, numbers_0, numbers_1))
     there = swap(due, "b")
     mid_5 = pick(early, cross_1, after(cross_0, at_3))
     out_5 = send(after(mid_5, out_4), OUTWARD)
@@ -234,25 +247,14 @@
 
     head_all = [heads, head_1, head_y, head_3]
 
-    def forward(rows, pieces, base=(), dtype=jnp.float32):
-        numbers = [core]
-        for row in rows:
-            slot = 2 * (row // 2 != chip) + ((row & 1) != core)
-            numbers += [slot, group, slot, 1 - group]
-        return forward_sum(numbers, head_all, list(base), pieces, dtype)
-
-    low = plane < 2
-    near, far, far_next = plane ^ 1, pick(low, 2, 1), pick(low, 3, 0)
-    rows_1 = [plane, near, pick(early, far, far_next), pick(early, far_next, far)]
-    rows_0 = [plane, pick(early, near, far), pick(early, far, far_next), pick(early, far_next, near)]
     pieces_1 = [mine_1, other_1, near_1, x_1, at_4, x_4, pick(early, at_5, at_3), pick(early, x_5, x_3)]
     pieces_0 = [mine_0, other_0, at_2, x_2, pick(early, at_3, at_5), pick(early, x_3, x_5), at_6]
-    total_1 = forward(rows_1, pieces_1)
+    total_1 = forward_sum(numbers_1, head_all, [], pieces_1, jnp.float32)
     due = sums((x_2, x_1), (x_5, x_4))
     third, due, total_1, x_6 = lax.optimization_barrier((there, due, total_1, x_6))
     there = swap(due, "b")
     other_part = swap(total_1, "k")
-    projected = forward(rows_0, pieces_0 + [x_6], [other_part], jnp.bfloat16)
+    projected = forward_sum(numbers_0, head_all, [other_part], pieces_0 + [x_6], jnp.bfloat16)
 
     done = [(k + t).astype(jnp.bfloat16) for k, t in ((kept_1, first), (kept_2, second))]
     last, kept = keep(

time: 141 us -> 140 us (level)
  waiting for transfers between devices: 49 us -> 47.4 us
  transfers between devices with their start and end apart: 29 -> 29, of which waited for: 14 -> 14; matrix products, arithmetic and copies ran while one was open for 21% -> 22% of each run, Pallas kernels for 17% -> 17%
where the time goes in v4:
time: 140 us; the launch traced here: 139 us
  waiting for transfers between devices  47.4 us (34%)
  starting transfers between devices  31.3 us (22%)
  Pallas kernels  23.2 us (17%)
  matrix products  15.1 us (11%)
  other arithmetic  12.2 us (9%)
  local copies, waits for them, and re-layouts  8.33 us (6%)
    ppermute x10, waiting for transfers between devices, send(): return lax.ppermute(value, 'a', pairs)  31.8 us
    pallas_call x2, Pallas kernels, forward_sum(): pl.pallas_call(functools.partial(sum_of_products, len(base)), grid_spec=s...  17.1 us
    ppermute x10, starting transfers between devices, send(): return lax.ppermute(value, 'a', pairs)  16.9 us
    ppermute x19, waiting for transfers between devices, swap(): return lax.ppermute(value, axis, [(0, 1), (1, 0)])  15.6 us
    dot_general x12, matrix products, times_rows(): lax.dot_general(left, right, (((1,), (1,)), ((), ())), preferred_element_...  15.1 us
    ppermute x19, starting transfers between devices, swap(): return lax.ppermute(value, axis, [(0, 1), (1, 0)])  14.4 us
    select_n x15, other arithmetic, pick(): return jnp.where(flag, yes, no)  12 us
    pallas_call x1, Pallas kernels, keep(): pl.pallas_call(kept_sums, grid=(tokens // tile,), in_specs=[pl.BlockSpec(...  6.15 us
  transfers between devices with their start and end apart: 29, of which 14 were waited for; matrix products, arithmetic and copies ran while one was open for 22% of the time, Pallas kernels for 17%

profile of v4, /device:TPU:0, one launch (start us, length us, event | category | flops | bytes accessed | tf_op | source)
XLA Modules:
  0.0 138.7 jit_solution(6516877278007347913)
XLA Ops:
  0.7 2.0 %dynamic-slice_bitcast_fusion.refs_5_ = bf16[256,1024]{1,0:T(8,128)(2,1)} fusion(bf16[1,1024,1024]{2,1,0:T(8,128)(2,1)} %param.5, s32[]{:T(128)S(6)} %select_n.205), kind=kLoop, calls=%fused_computation.34 | loop fusion | bytes 1048580 | tf_op jit(solution)/shard_map/dynamic_slice | solution.py:179
  2.7 1.1 constant_dynamic-slice_fusion.2
  4.3 1.5 %collective-permute-start = (bf16[256,1024]{1,0:T(8,128)(2,1)}, bf16[256,1024]{1,0:T(8,128)(2,1)}, u32[]{:S(2)}, u32[]{:S(2)}) collective-permute-start(bf16[256,1024]{1,0:T(8,128)(2,1)} %dynamic-slice_bitcast_fusion.refs_5_), channel_id=1, source_target_pairs={{4,8},{8,4},{5,9},{9,5},{6,10},{10,6},{7,11},{11,7},{20,24},{24,20... | collective-permute-start | bytes 1572872 | tf_op jit(solution)/shard_map/ppermute | solution.py:68
  5.9 4.5 %collective-permute-start.2 = (bf16[256,1024]{1,0:T(8,128)(2,1)}, bf16[256,1024]{1,0:T(8,128)(2,1)}, u32[]{:S(2)}, u32[]{:S(2)}) collective-permute-start(bf16[256,1024]{1,0:T(8,128)(2,1)} %collective-permute-done.1.refs_4_), channel_id=1, source_target_pairs={{0,4},{12,8},{4,0},{8,12},{1,5},{13,9},{5,1},{9,13},{2,6},{14,10},... | collective-permute-start | bytes 1572872 | tf_op jit(solution)/shard_map/ppermute | solution.py:68
  10.4 1.5 %collective-permute-start.9 = (bf16[768,1024]{1,0:T(8,128)(2,1)}, bf16[768,1024]{1,0:T(8,128)(2,1)}, u32[]{:S(2)}, u32[]{:S(2)}) collective-permute-start(bf16[768,1024]{1,0:T(8,128)(2,1)} %bitcast.58), channel_id=1, source_target_pairs={{0,2},{2,0},{1,3},{3,1},{4,6},{6,4},{5,7},{7,5},{8,10},{10,8},{9,1... | collective-permute-start | bytes 4718600 | tf_op jit(solution)/shard_map/ppermute | solution.py:64
  12.0 11.1 %collective-permute-done.2.refs_6_.refs_3_ = bf16[256,1024]{1,0:T(8,128)(2,1)} collective-permute-done((bf16[256,1024]{1,0:T(8,128)(2,1)}, bf16[256,1024]{1,0:T(8,128)(2,1)}, u32[]{:S(2)}, u32[]{:S(2)}) %collective-permute-start.2) | collective-permute-done | bytes 524320 | tf_op jit(solution)/shard_map/ppermute | solution.py:68
  23.0 1.5 %collective-permute-start.4 = (bf16[256,1024]{1,0:T(8,128)(2,1)}, bf16[256,1024]{1,0:T(8,128)(2,1)}, u32[]{:S(2)}, u32[]{:S(2)}) collective-permute-start(bf16[256,1024]{1,0:T(8,128)(2,1)} %collective-permute-done.1.refs_4_), channel_id=1, source_target_pairs={{4,8},{8,4},{5,9},{9,5},{6,10},{10,6},{7,11},{11,7},{20,24},{24,20... | collective-permute-start | bytes 1572872 | tf_op jit(solution)/shard_map/ppermute | solution.py:68
  24.5 2.0 %broadcast_select_fusion.4 = bf16[256,1024]{1,0:T(8,128)(2,1)} fusion(bf16[256,1024]{1,0:T(8,128)(2,1)} %collective-permute-done, pred[]{:T(512)S(6)} %and.55, bf16[1,1024,1024]{2,1,0:T(8,128)(2,1)} %param.5, s32[]{:T(128)S(6)} %select_n.205), kind=kLoop, calls=%fused_computation.39 | loop fusion | flops 262144 | bytes 1572869 | tf_op jit(solution)/shard_map/jit(_where)/select_n | solution.py:76
  26.5 2.8 %collective-permute-start.3 = (bf16[256,1024]{1,0:T(8,128)(2,1)}, bf16[256,1024]{1,0:T(8,128)(2,1)}, u32[]{:S(2)}, u32[]{:S(2)}) collective-permute-start(bf16[256,1024]{1,0:T(8,128)(2,1)} %broadcast_select_fusion.4), channel_id=1, source_target_pairs={{0,4},{12,8},{4,0},{8,12},{1,5},{13,9},{5,1},{9,13},{2,6},{14,10},... | collective-permute-start | bytes 1572872 | tf_op jit(solution)/shard_map/ppermute | solution.py:68
  29.4 1.5 %collective-permute-start.5 = (bf16[256,1024]{1,0:T(8,128)(2,1)}, bf16[256,1024]{1,0:T(8,128)(2,1)}, u32[]{:S(2)}, u32[]{:S(2)}) collective-permute-start(bf16[256,1024]{1,0:T(8,128)(2,1)} %collective-permute-done.2.refs_6_.refs_3_), channel_id=1, source_target_pairs={{0,16},{16,0},{1,17},{17,1},{2,18},{18,2},{3,19},{19,3},{4,20},{20... | collective-permute-start | bytes 1572872 | tf_op jit(solution)/shard_map/ppermute | solution.py:64
  32.9 1.1 broadcast_select_fusion.12
  34.0 7.0 %collective-permute-done.3 = bf16[256,1024]{1,0:T(8,128)(2,1)} collective-permute-done((bf16[256,1024]{1,0:T(8,128)(2,1)}, bf16[256,1024]{1,0:T(8,128)(2,1)}, u32[]{:S(2)}, u32[]{:S(2)}) %collective-permute-start.3) | collective-permute-done | bytes 524320 | tf_op jit(solution)/shard_map/ppermute | solution.py:68
  40.9 1.5 %collective-permute-done.5.refs_7_ = bf16[256,1024]{1,0:T(8,128)(2,1)} collective-permute-done((bf16[256,1024]{1,0:T(8,128)(2,1)}, bf16[256,1024]{1,0:T(8,128)(2,1)}, u32[]{:S(2)}, u32[]{:S(2)}) %collective-permute-start.5) | collective-permute-done | bytes 524320 | tf_op jit(solution)/shard_map/ppermute | solution.py:64
  42.4 1.3 collective-permute-start.6
  43.7 1.3 constant_dynamic-slice_fusion
  45.0 1.2 broadcast_select_fusion.3.refs_7_
  46.3 1.6 %collective-permute-start.12 = (bf16[256,1024]{1,0:T(8,128)(2,1)S(1)}, bf16[256,1024]{1,0:T(8,128)(2,1)S(1)}, u32[]{:S(2)}, u32[]{:S(2)}) collective-permute-start(bf16[256,1024]{1,0:T(8,128)(2,1)S(1)} %broadcast_select_fusion.3.refs_7_), channel_id=1, source_target_pairs={{0,16},{16,0},{1,17},{17,1},{2,18},{18,2},{3,19},{19,3},{4,20},{20... | collective-permute-start | bytes 1572872 | tf_op jit(solution)/shard_map/ppermute | solution.py:64
  48.0 8.1 %collective-permute-done.6 = bf16[256,1024]{1,0:T(8,128)(2,1)S(1)} collective-permute-done((bf16[256,1024]{1,0:T(8,128)(2,1)S(1)}, bf16[256,1024]{1,0:T(8,128)(2,1)S(1)}, u32[]{:S(2)}, u32[]{:S(2)}) %collective-permute-start.6) | collective-permute-done | bytes 524320 | tf_op jit(solution)/shard_map/ppermute | solution.py:68
  56.8 1.3 collective-permute-start.16
  59.4 1.2 collective-permute-done.12.refs_8_
  60.6 1.5 %collective-permute-start.13 = (bf16[256,1024]{1,0:T(8,128)(2,1)S(1)}, bf16[256,1024]{1,0:T(8,128)(2,1)S(1)}, u32[]{:S(2)}, u32[]{:S(2)}) collective-permute-start(bf16[256,1024]{1,0:T(8,128)(2,1)S(1)} %broadcast_select_fusion.2), channel_id=1, source_target_pairs={{0,16},{16,0},{1,17},{17,1},{2,18},{18,2},{3,19},{19,3},{4,20},{20... | collective-permute-start | bytes 1572872 | tf_op jit(solution)/shard_map/ppermute | solution.py:64
  62.1 2.5 %collective-permute-start.11 = (f32[768,256]{1,0:T(8,128)S(1)}, f32[768,256]{1,0:T(8,128)S(1)}, u32[]{:S(2)}, u32[]{:S(2)}) collective-permute-start(f32[768,256]{1,0:T(8,128)S(1)} %fusion.5), channel_id=1, source_target_pairs={{0,2},{2,0},{1,3},{3,1},{4,6},{6,4},{5,7},{7,5},{8,10},{10,8},{9,1... | collective-permute-start | bytes 2359304 | tf_op jit(solution)/shard_map/ppermute | solution.py:64
  65.1 4.5 %collective-permute-done.16 = bf16[256,1024]{1,0:T(8,128)(2,1)S(1)} collective-permute-done((bf16[256,1024]{1,0:T(8,128)(2,1)S(1)}, bf16[256,1024]{1,0:T(8,128)(2,1)S(1)}, u32[]{:S(2)}, u32[]{:S(2)}) %collective-permute-start.16) | collective-permute-done | bytes 524320 | tf_op jit(solution)/shard_map/ppermute | solution.py:68
  69.7 1.3 collective-permute-start.17
  71.0 3.0 %collective-permute-done.13 = bf16[256,1024]{1,0:T(8,128)(2,1)S(1)} collective-permute-done((bf16[256,1024]{1,0:T(8,128)(2,1)S(1)}, bf16[256,1024]{1,0:T(8,128)(2,1)S(1)}, u32[]{:S(2)}, u32[]{:S(2)}) %collective-permute-start.13) | collective-permute-done | bytes 524320 | tf_op jit(solution)/shard_map/ppermute | solution.py:64
  74.0 1.5 %collective-permute-start.20 = (bf16[256,1024]{1,0:T(8,128)(2,1)S(1)}, bf16[256,1024]{1,0:T(8,128)(2,1)S(1)}, u32[]{:S(2)}, u32[]{:S(2)}) collective-permute-start(bf16[256,1024]{1,0:T(8,128)(2,1)S(1)} %broadcast_select_fusion.1.refs_8_), channel_id=1, source_target_pairs={{0,16},{16,0},{1,17},{17,1},{2,18},{18,2},{3,19},{19,3},{4,20},{20... | collective-permute-start | bytes 1572872 | tf_op jit(solution)/shard_map/ppermute | solution.py:64
  76.1 1.1 broadcast_select_fusion.9
  78.4 2.4 %collective-permute-done.11 = f32[768,256]{1,0:T(8,128)S(1)} collective-permute-done((f32[768,256]{1,0:T(8,128)S(1)}, f32[768,256]{1,0:T(8,128)S(1)}, u32[]{:S(2)}, u32[]{:S(2)}) %collective-permute-start.11) | collective-permute-done | bytes 786464 | tf_op jit(solution)/shard_map/ppermute | solution.py:64
  80.8 1.4 %collective-permute-start.14 = (f32[768,256]{1,0:T(8,128)S(1)}, f32[768,256]{1,0:T(8,128)S(1)}, u32[]{:S(2)}, u32[]{:S(2)}) collective-permute-start(f32[768,256]{1,0:T(8,128)S(1)} %fusion.4), channel_id=1, source_target_pairs={{0,2},{2,0},{1,3},{3,1},{4,6},{6,4},{5,7},{7,5},{8,10},{10,8},{9,1... | collective-permute-start | bytes 2359304 | tf_op jit(solution)/shard_map/ppermute | solution.py:64
  82.2 1.7 %fusion.12 = f32[256,768]{0,1:T(8,128)S(1)} fusion(bf16[768,1024]{1,0:T(8,128)(2,1)S(1)} %collective-permute-done.10.grad_1, bf16[256,1024]{1,0:T(8,128)(2,1)S(1)} %broadcast_select_fusion.1.refs_8_, bf16[256,1024]{1,0:T(8,128)(2,1)} %collective-permute-done.1.refs_4_, pred[]{:T(512)S(6)} %ne.91), kind=kOutput, calls=%fused_computation.22 | convolution fusion | flops 402915328 | bytes 3407873 | tf_op jit(solution)/shard_map/dot_general | solution.py:84
  83.9 2.5 %fusion.2 = f32[768,256]{1,0:T(8,128)} fusion(f32[256,768]{0,1:T(8,128)S(1)} %fusion.12, bf16[256,1024]{1,0:T(8,128)(2,1)S(1)} %broadcast_select_fusion.2, bf16[256,1024]{1,0:T(8,128)(2,1)} %dynamic-slice_bitcast_fusion.refs_5_, pred[]{:T(512)S(6)} %ne.91, bf16[1,768,1024]{2,1,0:T(8,128)(2,1)S(1)} %copy-done), kind=kOutput, calls=%fused_computation.5 | convolution fusion | flops 403111936 | bytes 4194305 | tf_op jit(solution)/shard_map/dot_general | solution.py:84
  86.5 1.5 %collective-permute-start.23 = (bf16[256,1024]{1,0:T(8,128)(2,1)S(1)}, bf16[256,1024]{1,0:T(8,128)(2,1)S(1)}, u32[]{:S(2)}, u32[]{:S(2)}) collective-permute-start(bf16[256,1024]{1,0:T(8,128)(2,1)S(1)} %broadcast_select_fusion.9), channel_id=1, source_target_pairs={{4,0},{8,12},{5,1},{9,13},{6,2},{10,14},{7,3},{11,15},{20,16},{24,... | collective-permute-start | bytes 1572872 | tf_op jit(solution)/shard_map/ppermute | solution.py:68
  90.0 1.5 %fusion.3 = f32[768,256]{1,0:T(8,128)} fusion(f32[256,768]{0,1:T(8,128)S(1)} %fusion.15, bf16[256,1024]{1,0:T(8,128)(2,1)S(1)} %broadcast_select_fusion.3.refs_7_, bf16[256,1024]{1,0:T(8,128)(2,1)S(1)} %get-tuple-element.88.refs_1_, pred[]{:T(512)S(6)} %ne.91, bf16[1,768,1024]{2,1,0:T(8,128)(2,1)S(1)} %copy-done), kind=kOutput, calls=%fused_computation.7 | convolution fusion | flops 403111936 | bytes 4194305 | tf_op jit(solution)/shard_map/dot_general | solution.py:84
  91.5 1.5 %fusion.1 = f32[768,256]{1,0:T(8,128)} fusion(f32[256,768]{0,1:T(8,128)S(1)} %fusion.9, bf16[256,1024]{1,0:T(8,128)(2,1)S(1)} %collective-permute-done.13, bf16[256,1024]{1,0:T(8,128)(2,1)S(1)} %get-tuple-element.115.refs_6_, pred[]{:T(512)S(6)} %ne.91, bf16[1,768,1024]{2,1,0:T(8,128)(2,1)S(1)} %copy-done), kind=kOutput, calls=%fused_computation.3 | convolution fusion | flops 403111936 | bytes 4194305 | tf_op jit(solution)/shard_map/dot_general | solution.py:84
  93.0 1.5 %fusion.6 = f32[256,768]{0,1:T(8,128)} fusion(bf16[768,1024]{1,0:T(8,128)(2,1)S(1)} %collective-permute-done.10.grad_1, bf16[256,1024]{1,0:T(8,128)(2,1)} %collective-permute-done.5.refs_7_, bf16[256,1024]{1,0:T(8,128)(2,1)S(1)} %collective-permute-done.20.refs_9_, pred[]{:T(512)S(6)} %ne.91), kind=kOutput, calls=%fused_computation.16 | convolution fusion | flops 402915328 | bytes 3407873 | tf_op jit(solution)/shard_map/dot_general | solution.py:84
  95.4 2.8 %collective-permute-done.14 = f32[768,256]{1,0:T(8,128)S(1)} collective-permute-done((f32[768,256]{1,0:T(8,128)S(1)}, f32[768,256]{1,0:T(8,128)S(1)}, u32[]{:S(2)}, u32[]{:S(2)}) %collective-permute-start.14) | collective-permute-done | bytes 786464 | tf_op jit(solution)/shard_map/ppermute | solution.py:64
  98.2 1.2 collective-permute-done.23
  99.4 1.2 select_select_fusion.refs_0_.refs_2_.refs_11_
  101.5 1.1 broadcast_select_fusion.5
  102.6 8.4 %shard_map.50 = f32[768,1024]{1,0:T(8,128)} custom-call(s32[17]{0:T(128)} %stack.32.numbers, bf16[768,1024]{1,0:T(8,128)(2,1)} %bitcast.59, bf16[768,1024]{1,0:T(8,128)(2,1)} %copy-done.9, bf16[768,1024]{1,0:T(8,128)(2,1)} %collective-permute-done.9.refs_2_, bf16[768,1024]{1,0:T(8,128)(2,1)} %copy-done.8, bf16[256,1024]{1,0:T(8,128)(2,1)} %collective-permute-done.1.refs_4_, ...), custom_call_target="tpu_custom_call" | custom-call | flops 1000 | bytes 1000 | tf_op jit(solution)/shard_map/pallas_call | solution.py:150
  111.0 2.6 %fusion = f32[768,256]{1,0:T(8,128)} fusion(f32[256,768]{0,1:T(8,128)} %fusion.6, bf16[256,1024]{1,0:T(8,128)(2,1)S(1)} %collective-permute-done.12.refs_8_, bf16[256,1024]{1,0:T(8,128)(2,1)S(1)} %copy-done.12, pred[]{:T(512)S(6)} %ne.91, bf16[1,768,1024]{2,1,0:T(8,128)(2,1)S(1)} %copy-done), kind=kOutput, calls=%fused_computation.1 | convolution fusion | flops 403111936 | bytes 4194305 | tf_op jit(solution)/shard_map/dot_general | solution.py:84
  113.6 1.7 %collective-permute-done.21.there = f32[768,256]{1,0:T(8,128)} collective-permute-done((f32[768,256]{1,0:T(8,128)}, f32[768,256]{1,0:T(8,128)}, u32[]{:S(2)}, u32[]{:S(2)}) %collective-permute-start.21) | collective-permute-done | bytes 786464 | tf_op jit(solution)/shard_map/ppermute | solution.py:64
  116.0 6.2 %shard_map.51 = (bf16[768,256]{1,0:T(8,128)(2,1)}, f32[768,256]{1,0:T(8,128)}) custom-call(s32[1]{0:T(128)} %bitcast.18.flags, bf16[768,1024]{1,0:T(8,128)(2,1)} %bitcast.56, bf16[768,1024]{1,0:T(8,128)(2,1)} %copy-done.1, f32[768,256]{1,0:T(8,128)} %collective-permute-done.21.there, bf16[256,1024]{1,0:T(8,128)(2,1)} %copy-done.5, ...), custom_call_target="tpu_custom_call" | custom-call | flops 1000 | bytes 1000 | tf_op jit(solution)/shard_map/pallas_call | solution.py:122
  122.2 2.0 %broadcast_select_fusion.14 = (bf16[768,256]{1,0:T(8,128)(2,1)}, bf16[768,256]{1,0:T(8,128)(2,1)S(1)}) fusion(bf16[768,256]{1,0:T(8,128)(2,1)} %get-tuple-element.97, pred[]{:T(512)S(6)} %eq.11, f32[768,256]{1,0:T(8,128)S(1)} %copy-done.16, f32[768,256]{1,0:T(8,128)S(1)} %copy-done.21), kind=kLoop, calls=%fused_computation.65 | loop fusion | flops 589824 | bytes 2752513 | tf_op jit(solution)/shard_map/jit(_where)/select_n | solution.py:76
  125.2 8.7 %shard_map.52 = bf16[768,1024]{1,0:T(8,128)(2,1)} custom-call(s32[17]{0:T(128)} %stack.29.numbers, bf16[768,1024]{1,0:T(8,128)(2,1)} %bitcast.60, bf16[768,1024]{1,0:T(8,128)(2,1)} %copy-done.9, bf16[768,1024]{1,0:T(8,128)(2,1)} %collective-permute-done.9.refs_2_, bf16[768,1024]{1,0:T(8,128)(2,1)} %copy-done.8, f32[768,1024]{1,0:T(8,128)} %collective-permute-done.25.refs_4_, ...), custom_call_target="tpu_custom_call" | custom-call | flops 1000 | bytes 1000 | tf_op jit(solution)/shard_map/pallas_call | solution.py:150
  134.0 1.6 %collective-permute-done.27 = f32[768,256]{1,0:T(8,128)S(1)} collective-permute-done((f32[768,256]{1,0:T(8,128)}, f32[768,256]{1,0:T(8,128)S(1)}, u32[]{:S(2)}, u32[]{:S(2)}) %collective-permute-start.27) | collective-permute-done | bytes 786464 | tf_op jit(solution)/shard_map/ppermute | solution.py:64
  136.2 1.3 collective-permute-done.28
  137.6 1.1 copy-done.18
  (101 shorter events, 13.4 us)
Async XLA Ops:
  0.6 9.8 %copy-start = (bf16[1,768,1024]{2,1,0:T(8,128)(2,1)S(1)}, bf16[1,768,1024]{2,1,0:T(8,128)(2,1)}, u32[]{:S(2)}) copy-start(bf16[1,768,1024]{2,1,0:T(8,128)(2,1)} %param.4) | copy-start | bytes 4718596
  3.8 2.2 %collective-permute-start.1 = (bf16[256,1024]{1,0:T(8,128)(2,1)S(1)}, bf16[256,1024]{1,0:T(8,128)(2,1)}, u32[]{:S(2)}, u32[]{:S(2)}) collective-permute-start(bf16[256,1024]{1,0:T(8,128)(2,1)S(1)} %constant_dynamic-slice_fusion.2), channel_id=1, source_target_pairs={{0,1},{1,0},{2,3},{3,2},{4,5},{5,4},{6,7},{7,6},{8,9},{9,8},{10,11... | collective-permute-start | bytes 1572872 | tf_op jit(solution)/shard_map/ppermute | solution.py:64
  4.3 7.7 %collective-permute-start = (bf16[256,1024]{1,0:T(8,128)(2,1)}, bf16[256,1024]{1,0:T(8,128)(2,1)}, u32[]{:S(2)}, u32[]{:S(2)}) collective-permute-start(bf16[256,1024]{1,0:T(8,128)(2,1)} %dynamic-slice_bitcast_fusion.refs_5_), channel_id=1, source_target_pairs={{4,8},{8,4},{5,9},{9,5},{6,10},{10,6},{7,11},{11,7},{20,24},{24,20... | collective-permute-start | bytes 1572872 | tf_op jit(solution)/shard_map/ppermute | solution.py:68
  5.9 17.1 %collective-permute-start.2 = (bf16[256,1024]{1,0:T(8,128)(2,1)}, bf16[256,1024]{1,0:T(8,128)(2,1)}, u32[]{:S(2)}, u32[]{:S(2)}) collective-permute-start(bf16[256,1024]{1,0:T(8,128)(2,1)} %collective-permute-done.1.refs_4_), channel_id=1, source_target_pairs={{0,4},{12,8},{4,0},{8,12},{1,5},{13,9},{5,1},{9,13},{2,6},{14,10},... | collective-permute-start | bytes 1572872 | tf_op jit(solution)/shard_map/ppermute | solution.py:68
  10.4 35.8 %collective-permute-start.10 = (bf16[768,1024]{1,0:T(8,128)(2,1)S(1)}, bf16[768,1024]{1,0:T(8,128)(2,1)S(1)}, u32[]{:S(2)}, u32[]{:S(2)}) collective-permute-start(bf16[768,1024]{1,0:T(8,128)(2,1)S(1)} %bitcast.57), channel_id=1, source_target_pairs={{0,1},{1,0},{2,3},{3,2},{4,5},{5,4},{6,7},{7,6},{8,9},{9,8},{10,11... | collective-permute-start | bytes 4718600 | tf_op jit(solution)/shard_map/ppermute | solution.py:64
  10.4 37.5 %collective-permute-start.9 = (bf16[768,1024]{1,0:T(8,128)(2,1)}, bf16[768,1024]{1,0:T(8,128)(2,1)}, u32[]{:S(2)}, u32[]{:S(2)}) collective-permute-start(bf16[768,1024]{1,0:T(8,128)(2,1)} %bitcast.58), channel_id=1, source_target_pairs={{0,2},{2,0},{1,3},{3,1},{4,6},{6,4},{5,7},{7,5},{8,10},{10,8},{9,1... | collective-permute-start | bytes 4718600 | tf_op jit(solution)/shard_map/ppermute | solution.py:64
  23.0 9.1 %collective-permute-start.4 = (bf16[256,1024]{1,0:T(8,128)(2,1)}, bf16[256,1024]{1,0:T(8,128)(2,1)}, u32[]{:S(2)}, u32[]{:S(2)}) collective-permute-start(bf16[256,1024]{1,0:T(8,128)(2,1)} %collective-permute-done.1.refs_4_), channel_id=1, source_target_pairs={{4,8},{8,4},{5,9},{9,5},{6,10},{10,6},{7,11},{11,7},{20,24},{24,20... | collective-permute-start | bytes 1572872 | tf_op jit(solution)/shard_map/ppermute | solution.py:68
  26.5 14.4 %collective-permute-start.3 = (bf16[256,1024]{1,0:T(8,128)(2,1)}, bf16[256,1024]{1,0:T(8,128)(2,1)}, u32[]{:S(2)}, u32[]{:S(2)}) collective-permute-start(bf16[256,1024]{1,0:T(8,128)(2,1)} %broadcast_select_fusion.4), channel_id=1, source_target_pairs={{0,4},{12,8},{4,0},{8,12},{1,5},{13,9},{5,1},{9,13},{2,6},{14,10},... | collective-permute-start | bytes 1572872 | tf_op jit(solution)/shard_map/ppermute | solution.py:68
  29.4 13.0 %collective-permute-start.5 = (bf16[256,1024]{1,0:T(8,128)(2,1)}, bf16[256,1024]{1,0:T(8,128)(2,1)}, u32[]{:S(2)}, u32[]{:S(2)}) collective-permute-start(bf16[256,1024]{1,0:T(8,128)(2,1)} %collective-permute-done.2.refs_6_.refs_3_), channel_id=1, source_target_pairs={{0,16},{16,0},{1,17},{17,1},{2,18},{18,2},{3,19},{19,3},{4,20},{20... | collective-permute-start | bytes 1572872 | tf_op jit(solution)/shard_map/ppermute | solution.py:64
  32.2 15.7 %collective-permute-start.8 = (bf16[256,1024]{1,0:T(8,128)(2,1)}, bf16[256,1024]{1,0:T(8,128)(2,1)S(1)}, u32[]{:S(2)}, u32[]{:S(2)}) collective-permute-start(bf16[256,1024]{1,0:T(8,128)(2,1)} %collective-permute-done.2.refs_6_.refs_3_), channel_id=1, source_target_pairs={{4,8},{8,4},{5,9},{9,5},{6,10},{10,6},{7,11},{11,7},{20,24},{24,20... | collective-permute-start | bytes 1572872 | tf_op jit(solution)/shard_map/ppermute | solution.py:68
  42.4 13.7 %collective-permute-start.6 = (bf16[256,1024]{1,0:T(8,128)(2,1)S(1)}, bf16[256,1024]{1,0:T(8,128)(2,1)S(1)}, u32[]{:S(2)}, u32[]{:S(2)}) collective-permute-start(bf16[256,1024]{1,0:T(8,128)(2,1)S(1)} %broadcast_select_fusion.12), channel_id=1, source_target_pairs={{4,0},{8,12},{5,1},{9,13},{6,2},{10,14},{7,3},{11,15},{20,16},{24,... | collective-permute-start | bytes 1572872 | tf_op jit(solution)/shard_map/ppermute | solution.py:68
  45.0 46.5 %copy-start.4 = (bf16[256,1024]{1,0:T(8,128)(2,1)}, bf16[256,1024]{1,0:T(8,128)(2,1)S(1)}, u32[]{:S(2)}) copy-start(bf16[256,1024]{1,0:T(8,128)(2,1)S(1)} %get-tuple-element.115.refs_6_) | copy-start | bytes 1572868
  45.0 11.1 %collective-permute-start.7 = (bf16[256,1024]{1,0:T(8,128)(2,1)S(1)}, bf16[256,1024]{1,0:T(8,128)(2,1)S(1)}, u32[]{:S(2)}, u32[]{:S(2)}) collective-permute-start(bf16[256,1024]{1,0:T(8,128)(2,1)S(1)} %get-tuple-element.114), channel_id=1, source_target_pairs={{0,1},{1,0},{2,3},{3,2},{4,5},{5,4},{6,7},{7,6},{8,9},{9,8},{10,11... | collective-permute-start | bytes 1572872 | tf_op jit(solution)/shard_map/ppermute | solution.py:64
  46.3 43.7 %copy-start.2 = (bf16[256,1024]{1,0:T(8,128)(2,1)}, bf16[256,1024]{1,0:T(8,128)(2,1)S(1)}, u32[]{:S(2)}) copy-start(bf16[256,1024]{1,0:T(8,128)(2,1)S(1)} %broadcast_select_fusion.3.refs_7_) | copy-start | bytes 1572868
  46.3 46.8 %copy-start.1 = (bf16[768,1024]{1,0:T(8,128)(2,1)}, bf16[768,1024]{1,0:T(8,128)(2,1)S(1)}, u32[]{:S(2)}) copy-start(bf16[768,1024]{1,0:T(8,128)(2,1)S(1)} %collective-permute-done.10.grad_1) | copy-start | bytes 4718596
  46.3 14.3 %collective-permute-start.12 = (bf16[256,1024]{1,0:T(8,128)(2,1)S(1)}, bf16[256,1024]{1,0:T(8,128)(2,1)S(1)}, u32[]{:S(2)}, u32[]{:S(2)}) collective-permute-start(bf16[256,1024]{1,0:T(8,128)(2,1)S(1)} %broadcast_select_fusion.3.refs_7_), channel_id=1, source_target_pairs={{0,16},{16,0},{1,17},{17,1},{2,18},{18,2},{3,19},{19,3},{4,20},{20... | collective-permute-start | bytes 1572872 | tf_op jit(solution)/shard_map/ppermute | solution.py:64
  56.1 33.3 %copy-start.14 = (bf16[256,1024]{1,0:T(8,128)(2,1)}, bf16[256,1024]{1,0:T(8,128)(2,1)S(1)}, u32[]{:S(2)}) copy-start(bf16[256,1024]{1,0:T(8,128)(2,1)S(1)} %collective-permute-done.7.refs_5_) | copy-start | bytes 1572868
  56.1 8.4 %collective-permute-start.15 = (bf16[256,1024]{1,0:T(8,128)(2,1)}, bf16[256,1024]{1,0:T(8,128)(2,1)S(1)}, u32[]{:S(2)}, u32[]{:S(2)}) collective-permute-start(bf16[256,1024]{1,0:T(8,128)(2,1)} %collective-permute-done.3), channel_id=1, source_target_pairs={{4,8},{8,4},{5,9},{9,5},{6,10},{10,6},{7,11},{11,7},{20,24},{24,20... | collective-permute-start | bytes 1572872 | tf_op jit(solution)/shard_map/ppermute | solution.py:68
  56.8 12.8 %collective-permute-start.16 = (bf16[256,1024]{1,0:T(8,128)(2,1)S(1)}, bf16[256,1024]{1,0:T(8,128)(2,1)S(1)}, u32[]{:S(2)}, u32[]{:S(2)}) collective-permute-start(bf16[256,1024]{1,0:T(8,128)(2,1)S(1)} %broadcast_select_fusion.11), channel_id=1, source_target_pairs={{4,0},{8,12},{5,1},{9,13},{6,2},{10,14},{7,3},{11,15},{20,16},{24,... | collective-permute-start | bytes 1572872 | tf_op jit(solution)/shard_map/ppermute | solution.py:68
  58.8 5.8 %copy-start.7 = (bf16[1,768,1024]{2,1,0:T(8,128)(2,1)S(1)}, bf16[1,768,1024]{2,1,0:T(8,128)(2,1)}, u32[]{:S(2)}) copy-start(bf16[1,768,1024]{2,1,0:T(8,128)(2,1)} %param.3) | copy-start | bytes 4718596
  60.6 50.4 %copy-start.10 = (bf16[256,1024]{1,0:T(8,128)(2,1)}, bf16[256,1024]{1,0:T(8,128)(2,1)S(1)}, u32[]{:S(2)}) copy-start(bf16[256,1024]{1,0:T(8,128)(2,1)S(1)} %collective-permute-done.12.refs_8_) | copy-start | bytes 1572868
  60.6 13.4 %collective-permute-start.13 = (bf16[256,1024]{1,0:T(8,128)(2,1)S(1)}, bf16[256,1024]{1,0:T(8,128)(2,1)S(1)}, u32[]{:S(2)}, u32[]{:S(2)}) collective-permute-start(bf16[256,1024]{1,0:T(8,128)(2,1)S(1)} %broadcast_select_fusion.2), channel_id=1, source_target_pairs={{0,16},{16,0},{1,17},{17,1},{2,18},{18,2},{3,19},{19,3},{4,20},{20... | collective-permute-start | bytes 1572872 | tf_op jit(solution)/shard_map/ppermute | solution.py:64
  62.1 18.7 %collective-permute-start.11 = (f32[768,256]{1,0:T(8,128)S(1)}, f32[768,256]{1,0:T(8,128)S(1)}, u32[]{:S(2)}, u32[]{:S(2)}) collective-permute-start(f32[768,256]{1,0:T(8,128)S(1)} %fusion.5), channel_id=1, source_target_pairs={{0,2},{2,0},{1,3},{3,1},{4,6},{6,4},{5,7},{7,5},{8,10},{10,8},{9,1... | collective-permute-start | bytes 2359304 | tf_op jit(solution)/shard_map/ppermute | solution.py:64
  64.5 33.6 %collective-permute-start.19 = (bf16[768,1024]{1,0:T(8,128)(2,1)}, bf16[768,1024]{1,0:T(8,128)(2,1)S(1)}, u32[]{:S(2)}, u32[]{:S(2)}) collective-permute-start(bf16[768,1024]{1,0:T(8,128)(2,1)} %collective-permute-done.9.refs_2_), channel_id=1, source_target_pairs={{0,1},{1,0},{2,3},{3,2},{4,5},{5,4},{6,7},{7,6},{8,9},{9,8},{10,11... | collective-permute-start | bytes 4718600 | tf_op jit(solution)/shard_map/ppermute | solution.py:64
  64.5 33.6 %collective-permute-start.18 = (bf16[768,1024]{1,0:T(8,128)(2,1)S(1)}, bf16[768,1024]{1,0:T(8,128)(2,1)S(1)}, u32[]{:S(2)}, u32[]{:S(2)}) collective-permute-start(bf16[768,1024]{1,0:T(8,128)(2,1)S(1)} %bitcast.61), channel_id=1, source_target_pairs={{0,1},{1,0},{2,3},{3,2},{4,5},{5,4},{6,7},{7,6},{8,9},{9,8},{10,11... | collective-permute-start | bytes 4718600 | tf_op jit(solution)/shard_map/ppermute | solution.py:64
  69.6 12.6 %copy-start.6 = (bf16[256,1024]{1,0:T(8,128)(2,1)}, bf16[256,1024]{1,0:T(8,128)(2,1)S(1)}, u32[]{:S(2)}) copy-start(bf16[256,1024]{1,0:T(8,128)(2,1)S(1)} %broadcast_select_fusion.1.refs_8_) | copy-start | bytes 1572868
  69.7 16.8 %collective-permute-start.17 = (bf16[256,1024]{1,0:T(8,128)(2,1)S(1)}, bf16[256,1024]{1,0:T(8,128)(2,1)S(1)}, u32[]{:S(2)}, u32[]{:S(2)}) collective-permute-start(bf16[256,1024]{1,0:T(8,128)(2,1)S(1)} %broadcast_select_fusion.10), channel_id=1, source_target_pairs={{4,0},{8,12},{5,1},{9,13},{6,2},{10,14},{7,3},{11,15},{20,16},{24,... | collective-permute-start | bytes 1572872 | tf_op jit(solution)/shard_map/ppermute | solution.py:68
  74.0 14.9 %collective-permute-start.20 = (bf16[256,1024]{1,0:T(8,128)(2,1)S(1)}, bf16[256,1024]{1,0:T(8,128)(2,1)S(1)}, u32[]{:S(2)}, u32[]{:S(2)}) collective-permute-start(bf16[256,1024]{1,0:T(8,128)(2,1)S(1)} %broadcast_select_fusion.1.refs_8_), channel_id=1, source_target_pairs={{0,16},{16,0},{1,17},{17,1},{2,18},{18,2},{3,19},{19,3},{4,20},{20... | collective-permute-start | bytes 1572872 | tf_op jit(solution)/shard_map/ppermute | solution.py:64
  80.8 3.1 %copy-start.20 = (f32[768,256]{1,0:T(8,128)}, f32[768,256]{1,0:T(8,128)S(1)}, u32[]{:S(2)}) copy-start(f32[768,256]{1,0:T(8,128)S(1)} %collective-permute-done.11) | copy-start | bytes 2359300
  80.8 17.4 %collective-permute-start.14 = (f32[768,256]{1,0:T(8,128)S(1)}, f32[768,256]{1,0:T(8,128)S(1)}, u32[]{:S(2)}, u32[]{:S(2)}) collective-permute-start(f32[768,256]{1,0:T(8,128)S(1)} %fusion.4), channel_id=1, source_target_pairs={{0,2},{2,0},{1,3},{3,1},{4,6},{6,4},{5,7},{7,5},{8,10},{10,8},{9,1... | collective-permute-start | bytes 2359304 | tf_op jit(solution)/shard_map/ppermute | solution.py:64
  86.5 12.9 %collective-permute-start.23 = (bf16[256,1024]{1,0:T(8,128)(2,1)S(1)}, bf16[256,1024]{1,0:T(8,128)(2,1)S(1)}, u32[]{:S(2)}, u32[]{:S(2)}) collective-permute-start(bf16[256,1024]{1,0:T(8,128)(2,1)S(1)} %broadcast_select_fusion.9), channel_id=1, source_target_pairs={{4,0},{8,12},{5,1},{9,13},{6,2},{10,14},{7,3},{11,15},{20,16},{24,... | collective-permute-start | bytes 1572872 | tf_op jit(solution)/shard_map/ppermute | solution.py:68
  88.8 5.7 %copy-start.3 = (bf16[256,1024]{1,0:T(8,128)(2,1)}, bf16[256,1024]{1,0:T(8,128)(2,1)S(1)}, u32[]{:S(2)}) copy-start(bf16[256,1024]{1,0:T(8,128)(2,1)S(1)} %get-tuple-element.88.refs_1_) | copy-start | bytes 1572868
  88.8 4.2 %copy-start.15 = (bf16[256,1024]{1,0:T(8,128)(2,1)}, bf16[256,1024]{1,0:T(8,128)(2,1)S(1)}, u32[]{:S(2)}) copy-start(bf16[256,1024]{1,0:T(8,128)(2,1)S(1)} %collective-permute-done.20.refs_9_) | copy-start | bytes 1572868
  88.8 11.8 %collective-permute-start.22 = (bf16[256,1024]{1,0:T(8,128)(2,1)S(1)}, bf16[256,1024]{1,0:T(8,128)(2,1)S(1)}, u32[]{:S(2)}, u32[]{:S(2)}) collective-permute-start(bf16[256,1024]{1,0:T(8,128)(2,1)S(1)} %get-tuple-element.88.refs_1_), channel_id=1, source_target_pairs={{0,16},{16,0},{1,17},{17,1},{2,18},{18,2},{3,19},{19,3},{4,20},{20... | collective-permute-start | bytes 1572872 | tf_op jit(solution)/shard_map/ppermute | solution.py:64
  98.2 4.4 %copy-start.22 = (f32[768,256]{1,0:T(8,128)}, f32[768,256]{1,0:T(8,128)S(1)}, u32[]{:S(2)}) copy-start(f32[768,256]{1,0:T(8,128)S(1)} %collective-permute-done.14) | copy-start | bytes 2359300
  98.2 4.4 %copy-start.8 = (bf16[768,1024]{1,0:T(8,128)(2,1)}, bf16[768,1024]{1,0:T(8,128)(2,1)S(1)}, u32[]{:S(2)}) copy-start(bf16[768,1024]{1,0:T(8,128)(2,1)S(1)} %collective-permute-done.19.refs_3_) | copy-start | bytes 4718596
  98.2 4.4 %copy-start.9 = (bf16[768,1024]{1,0:T(8,128)(2,1)}, bf16[768,1024]{1,0:T(8,128)(2,1)S(1)}, u32[]{:S(2)}) copy-start(bf16[768,1024]{1,0:T(8,128)(2,1)S(1)} %collective-permute-done.18.refs_1_) | copy-start | bytes 4718596
  99.4 16.0 %collective-permute-start.21 = (f32[768,256]{1,0:T(8,128)}, f32[768,256]{1,0:T(8,128)}, u32[]{:S(2)}, u32[]{:S(2)}) collective-permute-start(f32[768,256]{1,0:T(8,128)} %fusion.3), channel_id=1, source_target_pairs={{0,2},{2,0},{1,3},{3,1},{4,6},{6,4},{5,7},{7,5},{8,10},{10,8},{9,1... | collective-permute-start | bytes 2359304 | tf_op jit(solution)/shard_map/ppermute | solution.py:64
  100.6 10.4 %copy-start.5 = (bf16[256,1024]{1,0:T(8,128)(2,1)}, bf16[256,1024]{1,0:T(8,128)(2,1)S(1)}, u32[]{:S(2)}) copy-start(bf16[256,1024]{1,0:T(8,128)(2,1)S(1)} %select_select_fusion.refs_0_.refs_2_.refs_11_) | copy-start | bytes 1572868
  100.6 13.0 %collective-permute-start.24 = (bf16[256,1024]{1,0:T(8,128)(2,1)S(1)}, bf16[256,1024]{1,0:T(8,128)(2,1)S(1)}, u32[]{:S(2)}, u32[]{:S(2)}) collective-permute-start(bf16[256,1024]{1,0:T(8,128)(2,1)S(1)} %select_select_fusion.refs_0_.refs_2_.refs_11_), channel_id=1, source_target_pairs={{0,16},{16,0},{1,17},{17,1},{2,18},{18,2},{3,19},{19,3},{4,20},{20... | collective-permute-start | bytes 1572872 | tf_op jit(solution)/shard_map/ppermute | solution.py:64
  102.6 8.4 %copy-start.12 = (bf16[256,1024]{1,0:T(8,128)(2,1)S(1)}, bf16[256,1024]{1,0:T(8,128)(2,1)}, u32[]{:S(2)}) copy-start(bf16[256,1024]{1,0:T(8,128)(2,1)} %copy-done.11) | copy-start | bytes 1572868
  115.4 9.8 %collective-permute-start.25 = (f32[768,1024]{1,0:T(8,128)}, f32[768,1024]{1,0:T(8,128)}, u32[]{:S(2)}, u32[]{:S(2)}) collective-permute-start(f32[768,1024]{1,0:T(8,128)} %shard_map.50), channel_id=1, source_target_pairs={{0,1},{1,0},{2,3},{3,2},{4,5},{5,4},{6,7},{7,6},{8,9},{9,8},{10,11... | collective-permute-start | bytes 9437192 | tf_op jit(solution)/shard_map/ppermute | solution.py:64
  115.4 20.2 %collective-permute-start.27 = (f32[768,256]{1,0:T(8,128)}, f32[768,256]{1,0:T(8,128)S(1)}, u32[]{:S(2)}, u32[]{:S(2)}) collective-permute-start(f32[768,256]{1,0:T(8,128)} %fusion), channel_id=1, source_target_pairs={{0,2},{2,0},{1,3},{3,1},{4,6},{6,4},{5,7},{7,5},{8,10},{10,8},{9,1... | collective-permute-start | bytes 2359304 | tf_op jit(solution)/shard_map/ppermute | solution.py:64
  116.0 6.2 %copy-start.16 = (f32[768,256]{1,0:T(8,128)S(1)}, f32[768,256]{1,0:T(8,128)}, u32[]{:S(2)}) copy-start(f32[768,256]{1,0:T(8,128)} %fusion.2) | copy-start | bytes 2359300
  116.0 6.2 %copy-start.21 = (f32[768,256]{1,0:T(8,128)S(1)}, f32[768,256]{1,0:T(8,128)}, u32[]{:S(2)}) copy-start(f32[768,256]{1,0:T(8,128)} %copy-done.20) | copy-start | bytes 2359300
  124.2 9.8 %collective-permute-start.26 = (bf16[768,256]{1,0:T(8,128)(2,1)}, bf16[768,256]{1,0:T(8,128)(2,1)S(1)}, u32[]{:S(2)}, u32[]{:S(2)}) collective-permute-start(bf16[768,256]{1,0:T(8,128)(2,1)} %get-tuple-element.110), channel_id=1, source_target_pairs={{0,1},{1,0},{2,3},{3,2},{4,5},{5,4},{6,7},{7,6},{8,9},{9,8},{10,11... | collective-permute-start | bytes 1179656 | tf_op jit(solution)/shard_map/ppermute | solution.py:64
  125.2 10.3 %copy-start.24 = (f32[768,256]{1,0:T(8,128)S(1)}, f32[768,256]{1,0:T(8,128)}, u32[]{:S(2)}) copy-start(f32[768,256]{1,0:T(8,128)} %get-tuple-element.106) | copy-start | bytes 2359300
  135.7 1.8 %collective-permute-start.28 = (bf16[768,256]{1,0:T(8,128)(2,1)S(1)}, bf16[768,256]{1,0:T(8,128)(2,1)S(1)}, u32[]{:S(2)}, u32[]{:S(2)}) collective-permute-start(bf16[768,256]{1,0:T(8,128)(2,1)S(1)} %get-tuple-element.108), channel_id=1, source_target_pairs={{0,1},{1,0},{2,3},{3,2},{4,5},{5,4},{6,7},{7,6},{8,9},{9,8},{10,11... | collective-permute-start | bytes 1179656 | tf_op jit(solution)/shard_map/ppermute | solution.py:64
  (6 other events, 9.4 us)

commit v5 on v4

--- a/solution.py
+++ b/solution.py
@@ -263,19 +263,14 @@
     done.append(last)
     first_mine = pick(early, plane // 2, plane & 1) == core
     here_z, got_z = pick(first_mine, done[0], done[2]), swap(pick(first_mine, done[2], done[0]), "k")
-    done, kept, projected, here_z, got_z, there = lax.optimization_barrier(
-        (done, kept, projected, here_z, got_z, there)
-    )
+    head_grad = jnp.zeros_like(heads)
+    for of_core, part in ((core, here_z), (1 - core, got_z)):
+        head_grad = lax.dynamic_update_slice_in_dim(head_grad, part, of_core * half + group * quarter, 1)
+    done, kept, projected, head_grad, there = lax.optimization_barrier((done, kept, projected, head_grad, there))
     done.append((kept + there).astype(jnp.bfloat16))
     here_x, got_x = pick(first_mine, done[1], done[3]), swap(pick(first_mine, done[3], done[1]), "k")
-    head_grad = jnp.zeros_like(heads)
-    for of_core, of_group, part in (
-        (core, group, here_z),
-        (1 - core, group, got_z),
-        (core, 1 - group, here_x),
-        (1 - core, 1 - group, got_x),
-    ):
-        head_grad = lax.dynamic_update_slice_in_dim(head_grad, part, of_core * half + of_group * quarter, 1)
+    for of_core, part in ((core, here_x), (1 - core, got_x)):
+        head_grad = lax.dynamic_update_slice_in_dim(head_grad, part, of_core * half + (1 - group) * quarter, 1)
     return projected[None], head_grad[None]
 
 

time: 140 us -> 140 us (level)
    select_n x15 -> x14, other arithmetic: 12 us -> 11.2 us  [pick(): return jnp.where(flag, yes, no)]
  transfers between devices with their start and end apart: 29 -> 29, of which waited for: 14 -> 15; matrix products, arithmetic and copies ran while one was open for 22% -> 21% of each run, Pallas kernels for 17% -> 17%
where the time goes in v5:
time: 140 us; the launch traced here: 139 us
  waiting for transfers between devices  48.5 us (35%)
  starting transfers between devices  31.4 us (22%)
  Pallas kernels  23.2 us (17%)
  matrix products  15.1 us (11%)
  other arithmetic  11.5 us (8%)
  local copies, waits for them, and re-layouts  7.96 us (6%)
    ppermute x10, waiting for transfers between devices, send(): return lax.ppermute(value, 'a', pairs)  31.9 us
    pallas_call x2, Pallas kernels, forward_sum(): pl.pallas_call(functools.partial(sum_of_products, len(base)), grid_spec=s...  17.1 us
    ppermute x10, starting transfers between devices, send(): return lax.ppermute(value, 'a', pairs)  16.9 us
    ppermute x19, waiting for transfers between devices, swap(): return lax.ppermute(value, axis, [(0, 1), (1, 0)])  16.5 us
    dot_general x12, matrix products, times_rows(): lax.dot_general(left, right, (((1,), (1,)), ((), ())), preferred_element_...  15.1 us
    ppermute x19, starting transfers between devices, swap(): return lax.ppermute(value, axis, [(0, 1), (1, 0)])  14.5 us
    select_n x14, other arithmetic, pick(): return jnp.where(flag, yes, no)  11.2 us
    pallas_call x1, Pallas kernels, keep(): pl.pallas_call(kept_sums, grid=(tokens // tile,), in_specs=[pl.BlockSpec(...  6.13 us
  transfers between devices with their start and end apart: 29, of which 15 were waited for; matrix products, arithmetic and copies ran while one was open for 21% of the time, Pallas kernels for 17%

profile of v5, /device:TPU:0, one launch (start us, length us, event | category | flops | bytes accessed | tf_op | source)
XLA Modules:
  0.0 138.7 jit_solution(5999843830988367960)
XLA Ops:
  0.7 2.0 %dynamic-slice_bitcast_fusion.refs_5_ = bf16[256,1024]{1,0:T(8,128)(2,1)} fusion(bf16[1,1024,1024]{2,1,0:T(8,128)(2,1)} %param.5, s32[]{:T(128)S(6)} %select_n.205), kind=kLoop, calls=%fused_computation.34 | loop fusion | bytes 1048580 | tf_op jit(solution)/shard_map/dynamic_slice | solution.py:179
  2.7 1.1 constant_dynamic-slice_fusion.2
  4.3 1.4 %collective-permute-start = (bf16[256,1024]{1,0:T(8,128)(2,1)}, bf16[256,1024]{1,0:T(8,128)(2,1)}, u32[]{:S(2)}, u32[]{:S(2)}) collective-permute-start(bf16[256,1024]{1,0:T(8,128)(2,1)} %dynamic-slice_bitcast_fusion.refs_5_), channel_id=1, source_target_pairs={{4,8},{8,4},{5,9},{9,5},{6,10},{10,6},{7,11},{11,7},{20,24},{24,20... | collective-permute-start | bytes 1572872 | tf_op jit(solution)/shard_map/ppermute | solution.py:68
  5.9 4.5 %collective-permute-start.2 = (bf16[256,1024]{1,0:T(8,128)(2,1)}, bf16[256,1024]{1,0:T(8,128)(2,1)}, u32[]{:S(2)}, u32[]{:S(2)}) collective-permute-start(bf16[256,1024]{1,0:T(8,128)(2,1)} %collective-permute-done.1.refs_4_), channel_id=1, source_target_pairs={{0,4},{12,8},{4,0},{8,12},{1,5},{13,9},{5,1},{9,13},{2,6},{14,10},... | collective-permute-start | bytes 1572872 | tf_op jit(solution)/shard_map/ppermute | solution.py:68
  10.4 1.5 %collective-permute-start.9 = (bf16[768,1024]{1,0:T(8,128)(2,1)}, bf16[768,1024]{1,0:T(8,128)(2,1)}, u32[]{:S(2)}, u32[]{:S(2)}) collective-permute-start(bf16[768,1024]{1,0:T(8,128)(2,1)} %bitcast.55), channel_id=1, source_target_pairs={{0,2},{2,0},{1,3},{3,1},{4,6},{6,4},{5,7},{7,5},{8,10},{10,8},{9,1... | collective-permute-start | bytes 4718600 | tf_op jit(solution)/shard_map/ppermute | solution.py:64
  12.0 11.1 %collective-permute-done.2.refs_6_.refs_3_ = bf16[256,1024]{1,0:T(8,128)(2,1)} collective-permute-done((bf16[256,1024]{1,0:T(8,128)(2,1)}, bf16[256,1024]{1,0:T(8,128)(2,1)}, u32[]{:S(2)}, u32[]{:S(2)}) %collective-permute-start.2) | collective-permute-done | bytes 524320 | tf_op jit(solution)/shard_map/ppermute | solution.py:68
  23.0 1.5 %collective-permute-start.4 = (bf16[256,1024]{1,0:T(8,128)(2,1)}, bf16[256,1024]{1,0:T(8,128)(2,1)}, u32[]{:S(2)}, u32[]{:S(2)}) collective-permute-start(bf16[256,1024]{1,0:T(8,128)(2,1)} %collective-permute-done.1.refs_4_), channel_id=1, source_target_pairs={{4,8},{8,4},{5,9},{9,5},{6,10},{10,6},{7,11},{11,7},{20,24},{24,20... | collective-permute-start | bytes 1572872 | tf_op jit(solution)/shard_map/ppermute | solution.py:68
  24.5 2.0 %broadcast_select_fusion.4 = bf16[256,1024]{1,0:T(8,128)(2,1)} fusion(bf16[256,1024]{1,0:T(8,128)(2,1)} %collective-permute-done, pred[]{:T(512)S(6)} %and.55, bf16[1,1024,1024]{2,1,0:T(8,128)(2,1)} %param.5, s32[]{:T(128)S(6)} %select_n.205), kind=kLoop, calls=%fused_computation.39 | loop fusion | flops 262144 | bytes 1572869 | tf_op jit(solution)/shard_map/jit(_where)/select_n | solution.py:76
  26.5 2.8 %collective-permute-start.3 = (bf16[256,1024]{1,0:T(8,128)(2,1)}, bf16[256,1024]{1,0:T(8,128)(2,1)}, u32[]{:S(2)}, u32[]{:S(2)}) collective-permute-start(bf16[256,1024]{1,0:T(8,128)(2,1)} %broadcast_select_fusion.4), channel_id=1, source_target_pairs={{0,4},{12,8},{4,0},{8,12},{1,5},{13,9},{5,1},{9,13},{2,6},{14,10},... | collective-permute-start | bytes 1572872 | tf_op jit(solution)/shard_map/ppermute | solution.py:68
  29.4 1.5 %collective-permute-start.5 = (bf16[256,1024]{1,0:T(8,128)(2,1)}, bf16[256,1024]{1,0:T(8,128)(2,1)}, u32[]{:S(2)}, u32[]{:S(2)}) collective-permute-start(bf16[256,1024]{1,0:T(8,128)(2,1)} %collective-permute-done.2.refs_6_.refs_3_), channel_id=1, source_target_pairs={{0,16},{16,0},{1,17},{17,1},{2,18},{18,2},{3,19},{19,3},{4,20},{20... | collective-permute-start | bytes 1572872 | tf_op jit(solution)/shard_map/ppermute | solution.py:64
  32.8 1.1 broadcast_select_fusion.12
  33.9 7.0 %collective-permute-done.3 = bf16[256,1024]{1,0:T(8,128)(2,1)} collective-permute-done((bf16[256,1024]{1,0:T(8,128)(2,1)}, bf16[256,1024]{1,0:T(8,128)(2,1)}, u32[]{:S(2)}, u32[]{:S(2)}) %collective-permute-start.3) | collective-permute-done | bytes 524320 | tf_op jit(solution)/shard_map/ppermute | solution.py:68
  40.9 1.5 %collective-permute-done.5.refs_7_ = bf16[256,1024]{1,0:T(8,128)(2,1)} collective-permute-done((bf16[256,1024]{1,0:T(8,128)(2,1)}, bf16[256,1024]{1,0:T(8,128)(2,1)}, u32[]{:S(2)}, u32[]{:S(2)}) %collective-permute-start.5) | collective-permute-done | bytes 524320 | tf_op jit(solution)/shard_map/ppermute | solution.py:64
  42.4 1.3 collective-permute-start.6
  43.7 1.3 constant_dynamic-slice_fusion
  45.0 1.2 broadcast_select_fusion.3.refs_7_
  46.3 1.6 %collective-permute-start.12 = (bf16[256,1024]{1,0:T(8,128)(2,1)S(1)}, bf16[256,1024]{1,0:T(8,128)(2,1)S(1)}, u32[]{:S(2)}, u32[]{:S(2)}) collective-permute-start(bf16[256,1024]{1,0:T(8,128)(2,1)S(1)} %broadcast_select_fusion.3.refs_7_), channel_id=1, source_target_pairs={{0,16},{16,0},{1,17},{17,1},{2,18},{18,2},{3,19},{19,3},{4,20},{20... | collective-permute-start | bytes 1572872 | tf_op jit(solution)/shard_map/ppermute | solution.py:64
  48.0 8.1 %collective-permute-done.6 = bf16[256,1024]{1,0:T(8,128)(2,1)S(1)} collective-permute-done((bf16[256,1024]{1,0:T(8,128)(2,1)S(1)}, bf16[256,1024]{1,0:T(8,128)(2,1)S(1)}, u32[]{:S(2)}, u32[]{:S(2)}) %collective-permute-start.6) | collective-permute-done | bytes 524320 | tf_op jit(solution)/shard_map/ppermute | solution.py:68
  56.8 1.3 collective-permute-start.16
  59.4 1.2 collective-permute-done.12.refs_8_
  60.6 1.5 %collective-permute-start.13 = (bf16[256,1024]{1,0:T(8,128)(2,1)S(1)}, bf16[256,1024]{1,0:T(8,128)(2,1)S(1)}, u32[]{:S(2)}, u32[]{:S(2)}) collective-permute-start(bf16[256,1024]{1,0:T(8,128)(2,1)S(1)} %broadcast_select_fusion.2), channel_id=1, source_target_pairs={{0,16},{16,0},{1,17},{17,1},{2,18},{18,2},{3,19},{19,3},{4,20},{20... | collective-permute-start | bytes 1572872 | tf_op jit(solution)/shard_map/ppermute | solution.py:64
  62.1 2.5 %collective-permute-start.11 = (f32[768,256]{1,0:T(8,128)S(1)}, f32[768,256]{1,0:T(8,128)S(1)}, u32[]{:S(2)}, u32[]{:S(2)}) collective-permute-start(f32[768,256]{1,0:T(8,128)S(1)} %fusion.5), channel_id=1, source_target_pairs={{0,2},{2,0},{1,3},{3,1},{4,6},{6,4},{5,7},{7,5},{8,10},{10,8},{9,1... | collective-permute-start | bytes 2359304 | tf_op jit(solution)/shard_map/ppermute | solution.py:64
  65.1 4.5 %collective-permute-done.16 = bf16[256,1024]{1,0:T(8,128)(2,1)S(1)} collective-permute-done((bf16[256,1024]{1,0:T(8,128)(2,1)S(1)}, bf16[256,1024]{1,0:T(8,128)(2,1)S(1)}, u32[]{:S(2)}, u32[]{:S(2)}) %collective-permute-start.16) | collective-permute-done | bytes 524320 | tf_op jit(solution)/shard_map/ppermute | solution.py:68
  69.7 1.3 collective-permute-start.17
  71.0 3.0 %collective-permute-done.13 = bf16[256,1024]{1,0:T(8,128)(2,1)S(1)} collective-permute-done((bf16[256,1024]{1,0:T(8,128)(2,1)S(1)}, bf16[256,1024]{1,0:T(8,128)(2,1)S(1)}, u32[]{:S(2)}, u32[]{:S(2)}) %collective-permute-start.13) | collective-permute-done | bytes 524320 | tf_op jit(solution)/shard_map/ppermute | solution.py:64
  74.0 1.5 %collective-permute-start.20 = (bf16[256,1024]{1,0:T(8,128)(2,1)S(1)}, bf16[256,1024]{1,0:T(8,128)(2,1)S(1)}, u32[]{:S(2)}, u32[]{:S(2)}) collective-permute-start(bf16[256,1024]{1,0:T(8,128)(2,1)S(1)} %broadcast_select_fusion.1.refs_8_), channel_id=1, source_target_pairs={{0,16},{16,0},{1,17},{17,1},{2,18},{18,2},{3,19},{19,3},{4,20},{20... | collective-permute-start | bytes 1572872 | tf_op jit(solution)/shard_map/ppermute | solution.py:64
  76.1 1.1 broadcast_select_fusion.9
  78.4 2.4 %collective-permute-done.11 = f32[768,256]{1,0:T(8,128)S(1)} collective-permute-done((f32[768,256]{1,0:T(8,128)S(1)}, f32[768,256]{1,0:T(8,128)S(1)}, u32[]{:S(2)}, u32[]{:S(2)}) %collective-permute-start.11) | collective-permute-done | bytes 786464 | tf_op jit(solution)/shard_map/ppermute | solution.py:64
  80.8 1.4 %collective-permute-start.14 = (f32[768,256]{1,0:T(8,128)S(1)}, f32[768,256]{1,0:T(8,128)S(1)}, u32[]{:S(2)}, u32[]{:S(2)}) collective-permute-start(f32[768,256]{1,0:T(8,128)S(1)} %fusion.4), channel_id=1, source_target_pairs={{0,2},{2,0},{1,3},{3,1},{4,6},{6,4},{5,7},{7,5},{8,10},{10,8},{9,1... | collective-permute-start | bytes 2359304 | tf_op jit(solution)/shard_map/ppermute | solution.py:64
  82.2 1.7 %fusion.12 = f32[256,768]{0,1:T(8,128)S(1)} fusion(bf16[768,1024]{1,0:T(8,128)(2,1)S(1)} %collective-permute-done.10.grad_1, bf16[256,1024]{1,0:T(8,128)(2,1)S(1)} %broadcast_select_fusion.1.refs_8_, bf16[256,1024]{1,0:T(8,128)(2,1)} %collective-permute-done.1.refs_4_, pred[]{:T(512)S(6)} %ne.91), kind=kOutput, calls=%fused_computation.22 | convolution fusion | flops 402915328 | bytes 3407873 | tf_op jit(solution)/shard_map/dot_general | solution.py:84
  83.9 2.5 %fusion.2 = f32[768,256]{1,0:T(8,128)} fusion(f32[256,768]{0,1:T(8,128)S(1)} %fusion.12, bf16[256,1024]{1,0:T(8,128)(2,1)S(1)} %broadcast_select_fusion.2, bf16[256,1024]{1,0:T(8,128)(2,1)} %dynamic-slice_bitcast_fusion.refs_5_, pred[]{:T(512)S(6)} %ne.91, bf16[1,768,1024]{2,1,0:T(8,128)(2,1)S(1)} %copy-done), kind=kOutput, calls=%fused_computation.5 | convolution fusion | flops 403111936 | bytes 4194305 | tf_op jit(solution)/shard_map/dot_general | solution.py:84
  86.5 1.5 %collective-permute-start.23 = (bf16[256,1024]{1,0:T(8,128)(2,1)S(1)}, bf16[256,1024]{1,0:T(8,128)(2,1)S(1)}, u32[]{:S(2)}, u32[]{:S(2)}) collective-permute-start(bf16[256,1024]{1,0:T(8,128)(2,1)S(1)} %broadcast_select_fusion.9), channel_id=1, source_target_pairs={{4,0},{8,12},{5,1},{9,13},{6,2},{10,14},{7,3},{11,15},{20,16},{24,... | collective-permute-start | bytes 1572872 | tf_op jit(solution)/shard_map/ppermute | solution.py:68
  90.0 1.5 %fusion.3 = f32[768,256]{1,0:T(8,128)} fusion(f32[256,768]{0,1:T(8,128)S(1)} %fusion.15, bf16[256,1024]{1,0:T(8,128)(2,1)S(1)} %broadcast_select_fusion.3.refs_7_, bf16[256,1024]{1,0:T(8,128)(2,1)S(1)} %get-tuple-element.87.refs_1_, pred[]{:T(512)S(6)} %ne.91, bf16[1,768,1024]{2,1,0:T(8,128)(2,1)S(1)} %copy-done), kind=kOutput, calls=%fused_computation.7 | convolution fusion | flops 403111936 | bytes 4194305 | tf_op jit(solution)/shard_map/dot_general | solution.py:84
  91.5 1.5 %fusion.1 = f32[768,256]{1,0:T(8,128)} fusion(f32[256,768]{0,1:T(8,128)S(1)} %fusion.9, bf16[256,1024]{1,0:T(8,128)(2,1)S(1)} %collective-permute-done.13, bf16[256,1024]{1,0:T(8,128)(2,1)S(1)} %get-tuple-element.113.refs_6_, pred[]{:T(512)S(6)} %ne.91, bf16[1,768,1024]{2,1,0:T(8,128)(2,1)S(1)} %copy-done), kind=kOutput, calls=%fused_computation.3 | convolution fusion | flops 403111936 | bytes 4194305 | tf_op jit(solution)/shard_map/dot_general | solution.py:84
  93.0 1.5 %fusion.6 = f32[256,768]{0,1:T(8,128)} fusion(bf16[768,1024]{1,0:T(8,128)(2,1)S(1)} %collective-permute-done.10.grad_1, bf16[256,1024]{1,0:T(8,128)(2,1)} %collective-permute-done.5.refs_7_, bf16[256,1024]{1,0:T(8,128)(2,1)S(1)} %collective-permute-done.20.refs_9_, pred[]{:T(512)S(6)} %ne.91), kind=kOutput, calls=%fused_computation.16 | convolution fusion | flops 402915328 | bytes 3407873 | tf_op jit(solution)/shard_map/dot_general | solution.py:84
  95.4 2.7 %collective-permute-done.14 = f32[768,256]{1,0:T(8,128)S(1)} collective-permute-done((f32[768,256]{1,0:T(8,128)S(1)}, f32[768,256]{1,0:T(8,128)S(1)}, u32[]{:S(2)}, u32[]{:S(2)}) %collective-permute-start.14) | collective-permute-done | bytes 786464 | tf_op jit(solution)/shard_map/ppermute | solution.py:64
  98.2 1.2 collective-permute-done.23
  99.4 1.2 select_select_fusion.refs_0_.refs_2_.refs_11_
  101.5 1.1 broadcast_select_fusion.5
  102.6 8.4 %shard_map.50 = f32[768,1024]{1,0:T(8,128)} custom-call(s32[17]{0:T(128)} %stack.32.numbers, bf16[768,1024]{1,0:T(8,128)(2,1)} %bitcast.56, bf16[768,1024]{1,0:T(8,128)(2,1)} %copy-done.9, bf16[768,1024]{1,0:T(8,128)(2,1)} %collective-permute-done.9.refs_2_, bf16[768,1024]{1,0:T(8,128)(2,1)} %copy-done.8, bf16[256,1024]{1,0:T(8,128)(2,1)} %collective-permute-done.1.refs_4_, ...), custom_call_target="tpu_custom_call" | custom-call | flops 1000 | bytes 1000 | tf_op jit(solution)/shard_map/pallas_call | solution.py:150
  111.0 2.6 %fusion = f32[768,256]{1,0:T(8,128)} fusion(f32[256,768]{0,1:T(8,128)} %fusion.6, bf16[256,1024]{1,0:T(8,128)(2,1)S(1)} %collective-permute-done.12.refs_8_, bf16[256,1024]{1,0:T(8,128)(2,1)S(1)} %copy-done.13, pred[]{:T(512)S(6)} %ne.91, bf16[1,768,1024]{2,1,0:T(8,128)(2,1)S(1)} %copy-done), kind=kOutput, calls=%fused_computation.1 | convolution fusion | flops 403111936 | bytes 4194305 | tf_op jit(solution)/shard_map/dot_general | solution.py:84
  113.6 1.8 %collective-permute-done.21.there = f32[768,256]{1,0:T(8,128)} collective-permute-done((f32[768,256]{1,0:T(8,128)}, f32[768,256]{1,0:T(8,128)}, u32[]{:S(2)}, u32[]{:S(2)}) %collective-permute-start.21) | collective-permute-done | bytes 786464 | tf_op jit(solution)/shard_map/ppermute | solution.py:64
  116.0 6.1 %shard_map.51 = (bf16[768,256]{1,0:T(8,128)(2,1)}, f32[768,256]{1,0:T(8,128)}) custom-call(s32[1]{0:T(128)} %bitcast.18.flags, bf16[768,1024]{1,0:T(8,128)(2,1)} %bitcast.53, bf16[768,1024]{1,0:T(8,128)(2,1)} %copy-done.1, f32[768,256]{1,0:T(8,128)} %collective-permute-done.21.there, bf16[256,1024]{1,0:T(8,128)(2,1)} %copy-done.5, ...), custom_call_target="tpu_custom_call" | custom-call | flops 1000 | bytes 1000 | tf_op jit(solution)/shard_map/pallas_call | solution.py:122
  122.1 1.3 broadcast_select_fusion.14
  125.3 8.7 %shard_map.52 = bf16[768,1024]{1,0:T(8,128)(2,1)} custom-call(s32[17]{0:T(128)} %stack.29.numbers, bf16[768,1024]{1,0:T(8,128)(2,1)} %bitcast.57, bf16[768,1024]{1,0:T(8,128)(2,1)} %copy-done.9, bf16[768,1024]{1,0:T(8,128)(2,1)} %collective-permute-done.9.refs_2_, bf16[768,1024]{1,0:T(8,128)(2,1)} %copy-done.8, f32[768,1024]{1,0:T(8,128)} %collective-permute-done.25.refs_4_, ...), custom_call_target="tpu_custom_call" | custom-call | flops 1000 | bytes 1000 | tf_op jit(solution)/shard_map/pallas_call | solution.py:150
  134.0 1.6 %collective-permute-done.27 = f32[768,256]{1,0:T(8,128)S(1)} collective-permute-done((f32[768,256]{1,0:T(8,128)}, f32[768,256]{1,0:T(8,128)S(1)}, u32[]{:S(2)}, u32[]{:S(2)}) %collective-permute-start.27) | collective-permute-done | bytes 786464 | tf_op jit(solution)/shard_map/ppermute | solution.py:64
  135.9 1.6 %collective-permute-done.28 = bf16[768,256]{1,0:T(8,128)(2,1)S(1)} collective-permute-done((bf16[768,256]{1,0:T(8,128)(2,1)S(1)}, bf16[768,256]{1,0:T(8,128)(2,1)S(1)}, u32[]{:S(2)}, u32[]{:S(2)}) %collective-permute-start.28) | collective-permute-done | bytes 393248 | tf_op jit(solution)/shard_map/ppermute | solution.py:64
  137.6 1.1 copy-done.18
  (100 shorter events, 13.8 us)
Async XLA Ops:
  0.6 9.8 %copy-start = (bf16[1,768,1024]{2,1,0:T(8,128)(2,1)S(1)}, bf16[1,768,1024]{2,1,0:T(8,128)(2,1)}, u32[]{:S(2)}) copy-start(bf16[1,768,1024]{2,1,0:T(8,128)(2,1)} %param.4) | copy-start | bytes 4718596
  3.8 2.2 %collective-permute-start.1 = (bf16[256,1024]{1,0:T(8,128)(2,1)S(1)}, bf16[256,1024]{1,0:T(8,128)(2,1)}, u32[]{:S(2)}, u32[]{:S(2)}) collective-permute-start(bf16[256,1024]{1,0:T(8,128)(2,1)S(1)} %constant_dynamic-slice_fusion.2), channel_id=1, source_target_pairs={{0,1},{1,0},{2,3},{3,2},{4,5},{5,4},{6,7},{7,6},{8,9},{9,8},{10,11... | collective-permute-start | bytes 1572872 | tf_op jit(solution)/shard_map/ppermute | solution.py:64
  4.3 7.7 %collective-permute-start = (bf16[256,1024]{1,0:T(8,128)(2,1)}, bf16[256,1024]{1,0:T(8,128)(2,1)}, u32[]{:S(2)}, u32[]{:S(2)}) collective-permute-start(bf16[256,1024]{1,0:T(8,128)(2,1)} %dynamic-slice_bitcast_fusion.refs_5_), channel_id=1, source_target_pairs={{4,8},{8,4},{5,9},{9,5},{6,10},{10,6},{7,11},{11,7},{20,24},{24,20... | collective-permute-start | bytes 1572872 | tf_op jit(solution)/shard_map/ppermute | solution.py:68
  5.9 17.1 %collective-permute-start.2 = (bf16[256,1024]{1,0:T(8,128)(2,1)}, bf16[256,1024]{1,0:T(8,128)(2,1)}, u32[]{:S(2)}, u32[]{:S(2)}) collective-permute-start(bf16[256,1024]{1,0:T(8,128)(2,1)} %collective-permute-done.1.refs_4_), channel_id=1, source_target_pairs={{0,4},{12,8},{4,0},{8,12},{1,5},{13,9},{5,1},{9,13},{2,6},{14,10},... | collective-permute-start | bytes 1572872 | tf_op jit(solution)/shard_map/ppermute | solution.py:68
  10.4 35.8 %collective-permute-start.10 = (bf16[768,1024]{1,0:T(8,128)(2,1)S(1)}, bf16[768,1024]{1,0:T(8,128)(2,1)S(1)}, u32[]{:S(2)}, u32[]{:S(2)}) collective-permute-start(bf16[768,1024]{1,0:T(8,128)(2,1)S(1)} %bitcast.54), channel_id=1, source_target_pairs={{0,1},{1,0},{2,3},{3,2},{4,5},{5,4},{6,7},{7,6},{8,9},{9,8},{10,11... | collective-permute-start | bytes 4718600 | tf_op jit(solution)/shard_map/ppermute | solution.py:64
  10.4 37.5 %collective-permute-start.9 = (bf16[768,1024]{1,0:T(8,128)(2,1)}, bf16[768,1024]{1,0:T(8,128)(2,1)}, u32[]{:S(2)}, u32[]{:S(2)}) collective-permute-start(bf16[768,1024]{1,0:T(8,128)(2,1)} %bitcast.55), channel_id=1, source_target_pairs={{0,2},{2,0},{1,3},{3,1},{4,6},{6,4},{5,7},{7,5},{8,10},{10,8},{9,1... | collective-permute-start | bytes 4718600 | tf_op jit(solution)/shard_map/ppermute | solution.py:64
  23.0 9.0 %collective-permute-start.4 = (bf16[256,1024]{1,0:T(8,128)(2,1)}, bf16[256,1024]{1,0:T(8,128)(2,1)}, u32[]{:S(2)}, u32[]{:S(2)}) collective-permute-start(bf16[256,1024]{1,0:T(8,128)(2,1)} %collective-permute-done.1.refs_4_), channel_id=1, source_target_pairs={{4,8},{8,4},{5,9},{9,5},{6,10},{10,6},{7,11},{11,7},{20,24},{24,20... | collective-permute-start | bytes 1572872 | tf_op jit(solution)/shard_map/ppermute | solution.py:68
  26.5 14.4 %collective-permute-start.3 = (bf16[256,1024]{1,0:T(8,128)(2,1)}, bf16[256,1024]{1,0:T(8,128)(2,1)}, u32[]{:S(2)}, u32[]{:S(2)}) collective-permute-start(bf16[256,1024]{1,0:T(8,128)(2,1)} %broadcast_select_fusion.4), channel_id=1, source_target_pairs={{0,4},{12,8},{4,0},{8,12},{1,5},{13,9},{5,1},{9,13},{2,6},{14,10},... | collective-permute-start | bytes 1572872 | tf_op jit(solution)/shard_map/ppermute | solution.py:68
  29.4 13.0 %collective-permute-start.5 = (bf16[256,1024]{1,0:T(8,128)(2,1)}, bf16[256,1024]{1,0:T(8,128)(2,1)}, u32[]{:S(2)}, u32[]{:S(2)}) collective-permute-start(bf16[256,1024]{1,0:T(8,128)(2,1)} %collective-permute-done.2.refs_6_.refs_3_), channel_id=1, source_target_pairs={{0,16},{16,0},{1,17},{17,1},{2,18},{18,2},{3,19},{19,3},{4,20},{20... | collective-permute-start | bytes 1572872 | tf_op jit(solution)/shard_map/ppermute | solution.py:64
  32.1 15.8 %collective-permute-start.8 = (bf16[256,1024]{1,0:T(8,128)(2,1)}, bf16[256,1024]{1,0:T(8,128)(2,1)S(1)}, u32[]{:S(2)}, u32[]{:S(2)}) collective-permute-start(bf16[256,1024]{1,0:T(8,128)(2,1)} %collective-permute-done.2.refs_6_.refs_3_), channel_id=1, source_target_pairs={{4,8},{8,4},{5,9},{9,5},{6,10},{10,6},{7,11},{11,7},{20,24},{24,20... | collective-permute-start | bytes 1572872 | tf_op jit(solution)/shard_map/ppermute | solution.py:68
  42.4 13.7 %collective-permute-start.6 = (bf16[256,1024]{1,0:T(8,128)(2,1)S(1)}, bf16[256,1024]{1,0:T(8,128)(2,1)S(1)}, u32[]{:S(2)}, u32[]{:S(2)}) collective-permute-start(bf16[256,1024]{1,0:T(8,128)(2,1)S(1)} %broadcast_select_fusion.12), channel_id=1, source_target_pairs={{4,0},{8,12},{5,1},{9,13},{6,2},{10,14},{7,3},{11,15},{20,16},{24,... | collective-permute-start | bytes 1572872 | tf_op jit(solution)/shard_map/ppermute | solution.py:68
  45.0 46.5 %copy-start.4 = (bf16[256,1024]{1,0:T(8,128)(2,1)}, bf16[256,1024]{1,0:T(8,128)(2,1)S(1)}, u32[]{:S(2)}) copy-start(bf16[256,1024]{1,0:T(8,128)(2,1)S(1)} %get-tuple-element.113.refs_6_) | copy-start | bytes 1572868
  45.0 11.1 %collective-permute-start.7 = (bf16[256,1024]{1,0:T(8,128)(2,1)S(1)}, bf16[256,1024]{1,0:T(8,128)(2,1)S(1)}, u32[]{:S(2)}, u32[]{:S(2)}) collective-permute-start(bf16[256,1024]{1,0:T(8,128)(2,1)S(1)} %get-tuple-element.112), channel_id=1, source_target_pairs={{0,1},{1,0},{2,3},{3,2},{4,5},{5,4},{6,7},{7,6},{8,9},{9,8},{10,11... | collective-permute-start | bytes 1572872 | tf_op jit(solution)/shard_map/ppermute | solution.py:64
  46.3 43.7 %copy-start.2 = (bf16[256,1024]{1,0:T(8,128)(2,1)}, bf16[256,1024]{1,0:T(8,128)(2,1)S(1)}, u32[]{:S(2)}) copy-start(bf16[256,1024]{1,0:T(8,128)(2,1)S(1)} %broadcast_select_fusion.3.refs_7_) | copy-start | bytes 1572868
  46.3 46.7 %copy-start.1 = (bf16[768,1024]{1,0:T(8,128)(2,1)}, bf16[768,1024]{1,0:T(8,128)(2,1)S(1)}, u32[]{:S(2)}) copy-start(bf16[768,1024]{1,0:T(8,128)(2,1)S(1)} %collective-permute-done.10.grad_1) | copy-start | bytes 4718596
  46.3 14.3 %collective-permute-start.12 = (bf16[256,1024]{1,0:T(8,128)(2,1)S(1)}, bf16[256,1024]{1,0:T(8,128)(2,1)S(1)}, u32[]{:S(2)}, u32[]{:S(2)}) collective-permute-start(bf16[256,1024]{1,0:T(8,128)(2,1)S(1)} %broadcast_select_fusion.3.refs_7_), channel_id=1, source_target_pairs={{0,16},{16,0},{1,17},{17,1},{2,18},{18,2},{3,19},{19,3},{4,20},{20... | collective-permute-start | bytes 1572872 | tf_op jit(solution)/shard_map/ppermute | solution.py:64
  56.1 33.3 %copy-start.14 = (bf16[256,1024]{1,0:T(8,128)(2,1)}, bf16[256,1024]{1,0:T(8,128)(2,1)S(1)}, u32[]{:S(2)}) copy-start(bf16[256,1024]{1,0:T(8,128)(2,1)S(1)} %collective-permute-done.7.refs_5_) | copy-start | bytes 1572868
  56.1 8.4 %collective-permute-start.15 = (bf16[256,1024]{1,0:T(8,128)(2,1)}, bf16[256,1024]{1,0:T(8,128)(2,1)S(1)}, u32[]{:S(2)}, u32[]{:S(2)}) collective-permute-start(bf16[256,1024]{1,0:T(8,128)(2,1)} %collective-permute-done.3), channel_id=1, source_target_pairs={{4,8},{8,4},{5,9},{9,5},{6,10},{10,6},{7,11},{11,7},{20,24},{24,20... | collective-permute-start | bytes 1572872 | tf_op jit(solution)/shard_map/ppermute | solution.py:68
  56.8 12.8 %collective-permute-start.16 = (bf16[256,1024]{1,0:T(8,128)(2,1)S(1)}, bf16[256,1024]{1,0:T(8,128)(2,1)S(1)}, u32[]{:S(2)}, u32[]{:S(2)}) collective-permute-start(bf16[256,1024]{1,0:T(8,128)(2,1)S(1)} %broadcast_select_fusion.11), channel_id=1, source_target_pairs={{4,0},{8,12},{5,1},{9,13},{6,2},{10,14},{7,3},{11,15},{20,16},{24,... | collective-permute-start | bytes 1572872 | tf_op jit(solution)/shard_map/ppermute | solution.py:68
  58.8 5.8 %copy-start.7 = (bf16[1,768,1024]{2,1,0:T(8,128)(2,1)S(1)}, bf16[1,768,1024]{2,1,0:T(8,128)(2,1)}, u32[]{:S(2)}) copy-start(bf16[1,768,1024]{2,1,0:T(8,128)(2,1)} %param.3) | copy-start | bytes 4718596
  60.6 50.4 %copy-start.10 = (bf16[256,1024]{1,0:T(8,128)(2,1)}, bf16[256,1024]{1,0:T(8,128)(2,1)S(1)}, u32[]{:S(2)}) copy-start(bf16[256,1024]{1,0:T(8,128)(2,1)S(1)} %collective-permute-done.12.refs_8_) | copy-start | bytes 1572868
  60.6 13.4 %collective-permute-start.13 = (bf16[256,1024]{1,0:T(8,128)(2,1)S(1)}, bf16[256,1024]{1,0:T(8,128)(2,1)S(1)}, u32[]{:S(2)}, u32[]{:S(2)}) collective-permute-start(bf16[256,1024]{1,0:T(8,128)(2,1)S(1)} %broadcast_select_fusion.2), channel_id=1, source_target_pairs={{0,16},{16,0},{1,17},{17,1},{2,18},{18,2},{3,19},{19,3},{4,20},{20... | collective-permute-start | bytes 1572872 | tf_op jit(solution)/shard_map/ppermute | solution.py:64
  62.1 18.7 %collective-permute-start.11 = (f32[768,256]{1,0:T(8,128)S(1)}, f32[768,256]{1,0:T(8,128)S(1)}, u32[]{:S(2)}, u32[]{:S(2)}) collective-permute-start(f32[768,256]{1,0:T(8,128)S(1)} %fusion.5), channel_id=1, source_target_pairs={{0,2},{2,0},{1,3},{3,1},{4,6},{6,4},{5,7},{7,5},{8,10},{10,8},{9,1... | collective-permute-start | bytes 2359304 | tf_op jit(solution)/shard_map/ppermute | solution.py:64
  64.5 33.6 %collective-permute-start.19 = (bf16[768,1024]{1,0:T(8,128)(2,1)}, bf16[768,1024]{1,0:T(8,128)(2,1)S(1)}, u32[]{:S(2)}, u32[]{:S(2)}) collective-permute-start(bf16[768,1024]{1,0:T(8,128)(2,1)} %collective-permute-done.9.refs_2_), channel_id=1, source_target_pairs={{0,1},{1,0},{2,3},{3,2},{4,5},{5,4},{6,7},{7,6},{8,9},{9,8},{10,11... | collective-permute-start | bytes 4718600 | tf_op jit(solution)/shard_map/ppermute | solution.py:64
  64.5 33.6 %collective-permute-start.18 = (bf16[768,1024]{1,0:T(8,128)(2,1)S(1)}, bf16[768,1024]{1,0:T(8,128)(2,1)S(1)}, u32[]{:S(2)}, u32[]{:S(2)}) collective-permute-start(bf16[768,1024]{1,0:T(8,128)(2,1)S(1)} %bitcast.58), channel_id=1, source_target_pairs={{0,1},{1,0},{2,3},{3,2},{4,5},{5,4},{6,7},{7,6},{8,9},{9,8},{10,11... | collective-permute-start | bytes 4718600 | tf_op jit(solution)/shard_map/ppermute | solution.py:64
  69.6 12.6 %copy-start.6 = (bf16[256,1024]{1,0:T(8,128)(2,1)}, bf16[256,1024]{1,0:T(8,128)(2,1)S(1)}, u32[]{:S(2)}) copy-start(bf16[256,1024]{1,0:T(8,128)(2,1)S(1)} %broadcast_select_fusion.1.refs_8_) | copy-start | bytes 1572868
  69.7 16.8 %collective-permute-start.17 = (bf16[256,1024]{1,0:T(8,128)(2,1)S(1)}, bf16[256,1024]{1,0:T(8,128)(2,1)S(1)}, u32[]{:S(2)}, u32[]{:S(2)}) collective-permute-start(bf16[256,1024]{1,0:T(8,128)(2,1)S(1)} %broadcast_select_fusion.10), channel_id=1, source_target_pairs={{4,0},{8,12},{5,1},{9,13},{6,2},{10,14},{7,3},{11,15},{20,16},{24,... | collective-permute-start | bytes 1572872 | tf_op jit(solution)/shard_map/ppermute | solution.py:68
  74.0 14.9 %collective-permute-start.20 = (bf16[256,1024]{1,0:T(8,128)(2,1)S(1)}, bf16[256,1024]{1,0:T(8,128)(2,1)S(1)}, u32[]{:S(2)}, u32[]{:S(2)}) collective-permute-start(bf16[256,1024]{1,0:T(8,128)(2,1)S(1)} %broadcast_select_fusion.1.refs_8_), channel_id=1, source_target_pairs={{0,16},{16,0},{1,17},{17,1},{2,18},{18,2},{3,19},{19,3},{4,20},{20... | collective-permute-start | bytes 1572872 | tf_op jit(solution)/shard_map/ppermute | solution.py:64
  80.8 3.1 %copy-start.20 = (f32[768,256]{1,0:T(8,128)}, f32[768,256]{1,0:T(8,128)S(1)}, u32[]{:S(2)}) copy-start(f32[768,256]{1,0:T(8,128)S(1)} %collective-permute-done.11) | copy-start | bytes 2359300
  80.8 17.4 %collective-permute-start.14 = (f32[768,256]{1,0:T(8,128)S(1)}, f32[768,256]{1,0:T(8,128)S(1)}, u32[]{:S(2)}, u32[]{:S(2)}) collective-permute-start(f32[768,256]{1,0:T(8,128)S(1)} %fusion.4), channel_id=1, source_target_pairs={{0,2},{2,0},{1,3},{3,1},{4,6},{6,4},{5,7},{7,5},{8,10},{10,8},{9,1... | collective-permute-start | bytes 2359304 | tf_op jit(solution)/shard_map/ppermute | solution.py:64
  86.5 12.9 %collective-permute-start.23 = (bf16[256,1024]{1,0:T(8,128)(2,1)S(1)}, bf16[256,1024]{1,0:T(8,128)(2,1)S(1)}, u32[]{:S(2)}, u32[]{:S(2)}) collective-permute-start(bf16[256,1024]{1,0:T(8,128)(2,1)S(1)} %broadcast_select_fusion.9), channel_id=1, source_target_pairs={{4,0},{8,12},{5,1},{9,13},{6,2},{10,14},{7,3},{11,15},{20,16},{24,... | collective-permute-start | bytes 1572872 | tf_op jit(solution)/shard_map/ppermute | solution.py:68
  88.8 5.7 %copy-start.3 = (bf16[256,1024]{1,0:T(8,128)(2,1)}, bf16[256,1024]{1,0:T(8,128)(2,1)S(1)}, u32[]{:S(2)}) copy-start(bf16[256,1024]{1,0:T(8,128)(2,1)S(1)} %get-tuple-element.87.refs_1_) | copy-start | bytes 1572868
  88.8 4.2 %copy-start.15 = (bf16[256,1024]{1,0:T(8,128)(2,1)}, bf16[256,1024]{1,0:T(8,128)(2,1)S(1)}, u32[]{:S(2)}) copy-start(bf16[256,1024]{1,0:T(8,128)(2,1)S(1)} %collective-permute-done.20.refs_9_) | copy-start | bytes 1572868
  88.8 11.8 %collective-permute-start.22 = (bf16[256,1024]{1,0:T(8,128)(2,1)S(1)}, bf16[256,1024]{1,0:T(8,128)(2,1)S(1)}, u32[]{:S(2)}, u32[]{:S(2)}) collective-permute-start(bf16[256,1024]{1,0:T(8,128)(2,1)S(1)} %get-tuple-element.87.refs_1_), channel_id=1, source_target_pairs={{0,16},{16,0},{1,17},{17,1},{2,18},{18,2},{3,19},{19,3},{4,20},{20... | collective-permute-start | bytes 1572872 | tf_op jit(solution)/shard_map/ppermute | solution.py:64
  98.2 4.4 %copy-start.22 = (f32[768,256]{1,0:T(8,128)}, f32[768,256]{1,0:T(8,128)S(1)}, u32[]{:S(2)}) copy-start(f32[768,256]{1,0:T(8,128)S(1)} %collective-permute-done.14) | copy-start | bytes 2359300
  98.2 4.4 %copy-start.8 = (bf16[768,1024]{1,0:T(8,128)(2,1)}, bf16[768,1024]{1,0:T(8,128)(2,1)S(1)}, u32[]{:S(2)}) copy-start(bf16[768,1024]{1,0:T(8,128)(2,1)S(1)} %collective-permute-done.19.refs_3_) | copy-start | bytes 4718596
  98.2 4.4 %copy-start.9 = (bf16[768,1024]{1,0:T(8,128)(2,1)}, bf16[768,1024]{1,0:T(8,128)(2,1)S(1)}, u32[]{:S(2)}) copy-start(bf16[768,1024]{1,0:T(8,128)(2,1)S(1)} %collective-permute-done.18.refs_1_) | copy-start | bytes 4718596
  99.4 16.0 %collective-permute-start.21 = (f32[768,256]{1,0:T(8,128)}, f32[768,256]{1,0:T(8,128)}, u32[]{:S(2)}, u32[]{:S(2)}) collective-permute-start(f32[768,256]{1,0:T(8,128)} %fusion.3), channel_id=1, source_target_pairs={{0,2},{2,0},{1,3},{3,1},{4,6},{6,4},{5,7},{7,5},{8,10},{10,8},{9,1... | collective-permute-start | bytes 2359304 | tf_op jit(solution)/shard_map/ppermute | solution.py:64
  100.6 10.4 %copy-start.5 = (bf16[256,1024]{1,0:T(8,128)(2,1)}, bf16[256,1024]{1,0:T(8,128)(2,1)S(1)}, u32[]{:S(2)}) copy-start(bf16[256,1024]{1,0:T(8,128)(2,1)S(1)} %select_select_fusion.refs_0_.refs_2_.refs_11_) | copy-start | bytes 1572868
  100.6 13.0 %collective-permute-start.24 = (bf16[256,1024]{1,0:T(8,128)(2,1)S(1)}, bf16[256,1024]{1,0:T(8,128)(2,1)S(1)}, u32[]{:S(2)}, u32[]{:S(2)}) collective-permute-start(bf16[256,1024]{1,0:T(8,128)(2,1)S(1)} %select_select_fusion.refs_0_.refs_2_.refs_11_), channel_id=1, source_target_pairs={{0,16},{16,0},{1,17},{17,1},{2,18},{18,2},{3,19},{19,3},{4,20},{20... | collective-permute-start | bytes 1572872 | tf_op jit(solution)/shard_map/ppermute | solution.py:64
  102.6 8.4 %copy-start.13 = (bf16[256,1024]{1,0:T(8,128)(2,1)S(1)}, bf16[256,1024]{1,0:T(8,128)(2,1)}, u32[]{:S(2)}) copy-start(bf16[256,1024]{1,0:T(8,128)(2,1)} %copy-done.12) | copy-start | bytes 1572868
  115.4 9.9 %collective-permute-start.25 = (f32[768,1024]{1,0:T(8,128)}, f32[768,1024]{1,0:T(8,128)}, u32[]{:S(2)}, u32[]{:S(2)}) collective-permute-start(f32[768,1024]{1,0:T(8,128)} %shard_map.50), channel_id=1, source_target_pairs={{0,1},{1,0},{2,3},{3,2},{4,5},{5,4},{6,7},{7,6},{8,9},{9,8},{10,11... | collective-permute-start | bytes 9437192 | tf_op jit(solution)/shard_map/ppermute | solution.py:64
  115.4 20.2 %collective-permute-start.27 = (f32[768,256]{1,0:T(8,128)}, f32[768,256]{1,0:T(8,128)S(1)}, u32[]{:S(2)}, u32[]{:S(2)}) collective-permute-start(f32[768,256]{1,0:T(8,128)} %fusion), channel_id=1, source_target_pairs={{0,2},{2,0},{1,3},{3,1},{4,6},{6,4},{5,7},{7,5},{8,10},{10,8},{9,1... | collective-permute-start | bytes 2359304 | tf_op jit(solution)/shard_map/ppermute | solution.py:64
  116.0 6.2 %copy-start.16 = (f32[768,256]{1,0:T(8,128)S(1)}, f32[768,256]{1,0:T(8,128)}, u32[]{:S(2)}) copy-start(f32[768,256]{1,0:T(8,128)} %fusion.2) | copy-start | bytes 2359300
  116.0 6.2 %copy-start.21 = (f32[768,256]{1,0:T(8,128)S(1)}, f32[768,256]{1,0:T(8,128)}, u32[]{:S(2)}) copy-start(f32[768,256]{1,0:T(8,128)} %copy-done.20) | copy-start | bytes 2359300
  123.4 1.8 %collective-permute-start.26 = (bf16[768,256]{1,0:T(8,128)(2,1)S(1)}, bf16[768,256]{1,0:T(8,128)(2,1)S(1)}, u32[]{:S(2)}, u32[]{:S(2)}) collective-permute-start(bf16[768,256]{1,0:T(8,128)(2,1)S(1)} %get-tuple-element.108), channel_id=1, source_target_pairs={{0,1},{1,0},{2,3},{3,2},{4,5},{5,4},{6,7},{7,6},{8,9},{9,8},{10,11... | collective-permute-start | bytes 1179656 | tf_op jit(solution)/shard_map/ppermute | solution.py:64
  125.3 10.3 %copy-start.24 = (f32[768,256]{1,0:T(8,128)S(1)}, f32[768,256]{1,0:T(8,128)}, u32[]{:S(2)}) copy-start(f32[768,256]{1,0:T(8,128)} %get-tuple-element.104) | copy-start | bytes 2359300
  135.7 1.8 %collective-permute-start.28 = (bf16[768,256]{1,0:T(8,128)(2,1)S(1)}, bf16[768,256]{1,0:T(8,128)(2,1)S(1)}, u32[]{:S(2)}, u32[]{:S(2)}) collective-permute-start(bf16[768,256]{1,0:T(8,128)(2,1)S(1)} %get-tuple-element.106), channel_id=1, source_target_pairs={{0,1},{1,0},{2,3},{3,2},{4,5},{5,4},{6,7},{7,6},{8,9},{9,8},{10,11... | collective-permute-start | bytes 1179656 | tf_op jit(solution)/shard_map/ppermute | solution.py:64
  (6 other events, 8.3 us)

commit v6 on v5

--- a/solution.py
+++ b/solution.py
@@ -116,7 +116,7 @@
 def keep(early, grads, there, pieces):
     tokens, width = grads[0].shape
     quarter = pieces[0][0][0].shape[0]
-    tile = tokens // 2
+    tile = tokens // 3
     by_rows = lambda columns: pl.BlockSpec((tile, columns), lambda i: (i, 0))
     flat = [p for four in pieces for two in four for p in two]
     return pl.pallas_call(
@@ -137,7 +137,7 @@
 
 def forward_sum(numbers, heads, base, pieces, dtype):
     tokens, width = heads[0].shape
-    tile = tokens // 2
+    tile = tokens // 3
     by_rows = pl.BlockSpec((tile, width), lambda i, _: (i, 0))
     spec = pltpu.PrefetchScalarGridSpec(
         num_scalar_prefetch=1,

time: 140 us -> 140 us (level)
  no operation moved by 1% of the time
where the time goes in v6:
time: 140 us; the launch traced here: 139 us
  waiting for transfers between devices  47.8 us (34%)
  starting transfers between devices  31.4 us (22%)
  Pallas kernels  23.9 us (17%)
  matrix products  15.1 us (11%)
  other arithmetic  11.5 us (8%)
  local copies, waits for them, and re-layouts  7.96 us (6%)
    ppermute x10, waiting for transfers between devices, send(): return lax.ppermute(value, 'a', pairs)  31.9 us
    pallas_call x2, Pallas kernels, forward_sum(): pl.pallas_call(functools.partial(sum_of_products, len(base)), grid_spec=s...  17.3 us
    ppermute x10, starting transfers between devices, send(): return lax.ppermute(value, 'a', pairs)  16.9 us
    ppermute x19, waiting for transfers between devices, swap(): return lax.ppermute(value, axis, [(0, 1), (1, 0)])  15.9 us
    dot_general x12, matrix products, times_rows(): lax.dot_general(left, right, (((1,), (1,)), ((), ())), preferred_element_...  15.1 us
    ppermute x19, starting transfers between devices, swap(): return lax.ppermute(value, axis, [(0, 1), (1, 0)])  14.5 us
    select_n x14, other arithmetic, pick(): return jnp.where(flag, yes, no)  11.2 us
    pallas_call x1, Pallas kernels, keep(): pl.pallas_call(kept_sums, grid=(tokens // tile,), in_specs=[pl.BlockSpec(...  6.63 us
  transfers between devices with their start and end apart: 29, of which 15 were waited for; matrix products, arithmetic and copies ran while one was open for 21% of the time, Pallas kernels for 17%

profile of v6, /device:TPU:0, one launch (start us, length us, event | category | flops | bytes accessed | tf_op | source)
XLA Modules:
  0.0 138.7 jit_solution(9914761704563394633)
XLA Ops:
  0.7 2.0 %dynamic-slice_bitcast_fusion.refs_5_ = bf16[256,1024]{1,0:T(8,128)(2,1)} fusion(bf16[1,1024,1024]{2,1,0:T(8,128)(2,1)} %param.5, s32[]{:T(128)S(6)} %select_n.205), kind=kLoop, calls=%fused_computation.34 | loop fusion | bytes 1048580 | tf_op jit(solution)/shard_map/dynamic_slice | solution.py:179
  2.7 1.1 constant_dynamic-slice_fusion.2
  4.3 1.4 %collective-permute-start = (bf16[256,1024]{1,0:T(8,128)(2,1)}, bf16[256,1024]{1,0:T(8,128)(2,1)}, u32[]{:S(2)}, u32[]{:S(2)}) collective-permute-start(bf16[256,1024]{1,0:T(8,128)(2,1)} %dynamic-slice_bitcast_fusion.refs_5_), channel_id=1, source_target_pairs={{4,8},{8,4},{5,9},{9,5},{6,10},{10,6},{7,11},{11,7},{20,24},{24,20... | collective-permute-start | bytes 1572872 | tf_op jit(solution)/shard_map/ppermute | solution.py:68
  5.9 4.5 %collective-permute-start.2 = (bf16[256,1024]{1,0:T(8,128)(2,1)}, bf16[256,1024]{1,0:T(8,128)(2,1)}, u32[]{:S(2)}, u32[]{:S(2)}) collective-permute-start(bf16[256,1024]{1,0:T(8,128)(2,1)} %collective-permute-done.1.refs_4_), channel_id=1, source_target_pairs={{0,4},{12,8},{4,0},{8,12},{1,5},{13,9},{5,1},{9,13},{2,6},{14,10},... | collective-permute-start | bytes 1572872 | tf_op jit(solution)/shard_map/ppermute | solution.py:68
  10.4 1.5 %collective-permute-start.9 = (bf16[768,1024]{1,0:T(8,128)(2,1)}, bf16[768,1024]{1,0:T(8,128)(2,1)}, u32[]{:S(2)}, u32[]{:S(2)}) collective-permute-start(bf16[768,1024]{1,0:T(8,128)(2,1)} %bitcast.55), channel_id=1, source_target_pairs={{0,2},{2,0},{1,3},{3,1},{4,6},{6,4},{5,7},{7,5},{8,10},{10,8},{9,1... | collective-permute-start | bytes 4718600 | tf_op jit(solution)/shard_map/ppermute | solution.py:64
  12.0 11.1 %collective-permute-done.2.refs_6_.refs_3_ = bf16[256,1024]{1,0:T(8,128)(2,1)} collective-permute-done((bf16[256,1024]{1,0:T(8,128)(2,1)}, bf16[256,1024]{1,0:T(8,128)(2,1)}, u32[]{:S(2)}, u32[]{:S(2)}) %collective-permute-start.2) | collective-permute-done | bytes 524320 | tf_op jit(solution)/shard_map/ppermute | solution.py:68
  23.0 1.5 %collective-permute-start.4 = (bf16[256,1024]{1,0:T(8,128)(2,1)}, bf16[256,1024]{1,0:T(8,128)(2,1)}, u32[]{:S(2)}, u32[]{:S(2)}) collective-permute-start(bf16[256,1024]{1,0:T(8,128)(2,1)} %collective-permute-done.1.refs_4_), channel_id=1, source_target_pairs={{4,8},{8,4},{5,9},{9,5},{6,10},{10,6},{7,11},{11,7},{20,24},{24,20... | collective-permute-start | bytes 1572872 | tf_op jit(solution)/shard_map/ppermute | solution.py:68
  24.5 2.0 %broadcast_select_fusion.4 = bf16[256,1024]{1,0:T(8,128)(2,1)} fusion(bf16[256,1024]{1,0:T(8,128)(2,1)} %collective-permute-done, pred[]{:T(512)S(6)} %and.55, bf16[1,1024,1024]{2,1,0:T(8,128)(2,1)} %param.5, s32[]{:T(128)S(6)} %select_n.205), kind=kLoop, calls=%fused_computation.39 | loop fusion | flops 262144 | bytes 1572869 | tf_op jit(solution)/shard_map/jit(_where)/select_n | solution.py:76
  26.5 2.8 %collective-permute-start.3 = (bf16[256,1024]{1,0:T(8,128)(2,1)}, bf16[256,1024]{1,0:T(8,128)(2,1)}, u32[]{:S(2)}, u32[]{:S(2)}) collective-permute-start(bf16[256,1024]{1,0:T(8,128)(2,1)} %broadcast_select_fusion.4), channel_id=1, source_target_pairs={{0,4},{12,8},{4,0},{8,12},{1,5},{13,9},{5,1},{9,13},{2,6},{14,10},... | collective-permute-start | bytes 1572872 | tf_op jit(solution)/shard_map/ppermute | solution.py:68
  29.4 1.5 %collective-permute-start.5 = (bf16[256,1024]{1,0:T(8,128)(2,1)}, bf16[256,1024]{1,0:T(8,128)(2,1)}, u32[]{:S(2)}, u32[]{:S(2)}) collective-permute-start(bf16[256,1024]{1,0:T(8,128)(2,1)} %collective-permute-done.2.refs_6_.refs_3_), channel_id=1, source_target_pairs={{0,16},{16,0},{1,17},{17,1},{2,18},{18,2},{3,19},{19,3},{4,20},{20... | collective-permute-start | bytes 1572872 | tf_op jit(solution)/shard_map/ppermute | solution.py:64
  32.8 1.1 broadcast_select_fusion.12
  33.9 7.0 %collective-permute-done.3 = bf16[256,1024]{1,0:T(8,128)(2,1)} collective-permute-done((bf16[256,1024]{1,0:T(8,128)(2,1)}, bf16[256,1024]{1,0:T(8,128)(2,1)}, u32[]{:S(2)}, u32[]{:S(2)}) %collective-permute-start.3) | collective-permute-done | bytes 524320 | tf_op jit(solution)/shard_map/ppermute | solution.py:68
  40.9 1.5 %collective-permute-done.5.refs_7_ = bf16[256,1024]{1,0:T(8,128)(2,1)} collective-permute-done((bf16[256,1024]{1,0:T(8,128)(2,1)}, bf16[256,1024]{1,0:T(8,128)(2,1)}, u32[]{:S(2)}, u32[]{:S(2)}) %collective-permute-start.5) | collective-permute-done | bytes 524320 | tf_op jit(solution)/shard_map/ppermute | solution.py:64
  42.4 1.3 collective-permute-start.6
  43.7 1.3 constant_dynamic-slice_fusion
  45.0 1.2 broadcast_select_fusion.3.refs_7_
  46.3 1.6 %collective-permute-start.12 = (bf16[256,1024]{1,0:T(8,128)(2,1)S(1)}, bf16[256,1024]{1,0:T(8,128)(2,1)S(1)}, u32[]{:S(2)}, u32[]{:S(2)}) collective-permute-start(bf16[256,1024]{1,0:T(8,128)(2,1)S(1)} %broadcast_select_fusion.3.refs_7_), channel_id=1, source_target_pairs={{0,16},{16,0},{1,17},{17,1},{2,18},{18,2},{3,19},{19,3},{4,20},{20... | collective-permute-start | bytes 1572872 | tf_op jit(solution)/shard_map/ppermute | solution.py:64
  48.0 8.1 %collective-permute-done.6 = bf16[256,1024]{1,0:T(8,128)(2,1)S(1)} collective-permute-done((bf16[256,1024]{1,0:T(8,128)(2,1)S(1)}, bf16[256,1024]{1,0:T(8,128)(2,1)S(1)}, u32[]{:S(2)}, u32[]{:S(2)}) %collective-permute-start.6) | collective-permute-done | bytes 524320 | tf_op jit(solution)/shard_map/ppermute | solution.py:68
  56.8 1.3 collective-permute-start.16
  59.4 1.2 collective-permute-done.12.refs_8_
  60.6 1.5 %collective-permute-start.13 = (bf16[256,1024]{1,0:T(8,128)(2,1)S(1)}, bf16[256,1024]{1,0:T(8,128)(2,1)S(1)}, u32[]{:S(2)}, u32[]{:S(2)}) collective-permute-start(bf16[256,1024]{1,0:T(8,128)(2,1)S(1)} %broadcast_select_fusion.2), channel_id=1, source_target_pairs={{0,16},{16,0},{1,17},{17,1},{2,18},{18,2},{3,19},{19,3},{4,20},{20... | collective-permute-start | bytes 1572872 | tf_op jit(solution)/shard_map/ppermute | solution.py:64
  62.1 2.5 %collective-permute-start.11 = (f32[768,256]{1,0:T(8,128)S(1)}, f32[768,256]{1,0:T(8,128)S(1)}, u32[]{:S(2)}, u32[]{:S(2)}) collective-permute-start(f32[768,256]{1,0:T(8,128)S(1)} %fusion.5), channel_id=1, source_target_pairs={{0,2},{2,0},{1,3},{3,1},{4,6},{6,4},{5,7},{7,5},{8,10},{10,8},{9,1... | collective-permute-start | bytes 2359304 | tf_op jit(solution)/shard_map/ppermute | solution.py:64
  65.1 4.5 %collective-permute-done.16 = bf16[256,1024]{1,0:T(8,128)(2,1)S(1)} collective-permute-done((bf16[256,1024]{1,0:T(8,128)(2,1)S(1)}, bf16[256,1024]{1,0:T(8,128)(2,1)S(1)}, u32[]{:S(2)}, u32[]{:S(2)}) %collective-permute-start.16) | collective-permute-done | bytes 524320 | tf_op jit(solution)/shard_map/ppermute | solution.py:68
  69.7 1.3 collective-permute-start.17
  71.0 3.0 %collective-permute-done.13 = bf16[256,1024]{1,0:T(8,128)(2,1)S(1)} collective-permute-done((bf16[256,1024]{1,0:T(8,128)(2,1)S(1)}, bf16[256,1024]{1,0:T(8,128)(2,1)S(1)}, u32[]{:S(2)}, u32[]{:S(2)}) %collective-permute-start.13) | collective-permute-done | bytes 524320 | tf_op jit(solution)/shard_map/ppermute | solution.py:64
  74.0 1.5 %collective-permute-start.20 = (bf16[256,1024]{1,0:T(8,128)(2,1)S(1)}, bf16[256,1024]{1,0:T(8,128)(2,1)S(1)}, u32[]{:S(2)}, u32[]{:S(2)}) collective-permute-start(bf16[256,1024]{1,0:T(8,128)(2,1)S(1)} %broadcast_select_fusion.1.refs_8_), channel_id=1, source_target_pairs={{0,16},{16,0},{1,17},{17,1},{2,18},{18,2},{3,19},{19,3},{4,20},{20... | collective-permute-start | bytes 1572872 | tf_op jit(solution)/shard_map/ppermute | solution.py:64
  76.1 1.1 broadcast_select_fusion.9
  78.4 2.4 %collective-permute-done.11 = f32[768,256]{1,0:T(8,128)S(1)} collective-permute-done((f32[768,256]{1,0:T(8,128)S(1)}, f32[768,256]{1,0:T(8,128)S(1)}, u32[]{:S(2)}, u32[]{:S(2)}) %collective-permute-start.11) | collective-permute-done | bytes 786464 | tf_op jit(solution)/shard_map/ppermute | solution.py:64
  80.8 1.4 %collective-permute-start.14 = (f32[768,256]{1,0:T(8,128)S(1)}, f32[768,256]{1,0:T(8,128)S(1)}, u32[]{:S(2)}, u32[]{:S(2)}) collective-permute-start(f32[768,256]{1,0:T(8,128)S(1)} %fusion.4), channel_id=1, source_target_pairs={{0,2},{2,0},{1,3},{3,1},{4,6},{6,4},{5,7},{7,5},{8,10},{10,8},{9,1... | collective-permute-start | bytes 2359304 | tf_op jit(solution)/shard_map/ppermute | solution.py:64
  82.2 1.7 %fusion.12 = f32[256,768]{0,1:T(8,128)S(1)} fusion(bf16[768,1024]{1,0:T(8,128)(2,1)S(1)} %collective-permute-done.10.grad_1, bf16[256,1024]{1,0:T(8,128)(2,1)S(1)} %broadcast_select_fusion.1.refs_8_, bf16[256,1024]{1,0:T(8,128)(2,1)} %collective-permute-done.1.refs_4_, pred[]{:T(512)S(6)} %ne.91), kind=kOutput, calls=%fused_computation.22 | convolution fusion | flops 402915328 | bytes 3407873 | tf_op jit(solution)/shard_map/dot_general | solution.py:84
  83.9 2.5 %fusion.2 = f32[768,256]{1,0:T(8,128)} fusion(f32[256,768]{0,1:T(8,128)S(1)} %fusion.12, bf16[256,1024]{1,0:T(8,128)(2,1)S(1)} %broadcast_select_fusion.2, bf16[256,1024]{1,0:T(8,128)(2,1)} %dynamic-slice_bitcast_fusion.refs_5_, pred[]{:T(512)S(6)} %ne.91, bf16[1,768,1024]{2,1,0:T(8,128)(2,1)S(1)} %copy-done), kind=kOutput, calls=%fused_computation.5 | convolution fusion | flops 403111936 | bytes 4194305 | tf_op jit(solution)/shard_map/dot_general | solution.py:84
  86.5 1.5 %collective-permute-start.23 = (bf16[256,1024]{1,0:T(8,128)(2,1)S(1)}, bf16[256,1024]{1,0:T(8,128)(2,1)S(1)}, u32[]{:S(2)}, u32[]{:S(2)}) collective-permute-start(bf16[256,1024]{1,0:T(8,128)(2,1)S(1)} %broadcast_select_fusion.9), channel_id=1, source_target_pairs={{4,0},{8,12},{5,1},{9,13},{6,2},{10,14},{7,3},{11,15},{20,16},{24,... | collective-permute-start | bytes 1572872 | tf_op jit(solution)/shard_map/ppermute | solution.py:68
  90.0 1.5 %fusion.3 = f32[768,256]{1,0:T(8,128)} fusion(f32[256,768]{0,1:T(8,128)S(1)} %fusion.15, bf16[256,1024]{1,0:T(8,128)(2,1)S(1)} %broadcast_select_fusion.3.refs_7_, bf16[256,1024]{1,0:T(8,128)(2,1)S(1)} %get-tuple-element.87.refs_1_, pred[]{:T(512)S(6)} %ne.91, bf16[1,768,1024]{2,1,0:T(8,128)(2,1)S(1)} %copy-done), kind=kOutput, calls=%fused_computation.7 | convolution fusion | flops 403111936 | bytes 4194305 | tf_op jit(solution)/shard_map/dot_general | solution.py:84
  91.5 1.5 %fusion.1 = f32[768,256]{1,0:T(8,128)} fusion(f32[256,768]{0,1:T(8,128)S(1)} %fusion.9, bf16[256,1024]{1,0:T(8,128)(2,1)S(1)} %collective-permute-done.13, bf16[256,1024]{1,0:T(8,128)(2,1)S(1)} %get-tuple-element.113.refs_6_, pred[]{:T(512)S(6)} %ne.91, bf16[1,768,1024]{2,1,0:T(8,128)(2,1)S(1)} %copy-done), kind=kOutput, calls=%fused_computation.3 | convolution fusion | flops 403111936 | bytes 4194305 | tf_op jit(solution)/shard_map/dot_general | solution.py:84
  93.0 1.5 %fusion.6 = f32[256,768]{0,1:T(8,128)} fusion(bf16[768,1024]{1,0:T(8,128)(2,1)S(1)} %collective-permute-done.10.grad_1, bf16[256,1024]{1,0:T(8,128)(2,1)} %collective-permute-done.5.refs_7_, bf16[256,1024]{1,0:T(8,128)(2,1)S(1)} %collective-permute-done.20.refs_9_, pred[]{:T(512)S(6)} %ne.91), kind=kOutput, calls=%fused_computation.16 | convolution fusion | flops 402915328 | bytes 3407873 | tf_op jit(solution)/shard_map/dot_general | solution.py:84
  95.4 2.7 %collective-permute-done.14 = f32[768,256]{1,0:T(8,128)S(1)} collective-permute-done((f32[768,256]{1,0:T(8,128)S(1)}, f32[768,256]{1,0:T(8,128)S(1)}, u32[]{:S(2)}, u32[]{:S(2)}) %collective-permute-start.14) | collective-permute-done | bytes 786464 | tf_op jit(solution)/shard_map/ppermute | solution.py:64
  98.2 1.2 collective-permute-done.23
  99.4 1.2 select_select_fusion.refs_0_.refs_2_.refs_11_
  101.5 1.1 broadcast_select_fusion.5
  102.6 8.5 %shard_map.50 = f32[768,1024]{1,0:T(8,128)} custom-call(s32[17]{0:T(128)} %stack.32.numbers, bf16[768,1024]{1,0:T(8,128)(2,1)} %bitcast.56, bf16[768,1024]{1,0:T(8,128)(2,1)} %copy-done.9, bf16[768,1024]{1,0:T(8,128)(2,1)} %collective-permute-done.9.refs_2_, bf16[768,1024]{1,0:T(8,128)(2,1)} %copy-done.8, bf16[256,1024]{1,0:T(8,128)(2,1)} %collective-permute-done.1.refs_4_, ...), custom_call_target="tpu_custom_call" | custom-call | flops 1000 | bytes 1000 | tf_op jit(solution)/shard_map/pallas_call | solution.py:150
  111.1 2.6 %fusion = f32[768,256]{1,0:T(8,128)} fusion(f32[256,768]{0,1:T(8,128)} %fusion.6, bf16[256,1024]{1,0:T(8,128)(2,1)S(1)} %collective-permute-done.12.refs_8_, bf16[256,1024]{1,0:T(8,128)(2,1)S(1)} %copy-done.13, pred[]{:T(512)S(6)} %ne.91, bf16[1,768,1024]{2,1,0:T(8,128)(2,1)S(1)} %copy-done), kind=kOutput, calls=%fused_computation.1 | convolution fusion | flops 403111936 | bytes 4194305 | tf_op jit(solution)/shard_map/dot_general | solution.py:84
  113.7 1.7 %collective-permute-done.21.there = f32[768,256]{1,0:T(8,128)} collective-permute-done((f32[768,256]{1,0:T(8,128)}, f32[768,256]{1,0:T(8,128)}, u32[]{:S(2)}, u32[]{:S(2)}) %collective-permute-start.21) | collective-permute-done | bytes 786464 | tf_op jit(solution)/shard_map/ppermute | solution.py:64
  116.0 6.6 %shard_map.51 = (bf16[768,256]{1,0:T(8,128)(2,1)}, f32[768,256]{1,0:T(8,128)}) custom-call(s32[1]{0:T(128)} %bitcast.18.flags, bf16[768,1024]{1,0:T(8,128)(2,1)} %bitcast.53, bf16[768,1024]{1,0:T(8,128)(2,1)} %copy-done.1, f32[768,256]{1,0:T(8,128)} %collective-permute-done.21.there, bf16[256,1024]{1,0:T(8,128)(2,1)} %copy-done.5, ...), custom_call_target="tpu_custom_call" | custom-call | flops 1000 | bytes 1000 | tf_op jit(solution)/shard_map/pallas_call | solution.py:122
  122.6 1.3 broadcast_select_fusion.14
  125.8 8.8 %shard_map.52 = bf16[768,1024]{1,0:T(8,128)(2,1)} custom-call(s32[17]{0:T(128)} %stack.29.numbers, bf16[768,1024]{1,0:T(8,128)(2,1)} %bitcast.57, bf16[768,1024]{1,0:T(8,128)(2,1)} %copy-done.9, bf16[768,1024]{1,0:T(8,128)(2,1)} %collective-permute-done.9.refs_2_, bf16[768,1024]{1,0:T(8,128)(2,1)} %copy-done.8, f32[768,1024]{1,0:T(8,128)} %collective-permute-done.25.refs_4_, ...), custom_call_target="tpu_custom_call" | custom-call | flops 1000 | bytes 1000 | tf_op jit(solution)/shard_map/pallas_call | solution.py:150
  134.6 0.9 collective-permute-done.27
  135.9 1.6 %collective-permute-done.28 = bf16[768,256]{1,0:T(8,128)(2,1)S(1)} collective-permute-done((bf16[768,256]{1,0:T(8,128)(2,1)S(1)}, bf16[768,256]{1,0:T(8,128)(2,1)S(1)}, u32[]{:S(2)}, u32[]{:S(2)}) %collective-permute-start.28) | collective-permute-done | bytes 393248 | tf_op jit(solution)/shard_map/ppermute | solution.py:64
  137.6 1.1 copy-done.18
  (100 shorter events, 13.8 us)
Async XLA Ops:
  0.6 9.8 %copy-start = (bf16[1,768,1024]{2,1,0:T(8,128)(2,1)S(1)}, bf16[1,768,1024]{2,1,0:T(8,128)(2,1)}, u32[]{:S(2)}) copy-start(bf16[1,768,1024]{2,1,0:T(8,128)(2,1)} %param.4) | copy-start | bytes 4718596
  3.8 2.2 %collective-permute-start.1 = (bf16[256,1024]{1,0:T(8,128)(2,1)S(1)}, bf16[256,1024]{1,0:T(8,128)(2,1)}, u32[]{:S(2)}, u32[]{:S(2)}) collective-permute-start(bf16[256,1024]{1,0:T(8,128)(2,1)S(1)} %constant_dynamic-slice_fusion.2), channel_id=1, source_target_pairs={{0,1},{1,0},{2,3},{3,2},{4,5},{5,4},{6,7},{7,6},{8,9},{9,8},{10,11... | collective-permute-start | bytes 1572872 | tf_op jit(solution)/shard_map/ppermute | solution.py:64
  4.3 7.7 %collective-permute-start = (bf16[256,1024]{1,0:T(8,128)(2,1)}, bf16[256,1024]{1,0:T(8,128)(2,1)}, u32[]{:S(2)}, u32[]{:S(2)}) collective-permute-start(bf16[256,1024]{1,0:T(8,128)(2,1)} %dynamic-slice_bitcast_fusion.refs_5_), channel_id=1, source_target_pairs={{4,8},{8,4},{5,9},{9,5},{6,10},{10,6},{7,11},{11,7},{20,24},{24,20... | collective-permute-start | bytes 1572872 | tf_op jit(solution)/shard_map/ppermute | solution.py:68
  5.9 17.1 %collective-permute-start.2 = (bf16[256,1024]{1,0:T(8,128)(2,1)}, bf16[256,1024]{1,0:T(8,128)(2,1)}, u32[]{:S(2)}, u32[]{:S(2)}) collective-permute-start(bf16[256,1024]{1,0:T(8,128)(2,1)} %collective-permute-done.1.refs_4_), channel_id=1, source_target_pairs={{0,4},{12,8},{4,0},{8,12},{1,5},{13,9},{5,1},{9,13},{2,6},{14,10},... | collective-permute-start | bytes 1572872 | tf_op jit(solution)/shard_map/ppermute | solution.py:68
  10.4 35.8 %collective-permute-start.10 = (bf16[768,1024]{1,0:T(8,128)(2,1)S(1)}, bf16[768,1024]{1,0:T(8,128)(2,1)S(1)}, u32[]{:S(2)}, u32[]{:S(2)}) collective-permute-start(bf16[768,1024]{1,0:T(8,128)(2,1)S(1)} %bitcast.54), channel_id=1, source_target_pairs={{0,1},{1,0},{2,3},{3,2},{4,5},{5,4},{6,7},{7,6},{8,9},{9,8},{10,11... | collective-permute-start | bytes 4718600 | tf_op jit(solution)/shard_map/ppermute | solution.py:64
  10.4 37.5 %collective-permute-start.9 = (bf16[768,1024]{1,0:T(8,128)(2,1)}, bf16[768,1024]{1,0:T(8,128)(2,1)}, u32[]{:S(2)}, u32[]{:S(2)}) collective-permute-start(bf16[768,1024]{1,0:T(8,128)(2,1)} %bitcast.55), channel_id=1, source_target_pairs={{0,2},{2,0},{1,3},{3,1},{4,6},{6,4},{5,7},{7,5},{8,10},{10,8},{9,1... | collective-permute-start | bytes 4718600 | tf_op jit(solution)/shard_map/ppermute | solution.py:64
  23.0 9.0 %collective-permute-start.4 = (bf16[256,1024]{1,0:T(8,128)(2,1)}, bf16[256,1024]{1,0:T(8,128)(2,1)}, u32[]{:S(2)}, u32[]{:S(2)}) collective-permute-start(bf16[256,1024]{1,0:T(8,128)(2,1)} %collective-permute-done.1.refs_4_), channel_id=1, source_target_pairs={{4,8},{8,4},{5,9},{9,5},{6,10},{10,6},{7,11},{11,7},{20,24},{24,20... | collective-permute-start | bytes 1572872 | tf_op jit(solution)/shard_map/ppermute | solution.py:68
  26.5 14.4 %collective-permute-start.3 = (bf16[256,1024]{1,0:T(8,128)(2,1)}, bf16[256,1024]{1,0:T(8,128)(2,1)}, u32[]{:S(2)}, u32[]{:S(2)}) collective-permute-start(bf16[256,1024]{1,0:T(8,128)(2,1)} %broadcast_select_fusion.4), channel_id=1, source_target_pairs={{0,4},{12,8},{4,0},{8,12},{1,5},{13,9},{5,1},{9,13},{2,6},{14,10},... | collective-permute-start | bytes 1572872 | tf_op jit(solution)/shard_map/ppermute | solution.py:68
  29.4 13.0 %collective-permute-start.5 = (bf16[256,1024]{1,0:T(8,128)(2,1)}, bf16[256,1024]{1,0:T(8,128)(2,1)}, u32[]{:S(2)}, u32[]{:S(2)}) collective-permute-start(bf16[256,1024]{1,0:T(8,128)(2,1)} %collective-permute-done.2.refs_6_.refs_3_), channel_id=1, source_target_pairs={{0,16},{16,0},{1,17},{17,1},{2,18},{18,2},{3,19},{19,3},{4,20},{20... | collective-permute-start | bytes 1572872 | tf_op jit(solution)/shard_map/ppermute | solution.py:64
  32.1 15.8 %collective-permute-start.8 = (bf16[256,1024]{1,0:T(8,128)(2,1)}, bf16[256,1024]{1,0:T(8,128)(2,1)S(1)}, u32[]{:S(2)}, u32[]{:S(2)}) collective-permute-start(bf16[256,1024]{1,0:T(8,128)(2,1)} %collective-permute-done.2.refs_6_.refs_3_), channel_id=1, source_target_pairs={{4,8},{8,4},{5,9},{9,5},{6,10},{10,6},{7,11},{11,7},{20,24},{24,20... | collective-permute-start | bytes 1572872 | tf_op jit(solution)/shard_map/ppermute | solution.py:68
  42.4 13.7 %collective-permute-start.6 = (bf16[256,1024]{1,0:T(8,128)(2,1)S(1)}, bf16[256,1024]{1,0:T(8,128)(2,1)S(1)}, u32[]{:S(2)}, u32[]{:S(2)}) collective-permute-start(bf16[256,1024]{1,0:T(8,128)(2,1)S(1)} %broadcast_select_fusion.12), channel_id=1, source_target_pairs={{4,0},{8,12},{5,1},{9,13},{6,2},{10,14},{7,3},{11,15},{20,16},{24,... | collective-permute-start | bytes 1572872 | tf_op jit(solution)/shard_map/ppermute | solution.py:68
  45.0 46.5 %copy-start.4 = (bf16[256,1024]{1,0:T(8,128)(2,1)}, bf16[256,1024]{1,0:T(8,128)(2,1)S(1)}, u32[]{:S(2)}) copy-start(bf16[256,1024]{1,0:T(8,128)(2,1)S(1)} %get-tuple-element.113.refs_6_) | copy-start | bytes 1572868
  45.0 11.1 %collective-permute-start.7 = (bf16[256,1024]{1,0:T(8,128)(2,1)S(1)}, bf16[256,1024]{1,0:T(8,128)(2,1)S(1)}, u32[]{:S(2)}, u32[]{:S(2)}) collective-permute-start(bf16[256,1024]{1,0:T(8,128)(2,1)S(1)} %get-tuple-element.112), channel_id=1, source_target_pairs={{0,1},{1,0},{2,3},{3,2},{4,5},{5,4},{6,7},{7,6},{8,9},{9,8},{10,11... | collective-permute-start | bytes 1572872 | tf_op jit(solution)/shard_map/ppermute | solution.py:64
  46.3 43.7 %copy-start.2 = (bf16[256,1024]{1,0:T(8,128)(2,1)}, bf16[256,1024]{1,0:T(8,128)(2,1)S(1)}, u32[]{:S(2)}) copy-start(bf16[256,1024]{1,0:T(8,128)(2,1)S(1)} %broadcast_select_fusion.3.refs_7_) | copy-start | bytes 1572868
  46.3 46.7 %copy-start.1 = (bf16[768,1024]{1,0:T(8,128)(2,1)}, bf16[768,1024]{1,0:T(8,128)(2,1)S(1)}, u32[]{:S(2)}) copy-start(bf16[768,1024]{1,0:T(8,128)(2,1)S(1)} %collective-permute-done.10.grad_1) | copy-start | bytes 4718596
  46.3 14.3 %collective-permute-start.12 = (bf16[256,1024]{1,0:T(8,128)(2,1)S(1)}, bf16[256,1024]{1,0:T(8,128)(2,1)S(1)}, u32[]{:S(2)}, u32[]{:S(2)}) collective-permute-start(bf16[256,1024]{1,0:T(8,128)(2,1)S(1)} %broadcast_select_fusion.3.refs_7_), channel_id=1, source_target_pairs={{0,16},{16,0},{1,17},{17,1},{2,18},{18,2},{3,19},{19,3},{4,20},{20... | collective-permute-start | bytes 1572872 | tf_op jit(solution)/shard_map/ppermute | solution.py:64
  56.1 33.3 %copy-start.14 = (bf16[256,1024]{1,0:T(8,128)(2,1)}, bf16[256,1024]{1,0:T(8,128)(2,1)S(1)}, u32[]{:S(2)}) copy-start(bf16[256,1024]{1,0:T(8,128)(2,1)S(1)} %collective-permute-done.7.refs_5_) | copy-start | bytes 1572868
  56.1 8.4 %collective-permute-start.15 = (bf16[256,1024]{1,0:T(8,128)(2,1)}, bf16[256,1024]{1,0:T(8,128)(2,1)S(1)}, u32[]{:S(2)}, u32[]{:S(2)}) collective-permute-start(bf16[256,1024]{1,0:T(8,128)(2,1)} %collective-permute-done.3), channel_id=1, source_target_pairs={{4,8},{8,4},{5,9},{9,5},{6,10},{10,6},{7,11},{11,7},{20,24},{24,20... | collective-permute-start | bytes 1572872 | tf_op jit(solution)/shard_map/ppermute | solution.py:68
  56.8 12.8 %collective-permute-start.16 = (bf16[256,1024]{1,0:T(8,128)(2,1)S(1)}, bf16[256,1024]{1,0:T(8,128)(2,1)S(1)}, u32[]{:S(2)}, u32[]{:S(2)}) collective-permute-start(bf16[256,1024]{1,0:T(8,128)(2,1)S(1)} %broadcast_select_fusion.11), channel_id=1, source_target_pairs={{4,0},{8,12},{5,1},{9,13},{6,2},{10,14},{7,3},{11,15},{20,16},{24,... | collective-permute-start | bytes 1572872 | tf_op jit(solution)/shard_map/ppermute | solution.py:68
  58.8 5.8 %copy-start.7 = (bf16[1,768,1024]{2,1,0:T(8,128)(2,1)S(1)}, bf16[1,768,1024]{2,1,0:T(8,128)(2,1)}, u32[]{:S(2)}) copy-start(bf16[1,768,1024]{2,1,0:T(8,128)(2,1)} %param.3) | copy-start | bytes 4718596
  60.6 50.5 %copy-start.10 = (bf16[256,1024]{1,0:T(8,128)(2,1)}, bf16[256,1024]{1,0:T(8,128)(2,1)S(1)}, u32[]{:S(2)}) copy-start(bf16[256,1024]{1,0:T(8,128)(2,1)S(1)} %collective-permute-done.12.refs_8_) | copy-start | bytes 1572868
  60.6 13.4 %collective-permute-start.13 = (bf16[256,1024]{1,0:T(8,128)(2,1)S(1)}, bf16[256,1024]{1,0:T(8,128)(2,1)S(1)}, u32[]{:S(2)}, u32[]{:S(2)}) collective-permute-start(bf16[256,1024]{1,0:T(8,128)(2,1)S(1)} %broadcast_select_fusion.2), channel_id=1, source_target_pairs={{0,16},{16,0},{1,17},{17,1},{2,18},{18,2},{3,19},{19,3},{4,20},{20... | collective-permute-start | bytes 1572872 | tf_op jit(solution)/shard_map/ppermute | solution.py:64
  62.1 18.7 %collective-permute-start.11 = (f32[768,256]{1,0:T(8,128)S(1)}, f32[768,256]{1,0:T(8,128)S(1)}, u32[]{:S(2)}, u32[]{:S(2)}) collective-permute-start(f32[768,256]{1,0:T(8,128)S(1)} %fusion.5), channel_id=1, source_target_pairs={{0,2},{2,0},{1,3},{3,1},{4,6},{6,4},{5,7},{7,5},{8,10},{10,8},{9,1... | collective-permute-start | bytes 2359304 | tf_op jit(solution)/shard_map/ppermute | solution.py:64
  64.5 33.6 %collective-permute-start.19 = (bf16[768,1024]{1,0:T(8,128)(2,1)}, bf16[768,1024]{1,0:T(8,128)(2,1)S(1)}, u32[]{:S(2)}, u32[]{:S(2)}) collective-permute-start(bf16[768,1024]{1,0:T(8,128)(2,1)} %collective-permute-done.9.refs_2_), channel_id=1, source_target_pairs={{0,1},{1,0},{2,3},{3,2},{4,5},{5,4},{6,7},{7,6},{8,9},{9,8},{10,11... | collective-permute-start | bytes 4718600 | tf_op jit(solution)/shard_map/ppermute | solution.py:64
  64.5 33.6 %collective-permute-start.18 = (bf16[768,1024]{1,0:T(8,128)(2,1)S(1)}, bf16[768,1024]{1,0:T(8,128)(2,1)S(1)}, u32[]{:S(2)}, u32[]{:S(2)}) collective-permute-start(bf16[768,1024]{1,0:T(8,128)(2,1)S(1)} %bitcast.58), channel_id=1, source_target_pairs={{0,1},{1,0},{2,3},{3,2},{4,5},{5,4},{6,7},{7,6},{8,9},{9,8},{10,11... | collective-permute-start | bytes 4718600 | tf_op jit(solution)/shard_map/ppermute | solution.py:64
  69.6 12.6 %copy-start.6 = (bf16[256,1024]{1,0:T(8,128)(2,1)}, bf16[256,1024]{1,0:T(8,128)(2,1)S(1)}, u32[]{:S(2)}) copy-start(bf16[256,1024]{1,0:T(8,128)(2,1)S(1)} %broadcast_select_fusion.1.refs_8_) | copy-start | bytes 1572868
  69.7 16.8 %collective-permute-start.17 = (bf16[256,1024]{1,0:T(8,128)(2,1)S(1)}, bf16[256,1024]{1,0:T(8,128)(2,1)S(1)}, u32[]{:S(2)}, u32[]{:S(2)}) collective-permute-start(bf16[256,1024]{1,0:T(8,128)(2,1)S(1)} %broadcast_select_fusion.10), channel_id=1, source_target_pairs={{4,0},{8,12},{5,1},{9,13},{6,2},{10,14},{7,3},{11,15},{20,16},{24,... | collective-permute-start | bytes 1572872 | tf_op jit(solution)/shard_map/ppermute | solution.py:68
  74.0 14.9 %collective-permute-start.20 = (bf16[256,1024]{1,0:T(8,128)(2,1)S(1)}, bf16[256,1024]{1,0:T(8,128)(2,1)S(1)}, u32[]{:S(2)}, u32[]{:S(2)}) collective-permute-start(bf16[256,1024]{1,0:T(8,128)(2,1)S(1)} %broadcast_select_fusion.1.refs_8_), channel_id=1, source_target_pairs={{0,16},{16,0},{1,17},{17,1},{2,18},{18,2},{3,19},{19,3},{4,20},{20... | collective-permute-start | bytes 1572872 | tf_op jit(solution)/shard_map/ppermute | solution.py:64
  80.8 3.1 %copy-start.20 = (f32[768,256]{1,0:T(8,128)}, f32[768,256]{1,0:T(8,128)S(1)}, u32[]{:S(2)}) copy-start(f32[768,256]{1,0:T(8,128)S(1)} %collective-permute-done.11) | copy-start | bytes 2359300
  80.8 17.4 %collective-permute-start.14 = (f32[768,256]{1,0:T(8,128)S(1)}, f32[768,256]{1,0:T(8,128)S(1)}, u32[]{:S(2)}, u32[]{:S(2)}) collective-permute-start(f32[768,256]{1,0:T(8,128)S(1)} %fusion.4), channel_id=1, source_target_pairs={{0,2},{2,0},{1,3},{3,1},{4,6},{6,4},{5,7},{7,5},{8,10},{10,8},{9,1... | collective-permute-start | bytes 2359304 | tf_op jit(solution)/shard_map/ppermute | solution.py:64
  86.5 12.9 %collective-permute-start.23 = (bf16[256,1024]{1,0:T(8,128)(2,1)S(1)}, bf16[256,1024]{1,0:T(8,128)(2,1)S(1)}, u32[]{:S(2)}, u32[]{:S(2)}) collective-permute-start(bf16[256,1024]{1,0:T(8,128)(2,1)S(1)} %broadcast_select_fusion.9), channel_id=1, source_target_pairs={{4,0},{8,12},{5,1},{9,13},{6,2},{10,14},{7,3},{11,15},{20,16},{24,... | collective-permute-start | bytes 1572872 | tf_op jit(solution)/shard_map/ppermute | solution.py:68
  88.8 5.7 %copy-start.3 = (bf16[256,1024]{1,0:T(8,128)(2,1)}, bf16[256,1024]{1,0:T(8,128)(2,1)S(1)}, u32[]{:S(2)}) copy-start(bf16[256,1024]{1,0:T(8,128)(2,1)S(1)} %get-tuple-element.87.refs_1_) | copy-start | bytes 1572868
  88.8 4.2 %copy-start.15 = (bf16[256,1024]{1,0:T(8,128)(2,1)}, bf16[256,1024]{1,0:T(8,128)(2,1)S(1)}, u32[]{:S(2)}) copy-start(bf16[256,1024]{1,0:T(8,128)(2,1)S(1)} %collective-permute-done.20.refs_9_) | copy-start | bytes 1572868
  88.8 11.8 %collective-permute-start.22 = (bf16[256,1024]{1,0:T(8,128)(2,1)S(1)}, bf16[256,1024]{1,0:T(8,128)(2,1)S(1)}, u32[]{:S(2)}, u32[]{:S(2)}) collective-permute-start(bf16[256,1024]{1,0:T(8,128)(2,1)S(1)} %get-tuple-element.87.refs_1_), channel_id=1, source_target_pairs={{0,16},{16,0},{1,17},{17,1},{2,18},{18,2},{3,19},{19,3},{4,20},{20... | collective-permute-start | bytes 1572872 | tf_op jit(solution)/shard_map/ppermute | solution.py:64
  98.2 4.4 %copy-start.22 = (f32[768,256]{1,0:T(8,128)}, f32[768,256]{1,0:T(8,128)S(1)}, u32[]{:S(2)}) copy-start(f32[768,256]{1,0:T(8,128)S(1)} %collective-permute-done.14) | copy-start | bytes 2359300
  98.2 4.4 %copy-start.8 = (bf16[768,1024]{1,0:T(8,128)(2,1)}, bf16[768,1024]{1,0:T(8,128)(2,1)S(1)}, u32[]{:S(2)}) copy-start(bf16[768,1024]{1,0:T(8,128)(2,1)S(1)} %collective-permute-done.19.refs_3_) | copy-start | bytes 4718596
  98.2 4.4 %copy-start.9 = (bf16[768,1024]{1,0:T(8,128)(2,1)}, bf16[768,1024]{1,0:T(8,128)(2,1)S(1)}, u32[]{:S(2)}) copy-start(bf16[768,1024]{1,0:T(8,128)(2,1)S(1)} %collective-permute-done.18.refs_1_) | copy-start | bytes 4718596
  99.4 16.0 %collective-permute-start.21 = (f32[768,256]{1,0:T(8,128)}, f32[768,256]{1,0:T(8,128)}, u32[]{:S(2)}, u32[]{:S(2)}) collective-permute-start(f32[768,256]{1,0:T(8,128)} %fusion.3), channel_id=1, source_target_pairs={{0,2},{2,0},{1,3},{3,1},{4,6},{6,4},{5,7},{7,5},{8,10},{10,8},{9,1... | collective-permute-start | bytes 2359304 | tf_op jit(solution)/shard_map/ppermute | solution.py:64
  100.6 10.4 %copy-start.5 = (bf16[256,1024]{1,0:T(8,128)(2,1)}, bf16[256,1024]{1,0:T(8,128)(2,1)S(1)}, u32[]{:S(2)}) copy-start(bf16[256,1024]{1,0:T(8,128)(2,1)S(1)} %select_select_fusion.refs_0_.refs_2_.refs_11_) | copy-start | bytes 1572868
  100.6 13.1 %collective-permute-start.24 = (bf16[256,1024]{1,0:T(8,128)(2,1)S(1)}, bf16[256,1024]{1,0:T(8,128)(2,1)S(1)}, u32[]{:S(2)}, u32[]{:S(2)}) collective-permute-start(bf16[256,1024]{1,0:T(8,128)(2,1)S(1)} %select_select_fusion.refs_0_.refs_2_.refs_11_), channel_id=1, source_target_pairs={{0,16},{16,0},{1,17},{17,1},{2,18},{18,2},{3,19},{19,3},{4,20},{20... | collective-permute-start | bytes 1572872 | tf_op jit(solution)/shard_map/ppermute | solution.py:64
  102.6 8.5 %copy-start.13 = (bf16[256,1024]{1,0:T(8,128)(2,1)S(1)}, bf16[256,1024]{1,0:T(8,128)(2,1)}, u32[]{:S(2)}) copy-start(bf16[256,1024]{1,0:T(8,128)(2,1)} %copy-done.12) | copy-start | bytes 1572868
  115.4 10.4 %collective-permute-start.25 = (f32[768,1024]{1,0:T(8,128)}, f32[768,1024]{1,0:T(8,128)}, u32[]{:S(2)}, u32[]{:S(2)}) collective-permute-start(f32[768,1024]{1,0:T(8,128)} %shard_map.50), channel_id=1, source_target_pairs={{0,1},{1,0},{2,3},{3,2},{4,5},{5,4},{6,7},{7,6},{8,9},{9,8},{10,11... | collective-permute-start | bytes 9437192 | tf_op jit(solution)/shard_map/ppermute | solution.py:64
  115.4 20.2 %collective-permute-start.27 = (f32[768,256]{1,0:T(8,128)}, f32[768,256]{1,0:T(8,128)S(1)}, u32[]{:S(2)}, u32[]{:S(2)}) collective-permute-start(f32[768,256]{1,0:T(8,128)} %fusion), channel_id=1, source_target_pairs={{0,2},{2,0},{1,3},{3,1},{4,6},{6,4},{5,7},{7,5},{8,10},{10,8},{9,1... | collective-permute-start | bytes 2359304 | tf_op jit(solution)/shard_map/ppermute | solution.py:64
  116.0 6.7 %copy-start.16 = (f32[768,256]{1,0:T(8,128)S(1)}, f32[768,256]{1,0:T(8,128)}, u32[]{:S(2)}) copy-start(f32[768,256]{1,0:T(8,128)} %fusion.2) | copy-start | bytes 2359300
  116.0 6.7 %copy-start.21 = (f32[768,256]{1,0:T(8,128)S(1)}, f32[768,256]{1,0:T(8,128)}, u32[]{:S(2)}) copy-start(f32[768,256]{1,0:T(8,128)} %copy-done.20) | copy-start | bytes 2359300
  123.9 1.8 %collective-permute-start.26 = (bf16[768,256]{1,0:T(8,128)(2,1)S(1)}, bf16[768,256]{1,0:T(8,128)(2,1)S(1)}, u32[]{:S(2)}, u32[]{:S(2)}) collective-permute-start(bf16[768,256]{1,0:T(8,128)(2,1)S(1)} %get-tuple-element.108), channel_id=1, source_target_pairs={{0,1},{1,0},{2,3},{3,2},{4,5},{5,4},{6,7},{7,6},{8,9},{9,8},{10,11... | collective-permute-start | bytes 1179656 | tf_op jit(solution)/shard_map/ppermute | solution.py:64
  125.8 9.8 %copy-start.24 = (f32[768,256]{1,0:T(8,128)S(1)}, f32[768,256]{1,0:T(8,128)}, u32[]{:S(2)}) copy-start(f32[768,256]{1,0:T(8,128)} %get-tuple-element.104) | copy-start | bytes 2359300
  135.7 1.8 %collective-permute-start.28 = (bf16[768,256]{1,0:T(8,128)(2,1)S(1)}, bf16[768,256]{1,0:T(8,128)(2,1)S(1)}, u32[]{:S(2)}, u32[]{:S(2)}) collective-permute-start(bf16[768,256]{1,0:T(8,128)(2,1)S(1)} %get-tuple-element.106), channel_id=1, source_target_pairs={{0,1},{1,0},{2,3},{3,2},{4,5},{5,4},{6,7},{7,6},{8,9},{9,8},{10,11... | collective-permute-start | bytes 1179656 | tf_op jit(solution)/shard_map/ppermute | solution.py:64
  (6 other events, 8.2 us)
